TPU v7x, 32 devices: a whole 2x2x4 slice. The times are simulated.
32 devices in a mesh: dp: 8 (over y, x, core), tensor: 4 (over z).
Axes of the slice: x: 2, y: 2, z: 4, core: 2. Of those that a mesh axis runs over, the one named last changes fastest.
Arguments:
- tokens: bfloat16 [16384, 768], P(('dp', 'tensor')), may hold values from -6 to 6
- w_query: bfloat16 [768, 768], P(('tensor', 'dp')), may hold values from -0.4375 to 0.4375
- w_key: bfloat16 [768, 768], P(('tensor', 'dp')), may hold values from -0.21875 to 0.21875
- w_value: bfloat16 [768, 768], P(('tensor', 'dp')), may hold values from -0.21875 to 0.21875
- w_out: bfloat16 [768, 768], P(('tensor', 'dp')), may hold values from -1.25 to 1.25
- qkv_bias: bfloat16 [3, 768], P(None, ('tensor', 'dp')), may hold values from -3 to 3
- w_ff_in: bfloat16 [3072, 768], P(('tensor', 'dp')), may hold values from -0.21875 to 0.21875
- w_ff_out: bfloat16 [3072, 768], P(('tensor', 'dp')), may hold values from -0.109375 to 0.109375
- ff_bias: bfloat16 [3072], P(('tensor', 'dp')), may hold values from -3 to 3
- rel_table: bfloat16 [256, 768], P('dp'), may hold values from -6 to 6
- gains: bfloat16 [2, 768], P(None, 'dp'), may hold values from 0.099609375 to 1.8984375
- shifts: bfloat16 [4, 768], P(None, 'dp'), may hold values from -3 to 3
- rel_bucket: int32 [4095], replicated, may hold values from 0 to 255
- lengths: int32 [8], P('dp'), may hold values from 1024 to 2048, as said below
- out_grad: bfloat16 [16384, 768], P(('dp', 'tensor')), may hold values from -6 to 6
Outputs:
- layer_result_rows: bfloat16 [16384, 768], P(('dp', 'tensor'))
- tokens_grad: float32 [16384, 768], P(('dp', 'tensor'))
- w_query_grad: float32 [768, 768], P(('tensor', 'dp'))
- w_key_grad: float32 [768, 768], P(('tensor', 'dp'))
- w_value_grad: float32 [768, 768], P(('tensor', 'dp'))
- w_out_grad: float32 [768, 768], P(('tensor', 'dp'))
- qkv_bias_grad: float32 [3, 768], P(None, ('tensor', 'dp'))
- w_ff_in_grad: float32 [3072, 768], P(('tensor', 'dp'))
- w_ff_out_grad: float32 [3072, 768], P(('tensor', 'dp'))
- ff_bias_grad: float32 [3072], P(('tensor', 'dp'))
- rel_table_grad: float32 [256, 768], P('dp')
- gains_grad: float32 [2, 768], P(None, 'dp')
- shifts_grad: float32 [4, 768], P(None, 'dp')
Inputs may be any that keep to these rules, and one draw needn't show every extreme that they name: lengths[s] is the number of leading tokens of sequence s whose keys count.
All inputs are finite; a program needn't handle non-finite values.
Results may differ from a plain program's by a relative error of at most 0.02.
Values may be sent and summed in bfloat16 or wider, within the bound.
A program may use at most 320 MiB of HBM per device.

v0:
```python
import math

import jax
import jax.numpy as jnp
from jax import lax
from jax.sharding import PartitionSpec as P

DH = 64
NB = 256


norm_eps = 1e-06


def layer_norm(values, gain, shift):
    middle = jnp.mean(values, axis=-1, keepdims=True)
    centered = values - middle
    spread = jnp.mean(centered * centered, axis=-1, keepdims=True)
    return centered * lax.rsqrt(spread + norm_eps) * gain + shift


def exact_gelu(values):
    return jax.nn.gelu(values, approximate=False)


def project(inputs, weights, bias):
    return (
        jnp.einsum("td,fd->tf", inputs, weights, preferred_element_type=jnp.float32) + bias
    ).astype(jnp.bfloat16)


def skew(table, rows, width):
    leading = table.shape[:-2]
    span = table.shape[-1]
    flat = table.reshape(leading + (rows * span,))
    cut = lax.slice_in_dim(flat, rows - 1, rows - 1 + rows * (span - 1), axis=flat.ndim - 1)
    return cut.reshape(leading + (rows, span - 1))[..., :width]


def unskew(grads, rows, width):
    leading = grads.shape[:-2]
    span = rows + width
    edges = [(0, 0)] * (grads.ndim - 1)
    widened = jnp.pad(grads, edges + [(0, span - 1 - grads.shape[-1])])
    flat = widened.reshape(leading + (rows * (span - 1),))
    placed = jnp.pad(flat, [(0, 0)] * len(leading) + [(rows - 1, 1)])
    return placed.reshape(leading + (rows, span))


def add_rows(table, piece, offset):
    current = lax.dynamic_slice_in_dim(table, offset, piece.shape[0], 0)
    return lax.dynamic_update_slice_in_dim(table, current + piece, offset, 0)


def masked_scores(raw, valid):
    factor = 1.0 / math.sqrt(3 * DH)
    return jnp.where(valid[None, None, :], raw * factor, -1000000000.0)


def block_scores(start, query_seq, key_seq, key_table, query_table, block):
    length, heads, width = key_seq.shape
    count = length // block
    query_tile_rows = lax.dynamic_slice_in_dim(query_seq, start, block, 0)
    content = jnp.einsum(
        "rhd,jhd->hrj", query_tile_rows, key_seq, preferred_element_type=jnp.float32
    )
    key_neighborhood = lax.dynamic_slice_in_dim(
        key_table, length - block - start, length + block, 0
    )
    to_keys = jnp.einsum(
        "bxi,jxi->xbj", query_tile_rows, key_neighborhood, preferred_element_type=jnp.float32
    )
    query_window = lax.dynamic_slice_in_dim(query_table, start, length + block, 0).reshape(
        count + 1, block, heads, width
    )
    windows = jnp.concatenate([query_window[:-1], query_window[1:]], axis=1)[::-1]
    key_blocks = key_seq.reshape(count, block, heads, width)
    from_keys = jnp.einsum(
        "kthd,kwhd->hktw", key_blocks, windows, preferred_element_type=jnp.float32
    )
    across = skew(from_keys, block, block).transpose(0, 3, 1, 2).reshape(heads, block, length)
    raw = content + skew(to_keys, block, length) + across
    return (raw, query_tile_rows, key_neighborhood, windows, key_blocks)


def sequence_forward(query_seq, key_seq, value_seq, valid, key_table, query_table, block):
    length = key_seq.shape[0]
    starts = jnp.arange(length // block, dtype=jnp.int32) * block

    def step(carry, start):
        found = block_scores(start, query_seq, key_seq, key_table, query_table, block)
        scores = masked_scores(found[0], valid)
        peak = jnp.max(scores, axis=-1, keepdims=True)
        powers = jnp.exp(scores - peak)
        total = jnp.sum(powers, axis=-1, keepdims=True)
        weights = (powers / total).astype(jnp.bfloat16)
        context = jnp.einsum("hrj,jhd->rhd", weights, value_seq, preferred_element_type=jnp.float32)
        return (carry, (context.astype(jnp.bfloat16), peak + jnp.log(total)))

    carry, outputs = lax.scan(step, jnp.zeros((), jnp.int32), starts)
    return (outputs[0].reshape(query_seq.shape), outputs[1])


def sequence_backward(
    query_seq, key_seq, value_seq, valid, d_seq, levels, key_table, query_table, tables, block
):
    length, heads, width = key_seq.shape
    count = length // block
    factor = 1.0 / math.sqrt(3 * DH)
    starts = jnp.arange(count, dtype=jnp.int32) * block

    def step(carry, items):
        d_key, d_value, d_key_table, d_query_table = carry
        start, level = items
        raw, query_tile_rows, key_neighborhood, windows, key_blocks = block_scores(
            start, query_seq, key_seq, key_table, query_table, block
        )
        shares = jnp.exp(masked_scores(raw, valid) - level)
        weights = shares.astype(jnp.bfloat16)
        d_block = lax.dynamic_slice_in_dim(d_seq, start, block, 0)
        d_shares = jnp.einsum(
            "rhd,jhd->hrj", d_block, value_seq, preferred_element_type=jnp.float32
        )
        d_value = d_value + jnp.einsum(
            "hrj,rhd->jhd", weights, d_block, preferred_element_type=jnp.float32
        )
        inner = jnp.sum(shares * d_shares, axis=-1, keepdims=True)
        d_raw = (shares * (d_shares - inner) * factor).astype(jnp.bfloat16)
        nearby_gradient = unskew(d_raw, block, length)
        d_query = jnp.einsum("hrj,jhd->rhd", d_raw, key_seq, preferred_element_type=jnp.float32)
        d_query = d_query + jnp.einsum(
            "kgq,qki->gki", nearby_gradient, key_neighborhood, preferred_element_type=jnp.float32
        )
        d_key = d_key + jnp.einsum(
            "hrj,rhd->jhd", d_raw, query_tile_rows, preferred_element_type=jnp.float32
        )
        d_window = jnp.einsum(
            "oli,loj->ioj", nearby_gradient, query_tile_rows, preferred_element_type=jnp.float32
        )
        d_key_table = add_rows(d_key_table, d_window, length - block - start)
        d_across = unskew(
            d_raw.reshape(heads, block, count, block).transpose(0, 2, 3, 1), block, block
        )
        d_key = d_key + jnp.einsum(
            "hktw,kwhd->kthd", d_across, windows, preferred_element_type=jnp.float32
        ).reshape(length, heads, width)
        d_windows = jnp.einsum(
            "hktw,kthd->kwhd", d_across, key_blocks, preferred_element_type=jnp.float32
        )[::-1]
        edge = ((0, 0), (0, 0), (0, 0))
        folded = jnp.pad(d_windows[:, :block], ((0, 1),) + edge) + jnp.pad(
            d_windows[:, block:], ((1, 0),) + edge
        )
        d_query_table = add_rows(d_query_table, folded.reshape(length + block, heads, width), start)
        return ((d_key, d_value, d_key_table, d_query_table), d_query)

    empty = jnp.zeros((length, heads, width), jnp.float32)
    carry, d_query = lax.scan(step, (empty, empty, tables[0], tables[1]), (starts, levels))
    rounded = (
        d_query.reshape(length, heads, width).astype(jnp.bfloat16),
        carry[0].astype(jnp.bfloat16),
        carry[1].astype(jnp.bfloat16),
    )
    return ((carry[2], carry[3]), rounded)


def local(
    tokens,
    w_query,
    w_key,
    w_value,
    w_out,
    qkv_bias,
    w_ff_in,
    w_ff_out,
    ff_bias,
    rel_table,
    gains,
    shifts,
    rel_bucket,
    lengths,
    out_grad,
):
    query_rows, key_rows, value_rows, out_rows, table, bias_rows = (
        lax.all_gather(w_query, "dp", axis=0, tiled=True),
        lax.all_gather(w_key, "dp", axis=0, tiled=True),
        lax.all_gather(w_value, "dp", axis=0, tiled=True),
        lax.all_gather(w_out, "dp", axis=0, tiled=True),
        lax.all_gather(rel_table, "dp", axis=0, tiled=True),
        lax.all_gather(qkv_bias, "dp", axis=1, tiled=True),
    )
    inner_rows, outer_rows, inner_bias, gain_all, shift_all = (
        lax.all_gather(w_ff_in, "dp", axis=0, tiled=True),
        lax.all_gather(w_ff_out, "dp", axis=0, tiled=True),
        lax.all_gather(ff_bias, "dp", axis=0, tiled=True),
        lax.all_gather(gains, "dp", axis=1, tiled=True),
        lax.all_gather(shifts, "dp", axis=1, tiled=True),
    )
    rows = tokens.shape[0]
    group = rows * lax.axis_size("tensor")
    length = (rel_bucket.shape[0] + 1) // 2
    per_group = group // length
    block = min(512, length)
    heads = query_rows.shape[0] // DH
    features = heads * DH
    gain_float = gain_all.astype(jnp.float32)
    shift_float = shift_all.astype(jnp.float32)
    bias_float = bias_rows.astype(jnp.float32)
    gathered = lax.all_gather(tokens, "tensor", axis=0, tiled=True)
    query = project(gathered, query_rows, bias_float[0])
    key = project(gathered, key_rows, bias_float[1])
    value = project(gathered, value_rows, bias_float[2])
    key_rel = project(table, key_rows, bias_float[1])
    query_rel = project(table, query_rows, bias_float[0])
    picker = (rel_bucket[::-1][:, None] == jnp.arange(NB, dtype=jnp.int32)[None, :]).astype(
        jnp.bfloat16
    )
    key_table = jnp.pad(
        jnp.dot(picker, key_rel, preferred_element_type=jnp.float32).astype(jnp.bfloat16),
        ((0, 1), (0, 0)),
    ).reshape(2 * length, heads, DH)
    query_table = jnp.pad(
        jnp.dot(picker, query_rel, preferred_element_type=jnp.float32).astype(jnp.bfloat16),
        ((0, 1), (0, 0)),
    ).reshape(2 * length, heads, DH)
    valid = jnp.arange(length, dtype=jnp.int32)[None, :] < lengths[:, None]
    shape_four = (per_group, length, heads, DH)
    query_four = query.reshape(shape_four)
    key_four = key.reshape(shape_four)
    value_four = value.reshape(shape_four)

    def forward_one(carry, items):
        return (
            carry,
            sequence_forward(items[0], items[1], items[2], items[3], key_table, query_table, block),
        )

    carry, found = lax.scan(
        forward_one, jnp.zeros((), jnp.int32), (query_four, key_four, value_four, valid)
    )
    context = found[0].reshape(group, features)
    levels = found[1]
    attended = lax.psum_scatter(
        jnp.dot(context, out_rows, preferred_element_type=jnp.float32).astype(jnp.bfloat16),
        "tensor",
        scatter_dimension=0,
        tiled=True,
    ).astype(jnp.float32)
    resid_one = tokens.astype(jnp.float32) + attended + shift_float[0]
    hidden_one, norm_one_back = jax.vjp(layer_norm, resid_one, gain_float[0], shift_float[1])
    hidden_low = hidden_one.astype(jnp.bfloat16)
    feed_inputs = lax.all_gather(hidden_low, "tensor", axis=0, tiled=True)
    pre = jnp.einsum(
        "td,fd->tf", feed_inputs, inner_rows, preferred_element_type=jnp.float32
    ) + inner_bias.astype(jnp.float32)
    activated, gelu_back = jax.vjp(exact_gelu, pre)
    gated = activated.astype(jnp.bfloat16)
    feed_out = lax.psum_scatter(
        jnp.dot(gated, outer_rows, preferred_element_type=jnp.float32).astype(jnp.bfloat16),
        "tensor",
        scatter_dimension=0,
        tiled=True,
    ).astype(jnp.float32)
    resid_two = hidden_one + feed_out + shift_float[2]
    final_value, norm_two_back = jax.vjp(layer_norm, resid_two, gain_float[1], shift_float[3])
    layer_result_rows = final_value.astype(jnp.bfloat16)
    grad_top = out_grad.astype(jnp.float32)
    d_resid_two, d_gain_two, d_shift_three = norm_two_back(grad_top)
    d_shift_two = jnp.sum(d_resid_two, axis=0)
    d_feed = d_resid_two.astype(jnp.bfloat16)
    d_feed_all = lax.all_gather(d_feed, "tensor", axis=0, tiled=True)
    d_gated = jnp.einsum("td,fd->tf", d_feed_all, outer_rows, preferred_element_type=jnp.float32)
    grad_outer = jnp.einsum("tf,td->fd", gated, d_feed_all, preferred_element_type=jnp.float32)
    d_pre = gelu_back(d_gated)[0].astype(jnp.bfloat16)
    grad_inner = jnp.einsum("tf,td->fd", d_pre, feed_inputs, preferred_element_type=jnp.float32)
    grad_bias_inner = jnp.sum(d_pre.astype(jnp.float32), axis=0)
    d_hidden_feed = lax.psum_scatter(
        jnp.dot(d_pre, inner_rows, preferred_element_type=jnp.float32).astype(jnp.bfloat16),
        "tensor",
        scatter_dimension=0,
        tiled=True,
    ).astype(jnp.float32)
    d_hidden_one = d_resid_two + d_hidden_feed
    d_resid_one, d_gain_one, d_shift_one = norm_one_back(d_hidden_one)
    d_shift_zero = jnp.sum(d_resid_one, axis=0)
    d_attended = lax.all_gather(d_resid_one.astype(jnp.bfloat16), "tensor", axis=0, tiled=True)
    grad_out = jnp.einsum("tf,td->fd", context, d_attended, preferred_element_type=jnp.float32)
    d_context = jnp.einsum(
        "td,fd->tf", d_attended, out_rows, preferred_element_type=jnp.float32
    ).astype(jnp.bfloat16)
    table_zero = jnp.zeros((2 * length, heads, DH), jnp.float32)

    def backward_one(carry, items):
        return sequence_backward(
            items[0],
            items[1],
            items[2],
            items[3],
            items[4],
            items[5],
            key_table,
            query_table,
            carry,
            block,
        )

    tables_grad, rounded = lax.scan(
        backward_one,
        (table_zero, table_zero),
        (query_four, key_four, value_four, valid, d_context.reshape(shape_four), levels),
    )
    d_query = rounded[0].reshape(group, features)
    d_key = rounded[1].reshape(group, features)
    d_value = rounded[2].reshape(group, features)
    picker_float = picker.astype(jnp.float32)
    d_key_rel = jnp.einsum(
        "cb,cf->bf",
        picker_float,
        tables_grad[0][:-1].reshape(2 * length - 1, features),
        precision=lax.Precision.HIGHEST,
        preferred_element_type=jnp.float32,
    )
    d_query_rel = jnp.einsum(
        "cb,cf->bf",
        picker_float,
        tables_grad[1][:-1].reshape(2 * length - 1, features),
        precision=lax.Precision.HIGHEST,
        preferred_element_type=jnp.float32,
    )
    table_float = table.astype(jnp.float32)
    grad_query = jnp.einsum(
        "tf,td->fd", d_query, gathered, preferred_element_type=jnp.float32
    ) + jnp.einsum(
        "bf,bd->fd",
        d_query_rel,
        table_float,
        precision=lax.Precision.HIGHEST,
        preferred_element_type=jnp.float32,
    )
    grad_key = jnp.einsum(
        "tf,td->fd", d_key, gathered, preferred_element_type=jnp.float32
    ) + jnp.einsum(
        "bf,bd->fd",
        d_key_rel,
        table_float,
        precision=lax.Precision.HIGHEST,
        preferred_element_type=jnp.float32,
    )
    grad_value = jnp.einsum("tf,td->fd", d_value, gathered, preferred_element_type=jnp.float32)
    bias_gradient = jnp.stack(
        [
            jnp.sum(d_query.astype(jnp.float32), axis=0) + jnp.sum(d_query_rel, axis=0),
            jnp.sum(d_key.astype(jnp.float32), axis=0) + jnp.sum(d_key_rel, axis=0),
            jnp.sum(d_value.astype(jnp.float32), axis=0),
        ]
    )
    d_rel = jnp.einsum(
        "bf,fd->bd",
        d_query_rel,
        query_rows.astype(jnp.float32),
        precision=lax.Precision.HIGHEST,
        preferred_element_type=jnp.float32,
    )
    d_rel = d_rel + jnp.einsum(
        "bf,fd->bd",
        d_key_rel,
        key_rows.astype(jnp.float32),
        precision=lax.Precision.HIGHEST,
        preferred_element_type=jnp.float32,
    )
    total = jnp.dot(d_query, query_rows, preferred_element_type=jnp.float32)
    total = total + jnp.dot(d_key, key_rows, preferred_element_type=jnp.float32)
    tokens_grad = d_resid_one + lax.psum_scatter(
        (total + jnp.dot(d_value, value_rows, preferred_element_type=jnp.float32)).astype(
            jnp.bfloat16
        ),
        "tensor",
        scatter_dimension=0,
        tiled=True,
    ).astype(jnp.float32)
    gain_grads = jnp.stack([d_gain_one, d_gain_two])
    shift_grads = jnp.stack([d_shift_zero, d_shift_one, d_shift_two, d_shift_three])
    summed = (
        lax.psum_scatter(grad_query, "dp", scatter_dimension=0, tiled=True),
        lax.psum_scatter(grad_key, "dp", scatter_dimension=0, tiled=True),
        lax.psum_scatter(grad_value, "dp", scatter_dimension=0, tiled=True),
        lax.psum_scatter(grad_out, "dp", scatter_dimension=0, tiled=True),
        lax.psum_scatter(bias_gradient, "dp", scatter_dimension=1, tiled=True),
        lax.psum_scatter(grad_inner, "dp", scatter_dimension=0, tiled=True),
        lax.psum_scatter(grad_outer, "dp", scatter_dimension=0, tiled=True),
        lax.psum_scatter(grad_bias_inner, "dp", scatter_dimension=0, tiled=True),
        lax.psum_scatter(d_rel, "dp", scatter_dimension=0, tiled=True),
        lax.psum_scatter(gain_grads, "dp", scatter_dimension=1, tiled=True),
        lax.psum_scatter(shift_grads, "dp", scatter_dimension=1, tiled=True),
    )
    rel_piece, gain_piece, shift_piece = lax.psum((summed[8], summed[9], summed[10]), "tensor")
    return (
        layer_result_rows,
        tokens_grad,
        summed[0],
        summed[1],
        summed[2],
        summed[3],
        summed[4],
        summed[5],
        summed[6],
        summed[7],
        rel_piece,
        gain_piece,
        shift_piece,
    )


def solution(mesh):
    return jax.shard_map(
        local,
        mesh=mesh,
        in_specs=(
            P(("dp", "tensor"), None),
            P(("tensor", "dp"), None),
            P(("tensor", "dp"), None),
            P(("tensor", "dp"), None),
            P(("tensor", "dp"), None),
            P(None, ("tensor", "dp")),
            P(("tensor", "dp"), None),
            P(("tensor", "dp"), None),
            P(("tensor", "dp")),
            P("dp", None),
            P(None, "dp"),
            P(None, "dp"),
            P(),
            P("dp"),
            P(("dp", "tensor"), None),
        ),
        out_specs=(
            P(("dp", "tensor"), None),
            P(("dp", "tensor"), None),
            P(("tensor", "dp"), None),
            P(("tensor", "dp"), None),
            P(("tensor", "dp"), None),
            P(("tensor", "dp"), None),
            P(None, ("tensor", "dp")),
            P(("tensor", "dp"), None),
            P(("tensor", "dp"), None),
            P(("tensor", "dp")),
            P("dp", None),
            P(None, "dp"),
            P(None, "dp"),
        ),
        check_vma=False,
    )
```

profile of v0, /device:TPU:13, one launch (start us, length us, event | category | flops | bytes accessed | tf_op | source)
XLA Modules:
  0.0 4376.2 jit_solution(3649324976767461940)
XLA Ops:
  86.8 1309.9 %while.60 = (s32[]{:T(128)}, bf16[4,512,3,64]{1,3,2,0:T(8,128)(2,1)}, f32[4,3,512,1]{2,1,3,0:T(4,128)}, s32[4]{0:T(128)}, bf16[2048,3,64]{0,2,1:T(8,128)(2,1)}, ...) while((s32[]{:T(128)}, ...), condition=%wide.region_3.4_spmd.clone, body=%wide.region_0.3_spmd.clone.sunk | while | flops 2148631040 | bytes 508742912 | solution.py:100
  114.9 25.0 copy.194
  139.9 37.0 reshape.419
  176.9 25.4 slice.228
  202.3 47.5 %reshape.420 = f32[3,4,512,1023]{3,2,1,0:T(8,128)} reshape(f32[3,4,523776]{2,1,0:T(4,128)} %slice.228) | data formatting | bytes 50282496 | tf_op jit(solution)/shard_map/while/body/eval_jaxpr/while/body/eval_jaxpr/reshape | solution.py:37
  279.2 33.0 copy.196
  325.9 44.5 %reshape.421 = f32[3930624]{0:T(1024)} reshape(f32[3,1310208]{1,0:T(4,128)} %slice.230) | data formatting | bytes 31444992 | tf_op jit(solution)/shard_map/while/body/eval_jaxpr/while
  440.5 25.0 copy.194
  465.5 37.0 reshape.419
  502.5 25.4 slice.228
  527.9 47.4 %reshape.420 = f32[3,4,512,1023]{3,2,1,0:T(8,128)} reshape(f32[3,4,523776]{2,1,0:T(4,128)} %slice.228) | data formatting | bytes 50282496 | tf_op jit(solution)/shard_map/while/body/eval_jaxpr/while/body/eval_jaxpr/reshape | solution.py:37
  604.7 33.0 copy.196
  651.4 44.5 %reshape.421 = f32[3930624]{0:T(1024)} reshape(f32[3,1310208]{1,0:T(4,128)} %slice.230) | data formatting | bytes 31444992 | tf_op jit(solution)/shard_map/while/body/eval_jaxpr/while
  766.0 25.0 copy.194
  791.1 37.0 reshape.419
  828.0 25.4 slice.228
  853.5 47.4 %reshape.420 = f32[3,4,512,1023]{3,2,1,0:T(8,128)} reshape(f32[3,4,523776]{2,1,0:T(4,128)} %slice.228) | data formatting | bytes 50282496 | tf_op jit(solution)/shard_map/while/body/eval_jaxpr/while/body/eval_jaxpr/reshape | solution.py:37
  930.3 33.0 copy.196
  977.0 44.5 %reshape.421 = f32[3930624]{0:T(1024)} reshape(f32[3,1310208]{1,0:T(4,128)} %slice.230) | data formatting | bytes 31444992 | tf_op jit(solution)/shard_map/while/body/eval_jaxpr/while
  1091.6 25.0 copy.194
  1116.6 37.0 reshape.419
  1153.6 25.4 slice.228
  1179.0 47.4 %reshape.420 = f32[3,4,512,1023]{3,2,1,0:T(8,128)} reshape(f32[3,4,523776]{2,1,0:T(4,128)} %slice.228) | data formatting | bytes 50282496 | tf_op jit(solution)/shard_map/while/body/eval_jaxpr/while/body/eval_jaxpr/reshape | solution.py:37
  1255.8 33.0 copy.196
  1302.5 44.5 %reshape.421 = f32[3930624]{0:T(1024)} reshape(f32[3,1310208]{1,0:T(4,128)} %slice.230) | data formatting | bytes 31444992 | tf_op jit(solution)/shard_map/while/body/eval_jaxpr/while
  1419.8 42.9 reduce-scatter.19.cloned.1.call-done
  1481.1 47.5 %all-gather.12.cloned.1.call-done = bf16[2048,768]{1,0:T(8,128)(2,1)} async-done(((bf16[512,768]{1,0:T(8,128)(2,1)}), bf16[2048,768]{1,0:T(8,128)(2,1)}) %all-gather.12.cloned.1.call-update) | async-done | bytes 3145744 | tf_op jit(solution)/shard_map/all_gather | solution.py:252
  1562.7 58.9 %reduce-scatter.21.cloned.1.call-done = bf16[512,768]{1,0:T(8,128)(2,1)} async-done(((bf16[2048,768]{1,0:T(8,128)(2,1)}), bf16[512,768]{1,0:T(8,128)(2,1)}) %reduce-scatter.21.cloned.1.call-update) | async-done | bytes 786448 | tf_op jit(solution)/shard_map/reduce_scatter | solution.py:258
  1629.7 61.8 %all-gather.18.cloned.1.call-done = bf16[2048,768]{1,0:T(8,128)(2,1)} async-done(((bf16[512,768]{1,0:T(8,128)(2,1)}), bf16[2048,768]{1,0:T(8,128)(2,1)}) %all-gather.18.cloned.1.call-update) | async-done | bytes 3145744 | tf_op jit(solution)/shard_map/all_gather | solution.py:271
  1708.5 60.7 %reduce-scatter.23.cloned.1.call-done = bf16[512,768]{1,0:T(8,128)(2,1)} async-done(((bf16[2048,768]{1,0:T(8,128)(2,1)}), bf16[512,768]{1,0:T(8,128)(2,1)}) %reduce-scatter.23.cloned.1.call-update) | async-done | bytes 786448 | tf_op jit(solution)/shard_map/reduce_scatter | solution.py:277
  1777.6 59.6 %all-gather.20.cloned.1.call-done = bf16[2048,768]{1,0:T(8,128)(2,1)} async-done(((bf16[512,768]{1,0:T(8,128)(2,1)}), bf16[2048,768]{1,0:T(8,128)(2,1)}) %all-gather.20.cloned.1.call-update) | async-done | bytes 3145744 | tf_op jit(solution)/shard_map/all_gather | solution.py:286
  1845.1 2161.7 %while.61 = (s32[]{:T(128)}, f32[2048,3,64]{0,2,1:T(8,128)}, f32[2048,3,64]{0,2,1:T(8,128)}, f32[4096,3,64]{0,2,1:T(8,128)}, f32[4096,3,64]{0,2,1:T(8,128)}, /*i...) while((s32[]{:T(128)}, f32[2048,3,64]{0,2,1:T(8,128)}, ...), condition=%wide.region_17.18_spmd.clone, body=%wide.region_15.17_spmd.clone.sunk | while | flops 5980427776 | bytes 909853504 | solution.py:158
  1873.3 25.0 copy.206
  1898.3 37.0 reshape.423
  1935.2 25.4 slice.234
  1960.7 47.4 %reshape.424 = f32[3,4,512,1023]{3,2,1,0:T(8,128)} reshape(f32[3,4,523776]{2,1,0:T(4,128)} %slice.234) | data formatting | bytes 50282496 | tf_op jit(solution)/shard_map/while/body/eval_jaxpr/while/body/eval_jaxpr/reshape | solution.py:37
  2037.5 33.0 copy.208
  2084.2 44.7 %reshape.425 = f32[3930624]{0:T(1024)} reshape(f32[3,1310208]{1,0:T(4,128)} %slice.236) | data formatting | bytes 31444992 | tf_op jit(solution)/shard_map/while/body/eval_jaxpr/while
  2269.4 26.7 reshape.427
  2436.2 37.0 reshape.423
  2473.2 25.4 slice.234
  2498.6 47.2 %reshape.424 = f32[3,4,512,1023]{3,2,1,0:T(8,128)} reshape(f32[3,4,523776]{2,1,0:T(4,128)} %slice.234) | data formatting | bytes 50282496 | tf_op jit(solution)/shard_map/while/body/eval_jaxpr/while/body/eval_jaxpr/reshape | solution.py:37
  2575.2 33.0 copy.208
  2622.1 44.5 %reshape.425 = f32[3930624]{0:T(1024)} reshape(f32[3,1310208]{1,0:T(4,128)} %slice.236) | data formatting | bytes 31444992 | tf_op jit(solution)/shard_map/while/body/eval_jaxpr/while
  2807.1 26.8 reshape.427
  2975.1 37.0 reshape.423
  3012.0 25.4 slice.234
  3037.5 47.4 %reshape.424 = f32[3,4,512,1023]{3,2,1,0:T(8,128)} reshape(f32[3,4,523776]{2,1,0:T(4,128)} %slice.234) | data formatting | bytes 50282496 | tf_op jit(solution)/shard_map/while/body/eval_jaxpr/while/body/eval_jaxpr/reshape | solution.py:37
  3114.3 33.0 copy.208
  3161.0 44.7 %reshape.425 = f32[3930624]{0:T(1024)} reshape(f32[3,1310208]{1,0:T(4,128)} %slice.236) | data formatting | bytes 31444992 | tf_op jit(solution)/shard_map/while/body/eval_jaxpr/while
  3346.3 26.7 reshape.427
  3514.2 37.0 reshape.423
  3551.2 25.4 slice.234
  3576.6 47.2 %reshape.424 = f32[3,4,512,1023]{3,2,1,0:T(8,128)} reshape(f32[3,4,523776]{2,1,0:T(4,128)} %slice.234) | data formatting | bytes 50282496 | tf_op jit(solution)/shard_map/while/body/eval_jaxpr/while/body/eval_jaxpr/reshape | solution.py:37
  3653.2 33.0 copy.208
  3700.1 44.5 %reshape.425 = f32[3930624]{0:T(1024)} reshape(f32[3,1310208]{1,0:T(4,128)} %slice.236) | data formatting | bytes 31444992 | tf_op jit(solution)/shard_map/while/body/eval_jaxpr/while
  3885.1 26.8 reshape.427
  4087.4 34.0 reduce-scatter.25.cloned.1.call-done
  4124.4 43.8 %reduce-scatter.37.cloned.1.call-done = f32[96,768]{1,0:T(8,128)} async-done(((f32[768,768]{1,0:T(8,128)}), f32[96,768]{1,0:T(8,128)}) %reduce-scatter.37.cloned.1.call-update) | async-done | bytes 294928 | tf_op jit(solution)/shard_map/reduce_scatter | solution.py:390
  4168.3 46.5 %reduce-scatter.35.cloned.1.call-done = f32[96,768]{1,0:T(8,128)} async-done(((f32[768,768]{1,0:T(8,128)}), f32[96,768]{1,0:T(8,128)}) %reduce-scatter.35.cloned.1.call-update) | async-done | bytes 294928 | tf_op jit(solution)/shard_map/reduce_scatter | solution.py:389
  4214.8 37.9 reduce-scatter.29.cloned.1.call-done
  4252.7 38.0 reduce-scatter.27.cloned.1.call-done
  4290.6 38.1 reduce-scatter.33.cloned.1.call-done
  4328.7 38.1 reduce-scatter.31.cloned.1.call-done
  (569 shorter events, 1958.9 us)
Async XLA Ops:
  8.0 71.4 %all-gather.10.cloned.1.call-start = ((), (), s32[]{:S(2)}) async-start(), calls=%async_computation.13 | async-start | bytes 3932160 | tf_op jit(solution)/shard_map/all_gather | solution.py:209
  8.7 1453.9 %reduce-scatter.19.cloned.1.call-start = ((), (), s32[]{:S(2)}) async-start(), calls=%async_computation.14 | async-start | bytes 3932160 | tf_op jit(solution)/shard_map/reduce_scatter | solution.py:243
  9.7 45.1 %copy-start.37 = (s32[4095]{0:T(1024)}, s32[4095]{0:T(1024)S(1)}, u32[]{:S(2)}) copy-start(s32[4095]{0:T(1024)S(1)} %slice.211) | copy-start | bytes 49144
  27.8 51.6 %copy-start.26 = (bf16[192,768]{1,0:T(8,128)(2,1)}, bf16[192,768]{1,0:T(8,128)(2,1)S(1)}, u32[]{:S(2)}) copy-start(bf16[192,768]{1,0:T(8,128)(2,1)S(1)} %all_gather.46) | copy-start | bytes 884740
  37.1 17.7 copy-start.22
  46.0 14.1 copy-start.40
  54.8 28.7 copy-start.28
  54.8 14.4 copy-start.41
  69.2 15.5 copy-start.34
  260.4 15.4 copy-start.1
  586.0 15.4 copy-start.1
  911.5 15.4 copy-start.1
  1237.1 15.4 copy-start.1
  1402.3 9.4 copy-start.47
  1402.3 60.4 %copy-start.9 = (bf16[512,768]{1,0:T(8,128)(2,1)S(1)}, bf16[512,768]{1,0:T(8,128)(2,1)}, u32[]{:S(2)}) copy-start(bf16[512,768]{1,0:T(8,128)(2,1)} %param.19) | copy-start | bytes 2359300
  1402.3 78.8 %all-gather.14.cloned.1.call-start = ((), (), s32[]{:S(2)}) async-start(), calls=%async_computation.16 | async-start | bytes 1327104 | tf_op jit(solution)/shard_map/all_gather | solution.py:193
  1402.9 125.7 %all-gather.12.cloned.1.call-start = ((), (), s32[]{:S(2)}) async-start(), calls=%async_computation.15 | async-start | bytes 3932160 | tf_op jit(solution)/shard_map/all_gather | solution.py:252
  1462.7 6.4 copy-start.50
  1467.2 88.6 %all-gather.16.cloned.1.call-start = ((), (), s32[]{:S(2)}) async-start(), calls=%async_computation.17 | async-start | bytes 1327104 | tf_op jit(solution)/shard_map/all_gather | solution.py:194
  1467.8 153.9 %reduce-scatter.21.cloned.1.call-start = ((), (), s32[]{:S(2)}) async-start(), calls=%async_computation.18 | async-start | bytes 3932160 | tf_op jit(solution)/shard_map/reduce_scatter | solution.py:258
  1562.3 129.3 %all-gather.18.cloned.1.call-start = ((), (), s32[]{:S(2)}) async-start(), calls=%async_computation.19 | async-start | bytes 3932160 | tf_op jit(solution)/shard_map/all_gather | solution.py:271
  1629.7 139.6 %reduce-scatter.23.cloned.1.call-start = ((), (), s32[]{:S(2)}) async-start(), calls=%async_computation.20 | async-start | bytes 3932160 | tf_op jit(solution)/shard_map/reduce_scatter | solution.py:277
  1691.5 12.9 copy-start.49
  1708.5 128.7 %all-gather.20.cloned.1.call-start = ((), (), s32[]{:S(2)}) async-start(), calls=%async_computation.21 | async-start | bytes 3932160 | tf_op jit(solution)/shard_map/all_gather | solution.py:286
  1775.4 2283.5 %reduce-scatter.41.cloned.1.call-start = ((), (), s32[]{:S(2)}) async-start(), calls=%async_computation.31 | async-start | bytes 442368
  1776.5 2283.2 %reduce-scatter.43.cloned.1.call-start = ((), (), s32[]{:S(2)}) async-start(), calls=%async_computation.32 | async-start | bytes 442368
  1777.5 2309.8 %reduce-scatter.39.cloned.1.call-start = ((), (), s32[]{:S(2)}) async-start(), calls=%async_computation.29 | async-start | bytes 884736 | tf_op jit(solution)/shard_map/reduce_scatter | solution.py:392
  1845.1 2161.7 %copy-start.38 = (s32[4095]{0:T(1024)S(1)}, s32[4095]{0:T(1024)}, u32[]{:S(2)}) copy-start(s32[4095]{0:T(1024)} %copy-done.37) | copy-start | bytes 49144
  2018.7 15.4 copy-start.2
  2153.4 14.5 copy-start.11
  2221.9 27.1 slice-start
  2233.6 12.8 copy-start.3
  2233.6 15.4 slice-start.1
  2556.4 15.4 copy-start.2
  2691.1 14.7 copy-start.11
  2759.6 27.1 slice-start
  2771.3 12.8 copy-start.3
  2771.3 15.4 slice-start.1
  2893.6 5.9 copy-start.4
  3095.6 15.4 copy-start.2
  3230.2 14.5 copy-start.11
  3298.8 27.1 slice-start
  3310.4 12.8 copy-start.3
  3310.4 15.4 slice-start.1
  3432.4 5.9 copy-start.4
  3634.5 15.4 copy-start.2
  3769.1 14.7 copy-start.11
  3837.6 27.1 slice-start
  3849.3 12.8 copy-start.3
  3849.3 15.4 slice-start.1
  4006.8 6.0 copy-start.5
  4015.1 6.2 copy-start.32
  4015.3 7.7 copy-start.20
  4022.8 98.6 %reduce-scatter.25.cloned.1.call-start = ((), (), s32[]{:S(2)}) async-start(), calls=%async_computation.22 | async-start | bytes 3932160 | tf_op jit(solution)/shard_map/reduce_scatter | solution.py:373
  4028.8 139.5 %reduce-scatter.37.cloned.1.call-start = ((), (), s32[]{:S(2)}) async-start(), calls=%async_computation.28 | async-start | bytes 2654208 | tf_op jit(solution)/shard_map/reduce_scatter | solution.py:390
  4036.8 7.2 copy-start.13
  4036.8 177.9 %reduce-scatter.35.cloned.1.call-start = ((), (), s32[]{:S(2)}) async-start(), calls=%async_computation.27 | async-start | bytes 2654208 | tf_op jit(solution)/shard_map/reduce_scatter | solution.py:389
  4044.0 208.6 %reduce-scatter.29.cloned.1.call-start = ((), (), s32[]{:S(2)}) async-start(), calls=%async_computation.24 | async-start | bytes 663552 | tf_op jit(solution)/shard_map/reduce_scatter | solution.py:385
  4047.5 243.2 %reduce-scatter.27.cloned.1.call-start = ((), (), s32[]{:S(2)}) async-start(), calls=%async_computation.23 | async-start | bytes 663552 | tf_op jit(solution)/shard_map/reduce_scatter | solution.py:384
  4050.8 278.0 %reduce-scatter.33.cloned.1.call-start = ((), (), s32[]{:S(2)}) async-start(), calls=%async_computation.26 | async-start | bytes 663552 | tf_op jit(solution)/shard_map/reduce_scatter | solution.py:387
  4054.6 17.6 copy-start.44
  4054.6 66.8 %copy-start.43 = (f32[512]{0:T(512)S(1)}, f32[512]{0:T(512)}, u32[]{:S(2)}) copy-start(f32[512]{0:T(512)} %copy-done.42) | copy-start | bytes 6148
  4054.6 312.2 %reduce-scatter.31.cloned.1.call-start = ((), (), s32[]{:S(2)}) async-start(), calls=%async_computation.25 | async-start | bytes 663552 | tf_op jit(solution)/shard_map/reduce_scatter | solution.py:386
  4057.5 309.4 %all-reduce.15.cloned.1.call-start = ((), (), s32[]{:S(2)}) async-start(), calls=%async_computation.30 | async-start | bytes 196608 | tf_op jit(solution)/shard_map/psum | solution.py:396
  (42 other events, 119.7 us)
Sparse Core Ops, SparseCore 0:
  10.4 62.2 all-gather.9
  1402.4 60.1 reduce-scatter.18
  1629.8 61.7 all-gather.17
  1775.5 61.6 all-gather.19
  4087.5 55.3 all-reduce.14
Sparse Core Ops, SparseCore 1:
  1404.7 24.6 all-gather.13
  1467.3 61.3 all-gather.11
  1530.4 25.3 all-gather.15
  1562.4 59.2 reduce-scatter.20
  1708.5 60.6 reduce-scatter.22
  1779.2 34.1 reduce-scatter.40
  1816.3 33.8 reduce-scatter.42
  4022.9 35.7 reduce-scatter.38
  4060.8 60.5 reduce-scatter.24
  4125.4 42.9 reduce-scatter.36
  4172.4 42.3 reduce-scatter.34
  4218.5 34.1 reduce-scatter.28
  4256.2 34.3 reduce-scatter.26
  4294.3 34.3 reduce-scatter.32
  4332.4 34.3 reduce-scatter.30
where the time goes:
time: 4400 us; the launch traced here: 4380 us
  local copies, waits for them, and re-layouts  2910 us (66%)
  waiting for transfers between devices  618 us (14%)
  matrix products  524 us (12%)
  other arithmetic  138 us (3%)
  blocking collectives  107 us (2%)
  loops' own time  59.8 us (1%)
    while x100, local copies, waits for them, and re-layouts  725 us
    reshape x16, local copies, waits for them, and re-layouts, skew(): return cut.reshape(leading + (rows, span - 1))[..., :width]  564 us
    slice x16, local copies, waits for them, and re-layouts, skew(): lax.slice_in_dim(flat, rows - 1, rows - 1 + rows * (span - 1), axis=flat....  314 us
    reshape x8, local copies, waits for them, and re-layouts, skew(): flat = table.reshape(leading + (rows * span,))  296 us
    dot_general x8, local copies, waits for them, and re-layouts, block_scores(): jnp.einsum('kthd,kwhd->hktw', key_blocks, windows, preferred_element_type...  200 us
    reshape x8, local copies, waits for them, and re-layouts, unskew(): flat = widened.reshape(leading + (rows * (span - 1),))  154 us
    reshape x8, local copies, waits for them, and re-layouts, block_scores(): skew(from_keys, block, block).transpose(0, 3, 1, 2)  103 us
    dot_general x8, matrix products, block_scores(): jnp.einsum('rhd,jhd->hrj', query_tile_rows, key_seq, preferred_element_ty...  101 us
  transfers between devices with their start and end apart: 20, of which 14 were waited for; matrix products, arithmetic and copies ran while one was open for 51% of the time, Pallas kernels for 0%

commit v1 on v0

v1 whole, which is shorter than its diff:
```python
import functools
import math

import jax
import jax.numpy as jnp
from jax import lax
from jax.experimental import pallas as pl
from jax.experimental.pallas import tpu as pltpu
from jax.sharding import PartitionSpec as P

bf=jnp.bfloat16; f32=jnp.float32
DH=64; NB=256
SCALE=1.0/math.sqrt(3*DH)
LOG2E=math.log2(math.e)

def dot_nt(a,b):
    return lax.dot_general(a,b,(((1,),(1,)),((),())),preferred_element_type=f32)
def dot_nn(a,b):
    return lax.dot_general(a,b,(((1,),(0,)),((),())),preferred_element_type=f32)
def dot_tn(a,b):
    return lax.dot_general(a,b,(((0,),(0,)),((),())),preferred_element_type=f32)

def flip_matrix(n):
    a=lax.broadcasted_iota(jnp.int32,(n,n),0); b=lax.broadcasted_iota(jnp.int32,(n,n),1)
    return jnp.where(a+b==n-1,1.0,0.0).astype(bf)

def flip_rows(x):
    n,w=x.shape
    idx=7-lax.broadcasted_iota(jnp.int32,(8,w),0)
    return jnp.concatenate([jnp.take_along_axis(x[n-8-8*g:n-8*g],idx,axis=0) for g in range(n//8)],axis=0)

def fwd_kernel(R,L,B,C,mask_ref,q_ref,k_ref,v_ref,kt_ref,qr_ref,ctx_ref,scale_ref,e_ref,yt_ref,acc_ref):
    hh=pl.program_id(1)
    W=L+R
    def lanes(n): return (lax.broadcasted_iota(jnp.int32,(n,128),1)//DH)==hh
    zero=jnp.zeros((),bf)
    def yblock(i,_):
        j0=pl.multiple_of(i*C,C)
        kb=jnp.where(lanes(C),k_ref[pl.ds(j0,C),:],zero)
        us=pl.multiple_of(L-C-j0,C)
        y=dot_nt(kb,qr_ref[pl.ds(us,R+C),:])
        y=pltpu.roll(y,R+1,1,stride=1,stride_axis=0)[:,:R]
        yt_ref[:,pl.ds(j0,C)]=y.T+mask_ref[:,pl.ds(j0,C)]
        return 0
    lax.fori_loop(0,L//C,yblock,0,unroll=2)
    v_one=jnp.where(lanes(L),v_ref[...],jnp.ones((),bf))
    def strip(i,_):
        r0=pl.multiple_of(i*B,B)
        q=jnp.where(lanes(B),q_ref[pl.ds(r0,B),:],zero)
        ws=pl.multiple_of(R-B-r0,B)
        x=dot_nt(q,kt_ref[pl.ds(ws,L+B),:])
        x=pltpu.roll(x,L+1,1,stride=1,stride_axis=0)[:,:L]
        raw=dot_nt(q,k_ref[...])+x+yt_ref[pl.ds(r0,B),:]
        peak=jnp.max(raw,axis=1,keepdims=True)
        e=jnp.exp2((raw-peak)*(SCALE*LOG2E))
        e=flip_rows(e).astype(bf)
        rr=pl.multiple_of(R-B-r0,B)
        e_ref[0,pl.ds(rr,B),:]=e
        acc_ref[pl.ds(rr,B),:]=dot_nn(e,v_one)
        return 0
    lax.fori_loop(0,R//B,strip,0,unroll=2)
    acc=acc_ref[...]
    inv=1.0/pltpu.roll(acc,DH,1)
    ctx=dot_nn(flip_matrix(R),(acc*inv).astype(bf)).astype(bf)
    mine=lanes(R)
    inv_hi=inv.astype(bf)
    J=flip_matrix(R)
    sc=dot_nn(J,inv_hi)+dot_nn(J,(inv-inv_hi.astype(f32)).astype(bf))
    sc=sc*SCALE
    @pl.when(hh==0)
    def _():
        ctx_ref[...]=ctx
        scale_ref[...]=sc
    @pl.when(hh==1)
    def _():
        ctx_ref[...]=jnp.where(mine,ctx,ctx_ref[...])
        scale_ref[...]=jnp.where(mine,sc,scale_ref[...])

def attention_forward(q,k,v,kt,qr,mask,B=128,C=256):
    R,F=q.shape; L=k.shape[0]; W=L+R; pairs=F//128
    col=lambda n: pl.BlockSpec((n,128),lambda p,h:(0,p))
    flops=2*pairs*2*R*L*128*4
    return pl.pallas_call(functools.partial(fwd_kernel,R,L,B,C),
        grid=(pairs,2),
        in_specs=[pl.BlockSpec((1,L),lambda p,h:(0,0)),col(R),col(L),col(L),col(W),col(W)],
        out_specs=[col(R),col(R),pl.BlockSpec((1,R,L),lambda p,h:(2*p+h,0,0))],
        out_shape=[jax.ShapeDtypeStruct((R,F),bf),jax.ShapeDtypeStruct((R,F),f32),jax.ShapeDtypeStruct((2*pairs,R,L),bf)],
        scratch_shapes=[pltpu.VMEM((R,L),f32),pltpu.VMEM((R,128),f32)],
        compiler_params=pltpu.CompilerParams(vmem_limit_bytes=48*1024*1024,dimension_semantics=("arbitrary","arbitrary")),
        cost_estimate=pl.CostEstimate(flops=flops,bytes_accessed=2*pairs*R*L*2+10*L*F,transcendentals=2*pairs*R*L),
        name="attend",
    )(mask,q,k,v,kt,qr)

def bwd_kernel(R,L,B,C,q_ref,k_ref,v_ref,do_ref,ctx_ref,e_ref,kr_ref,qrel_ref,ox_ref,oy_ref,
               dq_ref,dk_ref,dv_ref,dkr_ref,dqr_ref,ds_ref,dor_ref,qrev_ref,dqa_ref,dka_ref,dva_ref):
    hh=pl.program_id(1)
    def lanes(n): return (lax.broadcasted_iota(jnp.int32,(n,128),1)//DH)==hh
    zero=jnp.zeros((),bf)
    @pl.when(hh==0)
    def _():
        dqa_ref[...]=jnp.zeros_like(dqa_ref)
        dka_ref[...]=jnp.zeros_like(dka_ref)
        dva_ref[...]=jnp.zeros_like(dva_ref)
        dkr_ref[...]=jnp.zeros_like(dkr_ref)
        dqr_ref[...]=jnp.zeros_like(dqr_ref)
    J=flip_matrix(R)
    do=jnp.where(lanes(R),dot_nn(J,do_ref[...]).astype(bf),zero)
    ctx=dot_nn(J,ctx_ref[...])
    dor_ref[...]=do
    qrev_ref[...]=jnp.where(lanes(R),dot_nn(J,q_ref[...]).astype(bf),zero)
    delta_all=jnp.sum(do.astype(f32)*ctx,axis=1,keepdims=True)
    own=lanes(B)
    for i in range(R//B):
        r0=i*B
        do_s=dor_ref[r0:r0+B,:]
        dp=dot_nt(do_s,v_ref[...])
        ds=(e_ref[0,r0:r0+B,:].astype(f32)*(dp-delta_all[r0:r0+B])).astype(bf)
        ds_ref[r0:r0+B,:]=ds
        wide=jnp.concatenate([ds,jnp.zeros((B,B),bf)],axis=1)
        wide=pltpu.roll(wide,0,1,stride=1,stride_axis=0)
        db=dot_nn(wide,ox_ref[r0:r0+L+B,:]).astype(bf)
        dq=dot_nn(ds,k_ref[...])+dot_nn(db,kr_ref[...])
        dqa_ref[r0:r0+B,:]=jnp.where(own,dq,dqa_ref[r0:r0+B,:])
        dkr_ref[...]+=dot_tn(db,qrev_ref[r0:r0+B,:])
    ownk=lanes(C)
    qrel=jnp.where(lanes(NB),qrel_ref[...],zero)
    def jblock(i,_):
        j0=pl.multiple_of(i*C,C)
        dst=ds_ref[:,pl.ds(j0,C)].T
        et=e_ref[0,:,pl.ds(j0,C)].T
        wide=jnp.concatenate([dst,jnp.zeros((C,C),bf)],axis=1)
        wide=pltpu.roll(wide,0,1,stride=1,stride_axis=0)
        db=dot_nn(wide,oy_ref[pl.ds(j0,R+C),:]).astype(bf)
        dka_ref[pl.ds(j0,C),:]+=dot_nn(dst,qrev_ref[...])+dot_nn(db,qrel)
        dva_ref[pl.ds(j0,C),:]+=dot_nn(et,dor_ref[...])
        kb=jnp.where(ownk,k_ref[pl.ds(j0,C),:],zero)
        dqr_ref[...]+=dot_tn(db,kb)
        return 0
    lax.fori_loop(0,L//C,jblock,0,unroll=2)
    @pl.when(hh==1)
    def _():
        dq_ref[...]=dot_nn(J,dqa_ref[...].astype(bf)).astype(bf)
        dk_ref[...]=dka_ref[...].astype(bf)
        dv_ref[...]=(dva_ref[...]*(1.0/SCALE)).astype(bf)

def attention_backward(q,k,v,do,ctx,e,key_rel,query_rel,onehot_x,onehot_y,B=128,C=256):
    R,F=q.shape; L=k.shape[0]; W=L+R; pairs=F//128
    col=lambda n: pl.BlockSpec((n,128),lambda p,h:(0,p))
    full=pl.BlockSpec((W,NB),lambda p,h:(0,0))
    flops=2*pairs*2*R*L*128*8
    return pl.pallas_call(functools.partial(bwd_kernel,R,L,B,C),
        grid=(pairs,2),
        in_specs=[col(R),col(L),col(L),col(R),col(R),pl.BlockSpec((1,R,L),lambda p,h:(2*p+h,0,0)),col(NB),col(NB),full,full],
        out_specs=[col(R),col(L),col(L),col(NB),col(NB)],
        out_shape=[jax.ShapeDtypeStruct((R,F),bf),jax.ShapeDtypeStruct((L,F),bf),jax.ShapeDtypeStruct((L,F),bf),
                   jax.ShapeDtypeStruct((NB,F),f32),jax.ShapeDtypeStruct((NB,F),f32)],
        scratch_shapes=[pltpu.VMEM((R,L),bf),pltpu.VMEM((R,128),bf),pltpu.VMEM((R,128),bf),
                        pltpu.VMEM((R,128),f32),pltpu.VMEM((L,128),f32),pltpu.VMEM((L,128),f32)],
        compiler_params=pltpu.CompilerParams(vmem_limit_bytes=48*1024*1024,dimension_semantics=("arbitrary","arbitrary")),
        cost_estimate=pl.CostEstimate(flops=flops,bytes_accessed=2*pairs*R*L*2+20*L*F,transcendentals=0),
        name="attend_back",
    )(q,k,v,do,ctx,e,key_rel,query_rel,onehot_x,onehot_y)

EPS=1e-06
ALL=("tensor","dp")

def layer_norm(values, gain, shift):
    middle = jnp.mean(values, axis=-1, keepdims=True)
    centered = values - middle
    spread = jnp.mean(centered * centered, axis=-1, keepdims=True)
    return centered * lax.rsqrt(spread + EPS) * gain + shift

def exact_gelu(values):
    return jax.nn.gelu(values, approximate=False)

def project(inputs, weights, bias):
    return (jnp.einsum("td,fd->tf", inputs, weights, preferred_element_type=f32) + bias).astype(bf)

def local(tokens, w_query, w_key, w_value, w_out, qkv_bias, w_ff_in, w_ff_out, ff_bias, rel_table,
          gains, shifts, rel_bucket, lengths, out_grad):
    D = tokens.shape[1]
    n_t, n_dp = lax.axis_size("tensor"), lax.axis_size("dp")
    n_all = n_t * n_dp
    t = lax.axis_index("tensor")
    R = tokens.shape[0]
    L = (rel_bucket.shape[0] + 1) // 2
    W = L + R
    part = rel_table.shape[0] // n_t
    wide, inner, cols = qkv_bias.shape[1], ff_bias.shape[0], gains.shape[1]
    misc = jnp.concatenate([qkv_bias.reshape(-1), ff_bias, gains.reshape(-1), shifts.reshape(-1)])
    used = misc.shape[0]
    misc = jnp.pad(misc, (0, D - used))[None]
    rel_part = lax.dynamic_slice_in_dim(rel_table, t * part, part, 0)
    small = jnp.concatenate([misc, rel_part], axis=0)
    gather = lambda x: lax.all_gather(x, ALL, axis=0, tiled=True)
    small_all = lax.all_gather(small, ALL, axis=0, tiled=False)
    query_rows, key_rows, value_rows, out_rows = gather(w_query), gather(w_key), gather(w_value), gather(w_out)
    inner_rows, outer_rows = gather(w_ff_in), gather(w_ff_out)
    misc_all = small_all[:, 0]
    o1 = 3 * wide
    o2 = o1 + inner
    o3 = o2 + 2 * cols
    bias = misc_all[:, :o1].reshape(n_all, 3, wide).transpose(1, 0, 2).reshape(3, D).astype(f32)
    inner_bias = misc_all[:, o1:o2].reshape(-1).astype(f32)
    first = misc_all[:n_dp]
    gain = first[:, o2:o3].reshape(n_dp, 2, cols).transpose(1, 0, 2).reshape(2, D).astype(f32)
    shift = first[:, o3:used].reshape(n_dp, 4, cols).transpose(1, 0, 2).reshape(4, D).astype(f32)
    table = small_all[:, 1:].reshape(n_t, n_dp, part, D).transpose(1, 0, 2, 3).reshape(NB, D)

    gathered = lax.all_gather(tokens, "tensor", axis=0, tiled=True)
    query = project(tokens, query_rows, bias[0])
    key = project(gathered, key_rows, bias[1])
    value = project(gathered, value_rows, bias[2])
    key_rel = project(table, key_rows, bias[1])
    query_rel = project(table, query_rows, bias[0])

    none = jnp.full((1,), -1, jnp.int32)
    ahead = jnp.concatenate([rel_bucket, none])
    back = jnp.concatenate([rel_bucket[::-1], none])
    buckets = jnp.arange(NB, dtype=jnp.int32)[None, :]
    pick = lambda line, start: (lax.dynamic_slice_in_dim(line, start, W, 0)[:, None] == buckets).astype(bf)
    pick_x = pick(back, L - R - R * t)
    pick_y = pick(ahead, L - R - R * t)
    pick_u = pick(back, R * t)
    key_table = jnp.dot(pick_x, key_rel, preferred_element_type=f32).astype(bf)
    query_table = jnp.dot(pick_u, query_rel, preferred_element_type=f32).astype(bf)
    mask = jnp.where(jnp.arange(L, dtype=jnp.int32)[None, :] < lengths[0], 0.0, -1e9).astype(f32)

    context, scale, shares = attention_forward(query, key, value, key_table, query_table, mask)
    attended = jnp.dot(context, out_rows, preferred_element_type=f32)
    resid_one = tokens.astype(f32) + attended + shift[0]
    hidden_one, norm_one_back = jax.vjp(layer_norm, resid_one, gain[0], shift[1])
    hidden_low = hidden_one.astype(bf)
    pre = jnp.einsum("td,fd->tf", hidden_low, inner_rows, preferred_element_type=f32) + inner_bias
    activated, gelu_back = jax.vjp(exact_gelu, pre)
    gated = activated.astype(bf)
    feed_out = jnp.dot(gated, outer_rows, preferred_element_type=f32)
    resid_two = hidden_one + feed_out + shift[2]
    final_value, norm_two_back = jax.vjp(layer_norm, resid_two, gain[1], shift[3])
    layer_result_rows = final_value.astype(bf)
    d_resid_two, d_gain_two, d_shift_three = norm_two_back(out_grad.astype(f32))
    d_shift_two = jnp.sum(d_resid_two, axis=0)
    d_feed = d_resid_two.astype(bf)
    d_gated = jnp.einsum("td,fd->tf", d_feed, outer_rows, preferred_element_type=f32)
    grad_outer = jnp.einsum("tf,td->fd", gated, d_feed, preferred_element_type=f32)
    d_pre = gelu_back(d_gated)[0].astype(bf)
    grad_inner = jnp.einsum("tf,td->fd", d_pre, hidden_low, preferred_element_type=f32)
    grad_bias_inner = jnp.sum(d_pre.astype(f32), axis=0)
    d_hidden_one = d_resid_two + jnp.dot(d_pre, inner_rows, preferred_element_type=f32)
    d_resid_one, d_gain_one, d_shift_one = norm_one_back(d_hidden_one)
    d_shift_zero = jnp.sum(d_resid_one, axis=0)
    d_attended = d_resid_one.astype(bf)
    grad_out = jnp.einsum("tf,td->fd", context, d_attended, preferred_element_type=f32)
    d_context = jnp.einsum("td,fd->tf", d_attended, out_rows, preferred_element_type=f32)
    d_scaled = (d_context * scale).astype(bf)
    d_query, d_key, d_value, d_key_rel, d_query_rel = attention_backward(
        query, key, value, d_scaled, context, shares, key_rel, query_rel, pick_x, pick_y)

    scatter = lambda x: lax.psum_scatter(x, ALL, scatter_dimension=0, tiled=True)
    lowered = lambda x: scatter(x.astype(bf)).astype(f32)
    g_inner, g_outer, g_out = lowered(grad_inner), lowered(grad_outer), lowered(grad_out)
    dqr, dkr = d_query_rel.astype(bf), d_key_rel.astype(bf)
    grad_query = jnp.einsum("tf,td->fd", d_query, tokens, preferred_element_type=f32) + jnp.einsum(
        "tf,td->fd", dqr, table, preferred_element_type=f32)
    grad_key = jnp.einsum("tf,td->fd", d_key, gathered, preferred_element_type=f32) + jnp.einsum(
        "tf,td->fd", dkr, table, preferred_element_type=f32)
    grad_value = jnp.einsum("tf,td->fd", d_value, gathered, preferred_element_type=f32)
    bias_gradient = jnp.stack([
        jnp.sum(d_query.astype(f32), axis=0) + jnp.sum(d_query_rel, axis=0),
        jnp.sum(d_key.astype(f32), axis=0) + jnp.sum(d_key_rel, axis=0),
        jnp.sum(d_value.astype(f32), axis=0)])
    d_rel = jnp.dot(dqr, query_rows, preferred_element_type=f32) + jnp.dot(dkr, key_rows, preferred_element_type=f32)
    own = jnp.dot(d_query, query_rows, preferred_element_type=f32)
    spread = (jnp.dot(d_key, key_rows, preferred_element_type=f32)
              + jnp.dot(d_value, value_rows, preferred_element_type=f32)).astype(bf)
    back_sum = lax.psum_scatter(spread, "tensor", scatter_dimension=0, tiled=True)
    tokens_grad = d_resid_one + own + back_sum.astype(f32)
    g_query, g_key, g_value = lowered(grad_query), lowered(grad_key), lowered(grad_value)

    gain_grads = jnp.stack([d_gain_one, d_gain_two])
    shift_grads = jnp.stack([d_shift_zero, d_shift_one, d_shift_two, d_shift_three])
    shape_dp = lambda x, k: jnp.broadcast_to(
        x.reshape(k, n_dp, cols).transpose(1, 0, 2).reshape(1, n_dp, k * cols), (n_t, n_dp, k * cols)).reshape(n_all, k * cols)
    line = jnp.concatenate([
        bias_gradient.reshape(3, n_all, wide).transpose(1, 0, 2).reshape(n_all, o1),
        grad_bias_inner.reshape(n_all, inner),
        shape_dp(gain_grads, 2), shape_dp(shift_grads, 4)], axis=1)
    line = jnp.pad(line, ((0, 0), (0, D - used)))[:, None]
    rel_rows = rel_table.shape[0]
    d_rel_all = jnp.broadcast_to(d_rel.reshape(1, n_dp, rel_rows, D), (n_t, n_dp, rel_rows, D)).reshape(n_all, rel_rows, D)
    packed = jnp.concatenate([line, d_rel_all], axis=1)
    small_grad = lax.psum_scatter(packed, ALL, scatter_dimension=0, tiled=True)[0]
    row = small_grad[0]
    return (layer_result_rows, tokens_grad, g_query, g_key, g_value, g_out,
            row[:o1].reshape(3, wide), g_inner, g_outer, row[o1:o2], small_grad[1:],
            row[o2:o3].reshape(2, cols), row[o3:used].reshape(4, cols))

def solution(mesh):
    rows, params = P(("dp", "tensor"), None), P(ALL, None)
    return jax.shard_map(
        local, mesh=mesh,
        in_specs=(rows, params, params, params, params, P(None, ALL), params, params, P(ALL), P("dp", None),
                  P(None, "dp"), P(None, "dp"), P(), P("dp"), rows),
        out_specs=(rows, rows, params, params, params, params, P(None, ALL), params, params, P(ALL), P("dp", None),
                   P(None, "dp"), P(None, "dp")),
        check_vma=False)
```

time: 4400 us -> 1390 us (0.32)
  local copies, waits for them, and re-layouts: 2910 us -> 20 us
  matrix products: 524 us -> 118 us
  waiting for transfers between devices: 618 us -> 940 us
  Pallas kernels: 0 us -> 216 us
  other arithmetic: 138 us -> 25.5 us
  blocking collectives: 107 us -> 35.2 us
  loops' own time: 59.8 us -> 0 us
    reshape x60 -> x10, local copies, waits for them, and re-layouts: 1210 us -> 4.4 us  [the longest x1 0.76 us: local(): shifts.reshape(-1)]
    while x101 -> x0, local copies, waits for them, and re-layouts: 727 us -> none
    slice x62 -> x13, local copies, waits for them, and re-layouts: 502 us -> 5.6 us  [the longest x1 1.55 us: local(): small_grad[1:]]
    dot_general x86 -> x26, matrix products: 524 us -> 118 us  [the longest x1 22.2 us: local(): jnp.einsum('td,fd->tf', hidden_low, inner_rows, preferred_element_type=f32)]
    reduce_scatter x11 -> x8, waiting for transfers between devices: 439 us -> 713 us  [the longest x6 545 us: local(): lax.psum_scatter(x, ALL, scatter_dimension=0, tiled=True)]
    pallas_call x0 -> x2, Pallas kernels: none -> 216 us  [the longest x1 118 us: attention_backward(): pl.pallas_call(functools.partial(bwd_kernel, R, L, B, C), grid=(pairs, 2)...]
    dot_general x8 -> x0, local copies, waits for them, and re-layouts: 200 us -> none  [block_scores(): jnp.einsum('kthd,kwhd->hktw', key_blocks, windows, preferred_element_type...]
    pad x18 -> x0, local copies, waits for them, and re-layouts: 149 us -> none  [the longest x8 82.6 us: unskew(): placed = jnp.pad(flat, [(0, 0)] * len(leading) + [(rows - 1, 1)])]
  transfers between devices with their start and end apart: 20 -> 15, of which waited for: 14 -> 14; matrix products, arithmetic and copies ran while one was open for 51% -> 9% of each run, Pallas kernels for 0% -> 7%
where the time goes in v1:
time: 1390 us; the launch traced here: 1370 us
  waiting for transfers between devices  940 us (68%)
  Pallas kernels  216 us (16%)
  matrix products  118 us (8%)
  blocking collectives  35.2 us (3%)
  other arithmetic  25.5 us (2%)
  local copies, waits for them, and re-layouts  20 us (1%)
  between operations  15.6 us (1%)
    reduce_scatter x6, waiting for transfers between devices, local(): lax.psum_scatter(x, ALL, scatter_dimension=0, tiled=True)  545 us
    all_gather x6, waiting for transfers between devices, local(): gather = lambda x: lax.all_gather(x, ALL, axis=0, tiled=True)  172 us
    pallas_call x1, Pallas kernels, attention_backward(): pl.pallas_call(functools.partial(bwd_kernel, R, L, B, C), grid=(pairs, 2)...  118 us
    reduce_scatter x1, waiting for transfers between devices, local(): lax.psum_scatter(packed, ALL, scatter_dimension=0, tiled=True)[0]  107 us
    pallas_call x1, Pallas kernels, attention_forward(): pl.pallas_call(functools.partial(fwd_kernel, R, L, B, C), grid=(pairs, 2)...  97.6 us
    reduce_scatter x1, waiting for transfers between devices, local(): lax.psum_scatter(spread, 'tensor', scatter_dimension=0, tiled=True)  61.3 us
    all_gather x1, waiting for transfers between devices, local(): gathered = lax.all_gather(tokens, 'tensor', axis=0, tiled=True)  50.6 us
    all_gather x1, blocking collectives, local(): small_all = lax.all_gather(small, ALL, axis=0, tiled=False)  35.2 us
  transfers between devices with their start and end apart: 15, of which 14 were waited for; matrix products, arithmetic and copies ran while one was open for 9% of the time, Pallas kernels for 7%

profile of v1, /device:TPU:13, one launch (start us, length us, event | category | flops | bytes accessed | tf_op | source)
XLA Modules:
  0.0 1371.5 jit_solution(341414678655521845)
XLA Ops:
  15.0 35.2 %all-gather.1 = bf16[32,9,768]{2,1,0:T(8,128)(2,1)S(1)} all-gather(bf16[1,9,768]{2,1,0:T(8,128)(2,1)S(1)} %maximum_bitcast_fusion.1), channel_id=2, replica_groups=mesh['dp'=8,'tensor'=4] {'tensor','dp'}, dimensions={0}, use_global_device_ids=true | all-gather | bytes 456192 | tf_op jit(solution)/shard_map/all_gather | solution.py:196
  53.1 2.8 fusion.6
  55.9 10.6 all-gather.14.cloned.1.call-done
  66.5 1.8 fusion.15.kr_ref
  68.3 54.0 %all-gather.10.cloned.1.call-done = bf16[768,768]{1,0:T(8,128)(2,1)} async-done(((bf16[24,768]{1,0:T(8,128)(2,1)}), bf16[768,768]{1,0:T(8,128)(2,1)}) %all-gather.10.cloned.1.call-update) | async-done | bytes 1179664 | tf_op jit(solution)/shard_map/all_gather | solution.py:195
  122.3 1.8 fusion.16.qrel_ref
  124.1 3.0 add_convert_fusion.7.q_ref
  127.1 3.4 convolution_convert_fusion.1.kt_ref
  130.5 3.4 convolution_convert_fusion.qr_ref
  133.8 50.6 %all-gather.12.cloned.1.call-done = bf16[2048,768]{1,0:T(8,128)(2,1)} async-done(((bf16[512,768]{1,0:T(8,128)(2,1)}), bf16[2048,768]{1,0:T(8,128)(2,1)}) %all-gather.12.cloned.1.call-update) | async-done | bytes 3145744 | tf_op jit(solution)/shard_map/all_gather | solution.py:210
  184.5 6.2 add_convert_fusion.3.k_ref
  190.7 51.2 %all-gather.16.cloned.1.call-done = bf16[768,768]{1,0:T(8,128)(2,1)} async-done(((bf16[24,768]{1,0:T(8,128)(2,1)}), bf16[768,768]{1,0:T(8,128)(2,1)}) %all-gather.16.cloned.1.call-update) | async-done | bytes 1179664 | tf_op jit(solution)/shard_map/all_gather | solution.py:195
  241.8 6.6 add_convert_fusion.2.v_ref
  248.5 97.6 %attend.1 = (bf16[512,768]{1,0:T(8,128)(2,1)S(1)}, f32[512,768]{1,0:T(8,128)S(1)}, bf16[12,512,2048]{2,1,0:T(8,128)(2,1)}) custom-call(f32[1,2048]{1,0:T(1,128)S(1)} %compare_select_fusion.mask_ref, bf16[512,768]{1,0:T(8,128)(2,1)S(1)} %copy-done.5, bf16[2048,768]{1,0:T(8,128)(2,1)} %add_convert_fusion.3.k_ref, bf16[2048,768]{1,0:T(8,128)(2,1)} %add_convert_fusion.2.v_ref, ...), custom_call_target="tpu_custom_call" | custom-call | flops 12884901888 | bytes 40894464 | tf_op jit(solution)/shard_map/attend/pallas_call | solution.py:83
  346.1 0.9 copy-done.2
  347.0 2.6 fusion.42
  349.6 1.1 copy-done.10
  351.1 13.2 all-gather.20.cloned.1.call-done
  364.3 22.2 %multiply_convert_fusion = (bf16[512,3072]{1,0:T(8,128)(2,1)}, f32[512,3072]{1,0:T(8,128)}, f32[512,3072]{1,0:T(8,128)}) fusion(f32[3072]{0:T(1024)S(1)} %reshape.270, bf16[3072,768]{1,0:T(8,128)(2,1)} %all-gather.20.cloned.1.call-done, f32[512,768]{1,0:T(8,128)} %copy-done.10, f32[768]{0:T(1024)S(1)} %add.221, f32[768]{0:T(1024)S(1)} %mul.156, ...), kind=kOutput, calls=%fused_computation.7 | convolution fusion | flops 2521694208 | bytes 22042624 | tf_op jit(solution)/shard_map/td,fd->tf/dot_general | solution.py:234
  386.4 43.3 %all-gather.22.cloned.1.call-done = bf16[3072,768]{1,0:T(8,128)(2,1)} async-done(((bf16[96,768]{1,0:T(8,128)(2,1)}), bf16[3072,768]{1,0:T(8,128)(2,1)}) %all-gather.22.cloned.1.call-update) | async-done | bytes 4718608 | tf_op jit(solution)/shard_map/all_gather | solution.py:195
  429.7 6.5 fusion.43
  437.3 1.6 fusion.39
  438.9 9.3 convert_reduce_fusion
  448.3 3.0 multiply_reduce_fusion
  452.6 0.8 multiply_convert_fusion.1.do_ref
  454.0 118.1 %attend_back.1 = (bf16[512,768]{1,0:T(8,128)(2,1)S(1)}, bf16[2048,768]{1,0:T(8,128)(2,1)}, bf16[2048,768]{1,0:T(8,128)(2,1)}, f32[256,768]{1,0:T(8,128)S(1)}, f32[256,768]{1,0:T(8,128)S(1)}) custom-call(bf16[512,768]{1,0:T(8,128)(2,1)S(1)} %copy-done.6, bf16[2048,768]{1,0:T(8,128)(2,1)} %add_convert_fusion.3.k_ref, ...), custom_call_target="tpu_custom_call" | custom-call | flops 25769803776 | bytes 56623104 | tf_op jit(solution)/shard_map/attend_back/pallas_call | solution.py:151
  572.1 0.8 fusion.45
  573.1 1.5 add_convert_fusion.5
  574.9 5.6 fusion.46
  580.5 1.6 add_convert_fusion.4
  582.1 6.6 convolution_convert_fusion.5
  589.0 1.6 add_reduce_fusion.1
  590.8 1.6 add_reduce_fusion
  592.9 2.6 convert_reduce_fusion.1
  596.4 1.9 convolution_convert_fusion.4
  599.2 1.8 fusion.19
  601.0 1.8 convolution_add_fusion.1
  603.1 2.4 pad_maximum_fusion
  605.8 1.1 copy-done.12
  606.9 6.9 convolution_convert_fusion.3
  613.9 1.2 copy-done.23
  615.1 4.7 fusion.44
  619.8 4.0 add_convert_fusion
  623.9 1.3 copy-done.14
  625.2 6.8 convolution_convert_fusion.2
  632.1 35.2 %reduce-scatter.11.cloned.1.call-done = bf16[24,768]{1,0:T(8,128)(2,1)} async-done(((bf16[768,768]{1,0:T(8,128)(2,1)}), bf16[24,768]{1,0:T(8,128)(2,1)}) %reduce-scatter.11.cloned.1.call-update) | async-done | bytes 36880 | tf_op jit(solution)/shard_map/reduce_scatter | solution.py:259
  667.2 1.4 convert_element_type.192
  668.6 99.0 %reduce-scatter.13.cloned.1.call-done = bf16[24,768]{1,0:T(8,128)(2,1)} async-done(((bf16[768,768]{1,0:T(8,128)(2,1)}), bf16[24,768]{1,0:T(8,128)(2,1)}) %reduce-scatter.13.cloned.1.call-update) | async-done | bytes 36880 | tf_op jit(solution)/shard_map/reduce_scatter | solution.py:259
  767.6 1.4 convert_element_type.195
  769.0 98.8 %reduce-scatter.15.cloned.1.call-done = bf16[24,768]{1,0:T(8,128)(2,1)} async-done(((bf16[768,768]{1,0:T(8,128)(2,1)}), bf16[24,768]{1,0:T(8,128)(2,1)}) %reduce-scatter.15.cloned.1.call-update) | async-done | bytes 36880 | tf_op jit(solution)/shard_map/reduce_scatter | solution.py:259
  867.8 1.4 convert_element_type.197
  869.2 99.0 %reduce-scatter.17.cloned.1.call-done = bf16[24,768]{1,0:T(8,128)(2,1)} async-done(((bf16[768,768]{1,0:T(8,128)(2,1)}), bf16[24,768]{1,0:T(8,128)(2,1)}) %reduce-scatter.17.cloned.1.call-update) | async-done | bytes 36880 | tf_op jit(solution)/shard_map/reduce_scatter | solution.py:259
  968.2 1.4 convert_element_type.199
  969.6 106.8 %reduce-scatter.19.cloned.1.call-done = f32[1,33,768]{2,1,0:T(8,128)} async-done(((f32[32,33,768]{2,1,0:T(8,128)}), f32[1,33,768]{2,1,0:T(8,128)}) %reduce-scatter.19.cloned.1.call-update) | async-done | bytes 101392 | tf_op jit(solution)/shard_map/reduce_scatter | solution.py:292
  1077.7 0.8 slice_reduce_fusion.7
  1079.2 0.8 slice_reduce_fusion.6
  1080.6 1.3 slice_bitcast_fusion.1
  1081.9 1.5 slice_bitcast_fusion
  1083.5 104.5 %reduce-scatter.21.cloned.1.call-done = bf16[96,768]{1,0:T(8,128)(2,1)} async-done(((bf16[3072,768]{1,0:T(8,128)(2,1)}), bf16[96,768]{1,0:T(8,128)(2,1)}) %reduce-scatter.21.cloned.1.call-update) | async-done | bytes 147472 | tf_op jit(solution)/shard_map/reduce_scatter | solution.py:259
  1188.0 1.6 convert_element_type.205
  1189.6 61.3 %reduce-scatter.9.cloned.1.call-done = bf16[512,768]{1,0:T(8,128)(2,1)} async-done(((bf16[2048,768]{1,0:T(8,128)(2,1)}), bf16[512,768]{1,0:T(8,128)(2,1)}) %reduce-scatter.9.cloned.1.call-update) | async-done | bytes 786448 | tf_op jit(solution)/shard_map/reduce_scatter | solution.py:276
  1250.9 3.4 convert_add_fusion
  1254.3 108.6 %reduce-scatter.23.cloned.1.call-done = bf16[96,768]{1,0:T(8,128)(2,1)} async-done(((bf16[3072,768]{1,0:T(8,128)(2,1)}), bf16[96,768]{1,0:T(8,128)(2,1)}) %reduce-scatter.23.cloned.1.call-update) | async-done | bytes 147472 | tf_op jit(solution)/shard_map/reduce_scatter | solution.py:259
  1362.9 1.6 convert_element_type.207
  (171 shorter events, 19.6 us)
Async XLA Ops:
  7.2 7.8 copy-start
  7.2 45.3 %copy-start.25 = (s32[4095]{0:T(1024)S(1)}, s32[4095]{0:T(1024)}, u32[]{:S(2)}) copy-start(s32[4095]{0:T(1024)} %param.27) | copy-start | bytes 49144
  7.2 59.3 %all-gather.14.cloned.1.call-start = ((), (), s32[]{:S(2)}) async-start(), calls=%async_computation.10 | async-start | bytes 1216512 | tf_op jit(solution)/shard_map/all_gather | solution.py:195
  7.9 114.4 %all-gather.10.cloned.1.call-start = ((), (), s32[]{:S(2)}) async-start(), calls=%async_computation.8 | async-start | bytes 1216512 | tf_op jit(solution)/shard_map/all_gather | solution.py:195
  8.7 175.8 %all-gather.12.cloned.1.call-start = ((), (), s32[]{:S(2)}) async-start(), calls=%async_computation.9 | async-start | bytes 3932160 | tf_op jit(solution)/shard_map/all_gather | solution.py:210
  9.4 232.4 %all-gather.16.cloned.1.call-start = ((), (), s32[]{:S(2)}) async-start(), calls=%async_computation.11 | async-start | bytes 1216512 | tf_op jit(solution)/shard_map/all_gather | solution.py:195
  10.0 337.0 %all-gather.18.cloned.1.call-start = ((), (), s32[]{:S(2)}) async-start(), calls=%async_computation.12 | async-start | bytes 1216512 | tf_op jit(solution)/shard_map/all_gather | solution.py:195
  10.6 353.7 %all-gather.20.cloned.1.call-start = ((), (), s32[]{:S(2)}) async-start(), calls=%async_computation.13 | async-start | bytes 4866048 | tf_op jit(solution)/shard_map/all_gather | solution.py:195
  11.2 418.5 %all-gather.22.cloned.1.call-start = ((), (), s32[]{:S(2)}) async-start(), calls=%async_computation.14 | async-start | bytes 4866048 | tf_op jit(solution)/shard_map/all_gather | solution.py:195
  11.9 655.3 %reduce-scatter.11.cloned.1.call-start = ((), (), s32[]{:S(2)}) async-start(), calls=%async_computation.16 | async-start | bytes 1216512 | tf_op jit(solution)/shard_map/reduce_scatter | solution.py:259
  52.4 71.6 %copy-start.15 = (bf16[8,4,8,768]{3,2,1,0:T(8,128)(2,1)}, bf16[8,4,8,768]{3,2,1,0:T(8,128)(2,1)S(1)}, u32[]{:S(2)}) copy-start(bf16[8,4,8,768]{3,2,1,0:T(8,128)(2,1)S(1)} %copy.55) | copy-start | bytes 1179652
  55.9 68.2 %copy-start.20 = (bf16[512,768]{1,0:T(8,128)(2,1)S(1)}, bf16[512,768]{1,0:T(8,128)(2,1)}, u32[]{:S(2)}) copy-start(bf16[512,768]{1,0:T(8,128)(2,1)} %param.15) | copy-start | bytes 2359300
  130.5 54.0 %copy-start.22 = (bf16[768,768]{1,0:T(8,128)(2,1)S(1)}, bf16[768,768]{1,0:T(8,128)(2,1)}, u32[]{:S(2)}) copy-start(bf16[768,768]{1,0:T(8,128)(2,1)} %all-gather.14.cloned.1.call-done) | copy-start | bytes 3538948
  241.8 6.6 copy-start.5
  346.1 0.9 copy-start.2
  349.6 1.1 copy-start.10
  429.7 6.9 copy-start.19
  437.3 10.9 slice-start
  438.9 9.3 copy-start.13
  438.9 9.3 copy-start.11
  438.9 9.3 slice-start.1
  448.2 3.1 copy-start.27
  451.3 1.3 copy-start.24
  451.9 120.2 %copy-start.7 = (f32[512,768]{1,0:T(8,128)}, f32[512,768]{1,0:T(8,128)S(1)}, u32[]{:S(2)}) copy-start(f32[512,768]{1,0:T(8,128)S(1)} %get-tuple-element.42) | copy-start | bytes 4718596
  451.9 1.8 copy-start.3
  452.0 2.0 copy-start.6
  454.0 118.1 %copy-start.21 = (bf16[512,768]{1,0:T(8,128)(2,1)S(1)}, bf16[512,768]{1,0:T(8,128)(2,1)}, u32[]{:S(2)}) copy-start(bf16[512,768]{1,0:T(8,128)(2,1)} %param.15) | copy-start | bytes 2359300
  572.1 1.0 copy-start.16
  574.6 192.9 %reduce-scatter.13.cloned.1.call-start = ((), (), s32[]{:S(2)}) async-start(), calls=%async_computation.17 | async-start | bytes 1216512 | tf_op jit(solution)/shard_map/reduce_scatter | solution.py:259
  582.1 285.8 %reduce-scatter.15.cloned.1.call-start = ((), (), s32[]{:S(2)}) async-start(), calls=%async_computation.18 | async-start | bytes 1216512 | tf_op jit(solution)/shard_map/reduce_scatter | solution.py:259
  588.8 379.4 %reduce-scatter.17.cloned.1.call-start = ((), (), s32[]{:S(2)}) async-start(), calls=%async_computation.19 | async-start | bytes 1216512 | tf_op jit(solution)/shard_map/reduce_scatter | solution.py:259
  592.8 2.9 copy-start.18
  592.9 3.3 copy-start.4
  592.9 3.5 copy-start.8
  598.4 478.0 %reduce-scatter.19.cloned.1.call-start = ((), (), s32[]{:S(2)}) async-start(), calls=%async_computation.20 | async-start | bytes 4055040 | tf_op jit(solution)/shard_map/reduce_scatter | solution.py:292
  605.5 1.4 copy-start.12
  605.5 582.5 %reduce-scatter.21.cloned.1.call-start = ((), (), s32[]{:S(2)}) async-start(), calls=%async_computation.21 | async-start | bytes 4866048 | tf_op jit(solution)/shard_map/reduce_scatter | solution.py:259
  613.8 1.3 copy-start.23
  613.8 6.0 copy-start.26
  613.8 637.1 %reduce-scatter.9.cloned.1.call-start = ((), (), s32[]{:S(2)}) async-start(), calls=%async_computation.15 | async-start | bytes 3932160 | tf_op jit(solution)/shard_map/reduce_scatter | solution.py:276
  615.1 4.7 copy-start.17
  623.8 1.4 copy-start.14
  623.9 739.1 %reduce-scatter.23.cloned.1.call-start = ((), (), s32[]{:S(2)}) async-start(), calls=%async_computation.22 | async-start | bytes 4866048 | tf_op jit(solution)/shard_map/reduce_scatter | solution.py:259
  632.0 618.9 %copy-start.9 = (f32[512,768]{1,0:T(8,128)S(1)}, f32[512,768]{1,0:T(8,128)}, u32[]{:S(2)}) copy-start(f32[512,768]{1,0:T(8,128)} %copy-done.7) | copy-start | bytes 4718596
  1188.0 176.6 %copy-start.1 = (bf16[32,768]{1,0:T(8,128)(2,1)S(1)}, bf16[32,768]{1,0:T(8,128)(2,1)}, u32[]{:S(2)}) copy-start(bf16[32,768]{1,0:T(8,128)(2,1)} %param.24) | copy-start | bytes 147460
Sparse Core Ops, SparseCore 0:
  10.9 55.5 all-gather.13
  69.4 52.8 all-gather.9
  123.9 60.5 all-gather.11
  187.2 54.5 all-gather.15
  244.6 52.9 all-gather.17
  300.3 63.8 all-gather.19
  367.1 62.4 all-gather.21
  574.8 92.4 reduce-scatter.10
  672.3 95.2 reduce-scatter.12
  772.5 95.2 reduce-scatter.14
  872.9 95.2 reduce-scatter.16
  973.4 102.8 reduce-scatter.18
  1081.8 106.1 reduce-scatter.20
  1190.2 60.6 reduce-scatter.8
  1257.1 105.7 reduce-scatter.22

commit v2 on v1

--- a/solution.py
+++ b/solution.py
@@ -8,7 +8,8 @@
 from jax.experimental.pallas import tpu as pltpu
 from jax.sharding import PartitionSpec as P
 
-bf=jnp.bfloat16; f32=jnp.float32
+bf = jnp.bfloat16
+f32 = jnp.float32
 DH=64; NB=256
 SCALE=1.0/math.sqrt(3*DH)
 LOG2E=math.log2(math.e)
@@ -161,6 +162,240 @@
         name="attend_back",
     )(q,k,v,do,ctx,e,key_rel,query_rel,onehot_x,onehot_y)
 
+MESH=pl.DeviceIdType.MESH
+
+def places(n_t, n_dp):
+    dp, t = lax.axis_index("dp"), lax.axis_index("tensor")
+    high, core = dp // 2, dp % 2
+    bits = (n_dp // 2).bit_length() - 1
+    flips = [high + (1 - 2 * ((high // 2**i) % 2)) * 2**i for i in range(bits)]
+    right, left = lax.rem(t + 1, n_t), lax.rem(t + n_t - 1, n_t)
+    return dp, t, high, core, bits, flips, right, left
+
+def meet(peers):
+    barrier = pltpu.get_barrier_semaphore()
+    for peer in peers:
+        pl.semaphore_signal(barrier, inc=1, device_id=peer, device_id_type=MESH)
+    pl.semaphore_wait(barrier, len(peers))
+
+def remote(src, dst, send, recv, peer):
+    return pltpu.make_async_remote_copy(src_ref=src, dst_ref=dst, send_sem=send, recv_sem=recv,
+                                        device_id=peer, device_id_type=MESH)
+
+def interleave(*lists):
+    out = []
+    for i in range(max(len(x) for x in lists)):
+        out += [x[i] for x in lists if i < len(x)]
+    return out
+
+def gather_kernel(n_t, n_dp, tok_ref, pack_ref, toks_ref, packs_ref, own_sem, tok_send, tok_recv, pack_send, pack_recv):
+    dp, t, high, core, bits, flips, right, left = places(n_t, n_dp)
+    peers = [{"tensor": right}, {"tensor": left}, {"dp": high * 2 + 1 - core}] + [{"dp": f * 2 + core} for f in flips]
+    meet(peers)
+    own_tok = pltpu.make_async_copy(tok_ref, toks_ref.at[t], own_sem.at[0])
+    own_pack = pltpu.make_async_copy(pack_ref, packs_ref.at[t, high, core], own_sem.at[1])
+    own_tok.start()
+    own_pack.start()
+    rows = tok_ref.shape[0]
+    half = rows // 2
+    token = {}
+    pack = {}
+
+    def send_pack(s):
+        b = lax.rem(t - s + n_t, n_t)
+        src = pack_ref if s == 0 else packs_ref.at[b, high, core]
+        pack[s] = remote(src, packs_ref.at[b, high, core], pack_send.at[s], pack_recv.at[s], {"tensor": right})
+        pack[s].start()
+
+    def send_token(s, j):
+        b = lax.rem(t - s + n_t, n_t)
+        src = (tok_ref if s == 0 else toks_ref.at[b]).at[pl.ds(j * half, half)]
+        token[s, j] = remote(src, toks_ref.at[b, pl.ds(j * half, half)], tok_send.at[s, j], tok_recv.at[s, j], {"tensor": right})
+        token[s, j].start()
+
+    def swap(i):
+        s = n_t - 1 + i
+        if i < bits:
+            base = (high // 2**i) * 2**i
+            part = packs_ref.at[:, pl.ds(base, 2**i), core]
+            peer = {"dp": flips[i] * 2 + core}
+        else:
+            part = packs_ref.at[:, :, core]
+            peer = {"dp": high * 2 + 1 - core}
+        pack[s] = remote(part, part, pack_send.at[s], pack_recv.at[s], peer)
+        pack[s].start()
+
+    send_pack(0)
+    send_token(0, 0)
+    send_token(0, 1)
+    for s in range(1, n_t - 1):
+        pack[s - 1].wait_recv()
+        send_pack(s)
+    pack[n_t - 2].wait_recv()
+    own_pack.wait()
+    swap(0)
+
+    def token_step(s):
+        def run():
+            for j in range(2):
+                token[s - 1, j].wait_recv()
+                if s < n_t - 1:
+                    send_token(s, j)
+        return run
+
+    def pack_step(i):
+        def run():
+            pack[n_t - 1 + i - 1].wait_recv()
+            if i <= bits:
+                swap(i)
+        return run
+
+    for step in interleave([token_step(s) for s in range(1, n_t)], [pack_step(i) for i in range(1, bits + 2)]):
+        step()
+    own_tok.wait()
+    for copy in list(pack.values()) + list(token.values()):
+        copy.wait_send()
+
+def gather_start(tokens, pack, n_t, n_dp):
+    rows, D = tokens.shape
+    pr = pack.shape[0]
+    bits = (n_dp // 2).bit_length() - 1
+    n_pack = n_t + bits
+    hbm = pl.BlockSpec(memory_space=pl.ANY)
+    return pl.pallas_call(
+        functools.partial(gather_kernel, n_t, n_dp),
+        out_shape=[jax.ShapeDtypeStruct((n_t, rows, D), bf), jax.ShapeDtypeStruct((n_t, n_dp // 2, 2, pr, D), bf)],
+        in_specs=[hbm, hbm], out_specs=[hbm, hbm],
+        scratch_shapes=[pltpu.SemaphoreType.DMA((2,)), pltpu.SemaphoreType.DMA((n_t - 1, 2)), pltpu.SemaphoreType.DMA((n_t - 1, 2)),
+                        pltpu.SemaphoreType.DMA((n_pack,)), pltpu.SemaphoreType.DMA((n_pack,))],
+        compiler_params=pltpu.CompilerParams(collective_id=0, has_side_effects=True),
+        name="gather_start",
+    )(tokens, pack)
+
+def reduce_kernel(n_t, n_dp, tok_ref, pack_ref, tok_out, pack_out, tok_got, tok_acc, first, acc, ring_got, ring_acc, *rest):
+    dp, t, high, core, bits, flips, right, left = places(n_t, n_dp)
+    halves, (tok_send, tok_recv, send, recv) = rest[:bits], rest[bits:]
+    peers = [{"tensor": right}, {"tensor": left}, {"dp": high * 2 + 1 - core}] + [{"dp": f * 2 + core} for f in flips]
+    meet(peers)
+    n_hi = n_dp // 2
+    pr = pack_ref.shape[3]
+    rows = tok_ref.shape[1]
+    piece = 64 if rows % 64 == 0 else rows
+    copies = {}
+
+    def block(s):
+        return lax.rem(t - 1 - s + 2 * n_t, n_t)
+
+    def send_token(s):
+        src = tok_ref.at[block(0)] if s == 0 else tok_acc.at[s - 1]
+        copies["t", s] = remote(src, tok_got.at[s], tok_send.at[s], tok_recv.at[s], {"tensor": right})
+        copies["t", s].start()
+
+    def token_step(s):
+        def run():
+            copies["t", s - 1].wait_recv()
+            last = s == n_t - 1
+            b = t if last else block(s)
+
+            @pl.loop(0, rows // piece)
+            def _(i):
+                at = pl.ds(pl.multiple_of(i * piece, piece), piece)
+                total = tok_got[s - 1, at].astype(f32) + tok_ref[b, at].astype(f32)
+                if last:
+                    tok_out[at] = total
+                else:
+                    tok_acc[s - 1, at] = total.astype(bf)
+            if not last:
+                send_token(s)
+        return run
+
+    def start(k, src, dst, peer):
+        copies["p", k] = remote(src, dst, send.at[k], recv.at[k], peer)
+        copies["p", k].start()
+
+    def swap(k):
+        if k == 0:
+            start(0, pack_ref.at[:, :, 1 - core], first, {"dp": high * 2 + 1 - core})
+        else:
+            i = bits - k
+            base = (high // 2**(i + 1)) * 2**(i + 1)
+            other = base + (1 - (high // 2**i) % 2) * 2**i
+            start(k, acc.at[:, pl.ds(other, 2**i)], halves[i], {"dp": flips[i] * 2 + core})
+
+    def add_swap(k):
+        copies["p", k].wait_recv()
+        if k == 0:
+            @pl.loop(0, n_t * n_hi)
+            def _(m):
+                a, b = m // n_hi, m % n_hi
+                acc[a, b] = (pack_ref[a, b, core].astype(f32) + first[a, b].astype(f32)).astype(bf)
+        else:
+            i = bits - k
+            keep = (high // 2**i) * 2**i
+
+            @pl.loop(0, n_t * 2**i)
+            def _(m):
+                a, b = m // 2**i, m % 2**i
+                acc[a, keep + b] = (acc[a, keep + b].astype(f32) + halves[i][a, b].astype(f32)).astype(bf)
+
+    def ring(s):
+        src = acc.at[block(0), high] if s == 0 else ring_acc.at[s - 1]
+        start(bits + 1 + s, src, ring_got.at[s], {"tensor": right})
+
+    def ring_add(s):
+        copies["p", bits + s].wait_recv()
+        last = s == n_t - 1
+        b = t if last else block(s)
+        total = ring_got[s - 1].astype(f32) + acc[b, high].astype(f32)
+        if last:
+            pack_out[...] = total
+        else:
+            ring_acc[s - 1] = total.astype(bf)
+
+    swap(0)
+    send_token(0)
+
+    def pack_step(k):
+        def run():
+            if k <= bits:
+                add_swap(k)
+                if k < bits:
+                    swap(k + 1)
+                else:
+                    ring(0)
+            else:
+                s = k - bits
+                ring_add(s)
+                if s < n_t - 1:
+                    ring(s)
+        return run
+
+    for step in interleave([pack_step(k) for k in range(bits + n_t)], [lambda: None] + [token_step(s) for s in range(1, n_t)]):
+        step()
+    for copy in copies.values():
+        copy.wait_send()
+
+def reduce_end(spread, pack, n_t, n_dp):
+    _, rows, D = spread.shape
+    pr = pack.shape[3]
+    n_hi = n_dp // 2
+    bits = n_hi.bit_length() - 1
+    n_pack = bits + n_t
+    vm = pl.BlockSpec(memory_space=pltpu.VMEM)
+    return pl.pallas_call(
+        functools.partial(reduce_kernel, n_t, n_dp),
+        out_shape=[jax.ShapeDtypeStruct((rows, D), f32), jax.ShapeDtypeStruct((pr, D), f32)],
+        in_specs=[vm, vm], out_specs=[vm, vm],
+        scratch_shapes=[pltpu.VMEM((n_t - 1, rows, D), bf), pltpu.VMEM((max(n_t - 2, 1), rows, D), bf),
+                        pltpu.VMEM((n_t, n_hi, pr, D), bf), pltpu.VMEM((n_t, n_hi, pr, D), bf),
+                        pltpu.VMEM((n_t - 1, pr, D), bf), pltpu.VMEM((max(n_t - 2, 1), pr, D), bf)]
+                       + [pltpu.VMEM((n_t, 2**i, pr, D), bf) for i in range(bits)]
+                       + [pltpu.SemaphoreType.DMA((n_t - 1,)), pltpu.SemaphoreType.DMA((n_t - 1,)),
+                          pltpu.SemaphoreType.DMA((n_pack,)), pltpu.SemaphoreType.DMA((n_pack,))],
+        compiler_params=pltpu.CompilerParams(collective_id=1, has_side_effects=True, vmem_limit_bytes=56 * 1024 * 1024),
+        name="reduce_end",
+    )(spread, pack)
+
 EPS=1e-06
 ALL=("tensor","dp")
 
@@ -192,10 +427,21 @@
     misc = jnp.pad(misc, (0, D - used))[None]
     rel_part = lax.dynamic_slice_in_dim(rel_table, t * part, part, 0)
     small = jnp.concatenate([misc, rel_part], axis=0)
-    gather = lambda x: lax.all_gather(x, ALL, axis=0, tiled=True)
-    small_all = lax.all_gather(small, ALL, axis=0, tiled=False)
-    query_rows, key_rows, value_rows, out_rows = gather(w_query), gather(w_key), gather(w_value), gather(w_out)
-    inner_rows, outer_rows = gather(w_ff_in), gather(w_ff_out)
+    early = jnp.concatenate([w_query, w_key, w_value, small], axis=0)
+    own_rows = w_query.shape[0]
+    late_rows = w_ff_in.shape[0]
+    early_rows = early.shape[0]
+    early = jnp.pad(early, ((0, -early_rows % 16), (0, 0)))
+    late = jnp.concatenate([w_ff_in, w_ff_out, w_out], axis=0)
+    gathered, early_all = gather_start(tokens, early, n_t, n_dp)
+    late_all = lax.all_gather(late, ALL, axis=0, tiled=False)
+    gathered = gathered.reshape(L, D)
+    early_all = early_all.reshape(n_all, early.shape[0], D)
+    cut = lambda x, at, n: x[:, at:at + n].reshape(n_all * n, D)
+    query_rows, key_rows, value_rows = [cut(early_all, i * own_rows, own_rows) for i in range(3)]
+    small_all = early_all[:, 3 * own_rows:early_rows]
+    inner_rows, outer_rows = cut(late_all, 0, late_rows), cut(late_all, late_rows, late_rows)
+    out_rows = cut(late_all, 2 * late_rows, own_rows)
     misc_all = small_all[:, 0]
     o1 = 3 * wide
     o2 = o1 + inner
@@ -207,7 +453,6 @@
     shift = first[:, o3:used].reshape(n_dp, 4, cols).transpose(1, 0, 2).reshape(4, D).astype(f32)
     table = small_all[:, 1:].reshape(n_t, n_dp, part, D).transpose(1, 0, 2, 3).reshape(NB, D)
 
-    gathered = lax.all_gather(tokens, "tensor", axis=0, tiled=True)
     query = project(tokens, query_rows, bias[0])
     key = project(gathered, key_rows, bias[1])
     value = project(gathered, value_rows, bias[2])
@@ -256,9 +501,10 @@
     d_query, d_key, d_value, d_key_rel, d_query_rel = attention_backward(
         query, key, value, d_scaled, context, shares, key_rel, query_rel, pick_x, pick_y)
 
-    scatter = lambda x: lax.psum_scatter(x, ALL, scatter_dimension=0, tiled=True)
-    lowered = lambda x: scatter(x.astype(bf)).astype(f32)
-    g_inner, g_outer, g_out = lowered(grad_inner), lowered(grad_outer), lowered(grad_out)
+    parted = lambda x: x.astype(bf).reshape(n_all, -1, D)
+    late_grad = jnp.concatenate([parted(grad_inner), parted(grad_outer), parted(grad_out)], axis=1)
+    late_sum = lax.psum_scatter(late_grad, ALL, scatter_dimension=0, tiled=True)[0].astype(f32)
+    g_inner, g_outer, g_out = late_sum[:late_rows], late_sum[late_rows:2 * late_rows], late_sum[2 * late_rows:]
     dqr, dkr = d_query_rel.astype(bf), d_key_rel.astype(bf)
     grad_query = jnp.einsum("tf,td->fd", d_query, tokens, preferred_element_type=f32) + jnp.einsum(
         "tf,td->fd", dqr, table, preferred_element_type=f32)
@@ -273,10 +519,6 @@
     own = jnp.dot(d_query, query_rows, preferred_element_type=f32)
     spread = (jnp.dot(d_key, key_rows, preferred_element_type=f32)
               + jnp.dot(d_value, value_rows, preferred_element_type=f32)).astype(bf)
-    back_sum = lax.psum_scatter(spread, "tensor", scatter_dimension=0, tiled=True)
-    tokens_grad = d_resid_one + own + back_sum.astype(f32)
-    g_query, g_key, g_value = lowered(grad_query), lowered(grad_key), lowered(grad_value)
-
     gain_grads = jnp.stack([d_gain_one, d_gain_two])
     shift_grads = jnp.stack([d_shift_zero, d_shift_one, d_shift_two, d_shift_three])
     shape_dp = lambda x, k: jnp.broadcast_to(
@@ -288,11 +530,16 @@
     line = jnp.pad(line, ((0, 0), (0, D - used)))[:, None]
     rel_rows = rel_table.shape[0]
     d_rel_all = jnp.broadcast_to(d_rel.reshape(1, n_dp, rel_rows, D), (n_t, n_dp, rel_rows, D)).reshape(n_all, rel_rows, D)
-    packed = jnp.concatenate([line, d_rel_all], axis=1)
-    small_grad = lax.psum_scatter(packed, ALL, scatter_dimension=0, tiled=True)[0]
-    row = small_grad[0]
+    early_grad = jnp.concatenate([parted(grad_query), parted(grad_key), parted(grad_value), line.astype(bf), d_rel_all.astype(bf)], axis=1)
+    end_rows = early_grad.shape[1]
+    early_grad = jnp.pad(early_grad, ((0, 0), (0, -end_rows % 16), (0, 0)))
+    back_sum, early_sum = reduce_end(spread.reshape(n_t, R, D), early_grad.reshape(n_t, n_dp // 2, 2, -1, D), n_t, n_dp)
+    tokens_grad = d_resid_one + own + back_sum
+    g_query, g_key, g_value = [early_sum[i * own_rows:(i + 1) * own_rows] for i in range(3)]
+    row = early_sum[3 * own_rows]
+    g_rel = early_sum[3 * own_rows + 1:end_rows]
     return (layer_result_rows, tokens_grad, g_query, g_key, g_value, g_out,
-            row[:o1].reshape(3, wide), g_inner, g_outer, row[o1:o2], small_grad[1:],
+            row[:o1].reshape(3, wide), g_inner, g_outer, row[o1:o2], g_rel,
             row[o2:o3].reshape(2, cols), row[o3:used].reshape(4, cols))
 
 def solution(mesh):

time: 1390 us -> 645 us (0.46)
  the two profiles are of different devices: /device:TPU:13 before, /device:TPU:0 now
where the time goes in v2:
time: 645 us; the launch traced here: 633 us
  Pallas kernels  418 us (65%)
  matrix products  98.5 us (15%)
  local copies, waits for them, and re-layouts  76.1 us (12%)
  other arithmetic  25 us (4%)
  between operations  15.9 us (2%)
    pallas_call x1, Pallas kernels, attention_backward(): pl.pallas_call(functools.partial(bwd_kernel, R, L, B, C), grid=(pairs, 2)...  119 us
    pallas_call x1, Pallas kernels, gather_start(): pl.pallas_call(functools.partial(gather_kernel, n_t, n_dp), out_shape=[ja...  108 us
    pallas_call x1, Pallas kernels, attention_forward(): pl.pallas_call(functools.partial(fwd_kernel, R, L, B, C), grid=(pairs, 2)...  97.2 us
    pallas_call x1, Pallas kernels, reduce_end(): pl.pallas_call(functools.partial(reduce_kernel, n_t, n_dp), out_shape=[ja...  93.4 us
    concatenate x1, local copies, waits for them, and re-layouts, local(): jnp.concatenate([parted(grad_query), parted(grad_key), parted(grad_value)...  31.9 us
    dot_general x1, matrix products, local(): jnp.einsum('td,fd->tf', hidden_low, inner_rows, preferred_element_type=f32)  19.7 us
    dot_general x1, matrix products, local(): jnp.einsum('td,fd->tf', d_feed, outer_rows, preferred_element_type=f32)  17.6 us
  transfers between devices with their start and end apart: 2, of which 0 were waited for; matrix products, arithmetic and copies ran while one was open for 19% of the time, Pallas kernels for 66%

profile of v2, /device:TPU:0, one launch (start us, length us, event | category | flops | bytes accessed | tf_op | source)
XLA Modules:
  0.0 633.2 jit_solution(3074087626811844650)
XLA Ops:
  7.3 1.8 pad_maximum_fusion.1
  9.1 0.8 reshape.316
  9.8 0.7 reshape.315
  10.6 0.8 reshape.314
  11.3 0.7 fusion.43
  12.1 2.4 concatenate.30
  15.2 108.5 %gather_start.1 = (bf16[4,512,768]{2,1,0:T(8,128)(2,1)}, bf16[4,4,2,96,768]{4,3,2,1,0:T(8,128)(2,1)}) custom-call(bf16[512,768]{1,0:T(8,128)(2,1)} %tok_ref.1, bf16[96,768]{1,0:T(8,128)(2,1)} %pad.18.pack_ref), custom_call_target="tpu_custom_call" | custom-call | tf_op jit(solution)/shard_map/gather_start/pallas_call | solution.py:265
  123.7 0.9 slice.185
  124.6 1.1 slice.176
  125.7 1.4 slice.183
  129.6 2.2 fusion.54
  132.9 0.7 copy-done.20
  133.7 0.8 fusion.14.q_ref
  134.5 3.4 convolution_convert_fusion.1.kt_ref
  137.9 3.4 convolution_convert_fusion.qr_ref
  141.3 4.0 add_convert_fusion.3.k_ref
  145.3 4.0 add_convert_fusion.2.v_ref
  149.3 97.2 %attend.1 = (bf16[512,768]{1,0:T(8,128)(2,1)S(1)}, f32[512,768]{1,0:T(8,128)S(1)}, bf16[12,512,2048]{2,1,0:T(8,128)(2,1)}) custom-call(f32[1,2048]{1,0:T(1,128)S(1)} %compare_select_fusion.mask_ref, bf16[512,768]{1,0:T(8,128)(2,1)S(1)} %fusion.14.q_ref, bf16[2048,768]{1,0:T(8,128)(2,1)} %add_convert_fusion.3.k_ref, ...), custom_call_target="tpu_custom_call" | custom-call | flops 12884901888 | bytes 40894464 | tf_op jit(solution)/shard_map/attend/pallas_call | solution.py:84
  246.4 6.8 %fusion.53 = (bf16[32,96,768]{2,1,0:T(8,128)(2,1)}, bf16[32,96,768]{2,1,0:T(8,128)(2,1)S(1)}) fusion(bf16[32,216,768]{2,1,0:T(8,128)(2,1)} %bitcast.101), kind=kLoop, calls=%fused_computation.144 | loop fusion | bytes 18874368 | tf_op jit(solution)/shard_map/slice | solution.py:440
  253.3 1.4 slice.184
  254.7 0.9 fusion.57
  255.9 19.7 %multiply_convert_fusion = (bf16[512,3072]{1,0:T(8,128)(2,1)S(1)}, f32[512,3072]{1,0:T(8,128)}, f32[512,3072]{1,0:T(8,128)}) fusion(f32[3072]{0:T(1024)S(1)} %reshape.342, bf16[3072,768]{1,0:T(8,128)(2,1)S(1)} %bitcast.114, f32[512,768]{1,0:T(8,128)S(1)} %get-tuple-element.72, f32[768]{0:T(1024)S(1)} %add.212, f32[768]{0:T(1024)S(1)} %mul.156, ...), kind=kOutput, calls=%fused_computation.6 | convolution fusion | flops 2521694208 | bytes 22042624 | tf_op jit(solution)/shard_map/td,fd->tf/dot_general | solution.py:479
  275.7 2.8 fusion.58
  278.8 0.7 fusion.11
  279.5 1.6 fusion.51
  281.2 4.5 convolution_convert_fusion.2
  285.7 17.6 %fusion.59 = (bf16[3072]{0:T(1024)(128)(2,1)S(1)}, bf16[512,3072]{1,0:T(8,128)(2,1)}) fusion(f32[512,3072]{1,0:T(8,128)} %get-tuple-element.54, bf16[3072,768]{1,0:T(8,128)(2,1)S(1)} %bitcast.119, f32[512,768]{1,0:T(8,128)S(1)} %get-tuple-element.52, f32[512]{0:T(512)S(1)} %negate_multiply_fusion.2, f32[512,3072]{1,0:T(8,128)} %get-tuple-element.73, ...), kind=kOutput, calls=%fused_computation.150 | convolution fusion | flops 2441868288 | bytes 22040576 | tf_op jit(solution)/shard_map/td,fd->tf/dot_general | solution.py:489
  303.3 5.1 multiply_reduce_fusion
  308.5 3.3 convolution_convert_fusion.3
  312.5 0.9 convolution_convert_fusion.4
  313.6 0.9 slice-done.2
  314.7 4.9 pad_maximum_fusion
  319.6 2.0 fusion.6.ox_ref
  321.7 2.0 fusion.7.oy_ref
  323.8 1.6 add_reduce_fusion.1
  325.5 1.6 add_reduce_fusion
  327.7 2.7 multiply_convert_fusion.1.do_ref
  330.5 1.2 copy-done.3
  331.7 1.2 copy-done.5
  332.8 118.6 %attend_back.1 = (bf16[512,768]{1,0:T(8,128)(2,1)S(1)}, bf16[2048,768]{1,0:T(8,128)(2,1)}, bf16[2048,768]{1,0:T(8,128)(2,1)}, f32[256,768]{1,0:T(8,128)S(1)}, f32[256,768]{1,0:T(8,128)S(1)}) custom-call(bf16[512,768]{1,0:T(8,128)(2,1)S(1)} %copy-done.5, bf16[2048,768]{1,0:T(8,128)(2,1)} %add_convert_fusion.3.k_ref, ...), custom_call_target="tpu_custom_call" | custom-call | flops 25769803776 | bytes 56623104 | tf_op jit(solution)/shard_map/attend_back/pallas_call | solution.py:152
  451.4 2.4 reduce
  454.0 2.4 convert_reduce_fusion
  457.3 1.8 fusion.21
  459.0 1.8 fusion.18
  460.8 0.8 fusion.61
  461.8 1.6 add_convert_fusion.5
  463.4 1.1 copy-done.17
  464.4 2.7 fusion.62
  467.2 1.6 add_convert_fusion.4
  468.8 0.8 copy-done.15
  469.5 3.8 convolution_convert_fusion.5
  473.5 31.9 %concatenate.35 = bf16[32,105,768]{2,1,0:T(8,128)(2,1)} concatenate(bf16[32,24,768]{2,1,0:T(8,128)(2,1)} %bitcast.124, bf16[32,24,768]{2,1,0:T(8,128)(2,1)} %bitcast.125, bf16[32,24,768]{2,1,0:T(8,128)(2,1)} %bitcast.139, bf16[32,1,768]{2,1,0:T(2,128)(2,1)S(1)} %copy.48, bf16[32,32,768]{2,1,0:T(8,128)(2,1)S(1)} %bitcast.107), dimensions={1} | concatenate | bytes 10321920 | tf_op jit(solution)/shard_map/concatenate | solution.py:533
  505.4 5.5 pad.20
  510.9 2.6 fusion.60
  513.5 4.0 add_convert_fusion
  517.6 93.4 %reduce_end.1 = (f32[512,768]{1,0:T(8,128)}, f32[112,768]{1,0:T(8,128)}) custom-call(bf16[4,512,768]{2,1,0:T(8,128)(2,1)} %bitcast.134, bf16[4,4,2,112,768]{4,3,2,1,0:T(8,128)(2,1)} %bitcast.100), custom_call_target="tpu_custom_call" | custom-call | tf_op jit(solution)/shard_map/reduce_end/pallas_call | solution.py:385
  611.0 1.6 slice.172
  613.9 0.8 slice_reduce_fusion.7
  615.4 0.8 slice_reduce_fusion.6
  616.8 1.3 slice_bitcast_fusion.3
  618.1 1.6 fusion.55
  619.8 3.7 add_add_fusion.2
  623.5 1.0 convert_element_type.209
  625.1 0.8 slice_bitcast_fusion
  (145 shorter events, 10.9 us)
Async XLA Ops:
  7.2 4.9 copy-start
  7.2 121.9 %copy-start.25 = (s32[4095]{0:T(1024)S(1)}, s32[4095]{0:T(1024)}, u32[]{:S(2)}) copy-start(s32[4095]{0:T(1024)} %param.27) | copy-start | bytes 49144
  7.2 239.2 %all-gather.3.cloned.1.call-start = ((), (), s32[]{:S(2)}) async-start(), calls=%async_computation.2 | async-start | bytes 10948608 | tf_op jit(solution)/shard_map/all_gather | solution.py:437
  9.0 614.4 %reduce-scatter.2.cloned.1.call-start = ((), (), s32[]{:S(2)}) async-start(), calls=%async_computation.1 | async-start | bytes 10948608 | tf_op jit(solution)/shard_map/reduce_scatter | solution.py:506
  129.0 3.4 copy-start.13
  131.9 2.6 copy-start.8
  131.9 9.4 %copy-start.10 = (bf16[32,24,768]{2,1,0:T(8,128)(2,1)}, bf16[32,24,768]{2,1,0:T(8,128)(2,1)S(1)}, u32[]{:S(2)}) copy-start(bf16[32,24,768]{2,1,0:T(8,128)(2,1)S(1)} %get-tuple-element.58) | copy-start | bytes 3538948
  131.9 13.4 %copy-start.23 = (bf16[32,24,768]{2,1,0:T(8,128)(2,1)}, bf16[32,24,768]{2,1,0:T(8,128)(2,1)S(1)}, u32[]{:S(2)}) copy-start(bf16[32,24,768]{2,1,0:T(8,128)(2,1)S(1)} %get-tuple-element.57) | copy-start | bytes 3538948
  131.9 1.8 copy-start.20
  134.5 14.8 %copy-start.4 = (bf16[512,768]{1,0:T(8,128)(2,1)}, bf16[512,768]{1,0:T(8,128)(2,1)S(1)}, u32[]{:S(2)}) copy-start(bf16[512,768]{1,0:T(8,128)(2,1)S(1)} %fusion.14.q_ref) | copy-start | bytes 2359300
  137.9 3.4 copy-start.26
  246.4 66.1 %copy-start.2 = (bf16[512,768]{1,0:T(8,128)(2,1)}, bf16[512,768]{1,0:T(8,128)(2,1)S(1)}, u32[]{:S(2)}) copy-start(bf16[512,768]{1,0:T(8,128)(2,1)S(1)} %get-tuple-element.27.ctx_ref) | copy-start | bytes 2359300
  246.4 8.2 %copy-start.21 = (bf16[512,768]{1,0:T(8,128)(2,1)S(1)}, bf16[512,768]{1,0:T(8,128)(2,1)}, u32[]{:S(2)}) copy-start(bf16[512,768]{1,0:T(8,128)(2,1)} %tok_ref.1) | copy-start | bytes 2359300
  254.6 1.2 copy-start.12
  254.7 21.0 %slice-start = ((s8[4718592]{0:T(1024)(128)(4,1)}), s8[4194304]{0:T(1024)(128)(4,1)S(1)}, s32[]{:S(2)}) async-start(s8[4718592]{0:T(1024)(128)(4,1)} %bitcast.116), calls=%async_computation.3 | async-start | bytes 8388608
  255.9 19.8 %slice-start.1 = ((s8[4718592]{0:T(1024)(128)(4,1)}), s8[524288]{0:T(1024)(128)(4,1)S(1)}, s32[]{:S(2)}) async-start(s8[4718592]{0:T(1024)(128)(4,1)} %bitcast.116), calls=%async_computation.4 | async-start | bytes 1048576
  275.7 3.2 copy-start.19
  281.2 22.2 %copy-start.9 = (f32[512,768]{1,0:T(8,128)}, f32[512,768]{1,0:T(8,128)S(1)}, u32[]{:S(2)}) copy-start(f32[512,768]{1,0:T(8,128)S(1)} %get-tuple-element.52) | copy-start | bytes 4718596
  303.3 5.2 copy-start.28
  311.8 2.8 slice-start.2
  311.8 2.9 slice-start.3
  312.5 1.1 copy-start.6
  330.5 1.2 copy-start.3
  331.7 1.2 copy-start.5
  456.9 3.9 copy-start.22
  460.8 1.0 copy-start.14
  460.8 2.6 copy-start.27
  461.8 2.6 copy-start.17
  467.2 2.3 copy-start.15
  505.4 5.5 copy-start.11
  505.4 5.5 copy-start.18
  510.9 2.6 copy-start.16
  510.9 2.6 copy-start.24
  517.6 102.2 %copy-start.7 = (f32[512,768]{1,0:T(8,128)S(1)}, f32[512,768]{1,0:T(8,128)}, u32[]{:S(2)}) copy-start(f32[512,768]{1,0:T(8,128)} %copy-done.6) | copy-start | bytes 4718596
  619.7 6.2 copy-start.1
Sparse Core Ops, SparseCore 0:
  11.5 128.2 all-gather.2
  319.8 142.3 reduce-scatter.1

commit v3 on v2

--- a/solution.py
+++ b/solution.py
@@ -30,42 +30,68 @@
     idx=7-lax.broadcasted_iota(jnp.int32,(8,w),0)
     return jnp.concatenate([jnp.take_along_axis(x[n-8-8*g:n-8*g],idx,axis=0) for g in range(n//8)],axis=0)
 
-def fwd_kernel(R,L,B,C,mask_ref,q_ref,k_ref,v_ref,kt_ref,qr_ref,ctx_ref,scale_ref,e_ref,yt_ref,acc_ref):
+def fwd_kernel(R,L,B,C,mask_ref,q_ref,k_ref,v_ref,kt_ref,qr_ref,ctx_ref,scale_ref,e_ref,yt_ref,acc_ref,km_ref,y_ref,s_ref,x_ref,p_ref):
     hh=pl.program_id(1)
-    W=L+R
-    def lanes(n): return (lax.broadcasted_iota(jnp.int32,(n,128),1)//DH)==hh
-    zero=jnp.zeros((),bf)
-    def yblock(i,_):
-        j0=pl.multiple_of(i*C,C)
-        kb=jnp.where(lanes(C),k_ref[pl.ds(j0,C),:],zero)
-        us=pl.multiple_of(L-C-j0,C)
-        y=dot_nt(kb,qr_ref[pl.ds(us,R+C),:])
-        y=pltpu.roll(y,R+1,1,stride=1,stride_axis=0)[:,:R]
-        yt_ref[:,pl.ds(j0,C)]=y.T+mask_ref[:,pl.ds(j0,C)]
-        return 0
-    lax.fori_loop(0,L//C,yblock,0,unroll=2)
-    v_one=jnp.where(lanes(L),v_ref[...],jnp.ones((),bf))
-    def strip(i,_):
-        r0=pl.multiple_of(i*B,B)
-        q=jnp.where(lanes(B),q_ref[pl.ds(r0,B),:],zero)
-        ws=pl.multiple_of(R-B-r0,B)
-        x=dot_nt(q,kt_ref[pl.ds(ws,L+B),:])
-        x=pltpu.roll(x,L+1,1,stride=1,stride_axis=0)[:,:L]
-        raw=dot_nt(q,k_ref[...])+x+yt_ref[pl.ds(r0,B),:]
-        peak=jnp.max(raw,axis=1,keepdims=True)
-        e=jnp.exp2((raw-peak)*(SCALE*LOG2E))
-        e=flip_rows(e).astype(bf)
-        rr=pl.multiple_of(R-B-r0,B)
-        e_ref[0,pl.ds(rr,B),:]=e
-        acc_ref[pl.ds(rr,B),:]=dot_nn(e,v_one)
-        return 0
-    lax.fori_loop(0,R//B,strip,0,unroll=2)
-    acc=acc_ref[...]
+    lane=lambda n: lax.broadcasted_iota(jnp.int32,(n,128),1)
+    def lanes(n): return (lane(n)//DH)==hh
+    zero,one=jnp.zeros((),bf),jnp.ones((),bf)
+    spare=(1-hh)*DH
+    for i in range(L//C):
+        at=slice(i*C,i*C+C)
+        km_ref[at,:]=jnp.where(lane(C)==spare,mask_ref[at,:],k_ref[at,:])
+    def yblock(i):
+        at=slice(i*C,i*C+C)
+        us=L-C-i*C
+        kb=jnp.where(lanes(C),k_ref[at,:],zero)
+        y=y_ref.at[i%2]
+        y[...]=dot_nt(kb,qr_ref[us:us+R+C,:])
+        for g in range(C//16):
+            rows=slice(16*g,16*g+16)
+            part=y[rows,:].astype(bf)
+            s_part=pltpu.roll(part,R+1+16*g,1,stride=1,stride_axis=0)[:,:R]
+            yt_ref[i%2,rows,:]=s_part
+        return yt_ref[i%2].T
+    for i in range(L//C):
+        acc_ref[:,i*C:i*C+C]=yblock(i)
+    v_one=jnp.where(lanes(L),v_ref[...],one)
+    own=lanes(B)
+    sp=lane(B)==spare
+    accs=[]
+    for i in range(R//B):
+        r0=i*B
+        qm=q_ref[r0:r0+B,:]
+        q=jnp.where(own,qm,zero)
+        qs=jnp.where(sp,one,q)
+        ws=R-B-r0
+        x,s=x_ref.at[i%2],s_ref.at[i%2]
+        x[...]=dot_nt(q,kt_ref[ws:ws+L+B,:])
+        s[...]=dot_nt(qs,km_ref[...])
+        rr=R-B-r0
+        p=p_ref.at[i%2]
+        for g in range(B//16):
+            rows=slice(16*g,16*g+16)
+            xr=pltpu.roll(x[rows,:],(L+1+16*g)%(L+B),1,stride=1,stride_axis=0)[:,:L]
+            raw=s[rows,:]+xr+acc_ref[r0+16*g:r0+16*g+16,:].astype(f32)
+            s[rows,:]=raw
+            top=raw[:,:128]
+            for j in range(1,L//128):
+                top=jnp.maximum(top,raw[:,128*j:128*j+128])
+            p[rows,:]=top
+        p[...]=jnp.broadcast_to(jnp.max(p[...],axis=1,keepdims=True)*(SCALE*LOG2E),(B,128))
+        for g in range(B//16):
+            rows=slice(16*g,16*g+16)
+            peak=jnp.concatenate([p[rows,:]]*(L//128),axis=1)
+            e=jnp.exp2(s[rows,:]*(SCALE*LOG2E)-peak)
+            e=flip_rows(e).astype(bf)
+            to=rr+B-16-16*g
+            e_ref[0,to:to+16,:]=e
+        accs.append(dot_nn(e_ref[0,rr:rr+B,:],v_one))
+    acc=jnp.concatenate(accs[::-1],axis=0)
     inv=1.0/pltpu.roll(acc,DH,1)
-    ctx=dot_nn(flip_matrix(R),(acc*inv).astype(bf)).astype(bf)
+    J=flip_matrix(R)
+    ctx=dot_nn(J,(acc*inv).astype(bf)).astype(bf)
     mine=lanes(R)
     inv_hi=inv.astype(bf)
-    J=flip_matrix(R)
     sc=dot_nn(J,inv_hi)+dot_nn(J,(inv-inv_hi.astype(f32)).astype(bf))
     sc=sc*SCALE
     @pl.when(hh==0)
@@ -79,21 +105,24 @@
 
 def attention_forward(q,k,v,kt,qr,mask,B=128,C=256):
     R,F=q.shape; L=k.shape[0]; W=L+R; pairs=F//128
+    B=min(B,R)
     col=lambda n: pl.BlockSpec((n,128),lambda p,h:(0,p))
     flops=2*pairs*2*R*L*128*4
     return pl.pallas_call(functools.partial(fwd_kernel,R,L,B,C),
         grid=(pairs,2),
-        in_specs=[pl.BlockSpec((1,L),lambda p,h:(0,0)),col(R),col(L),col(L),col(W),col(W)],
+        in_specs=[pl.BlockSpec((L,128),lambda p,h:(0,0)),col(R),col(L),col(L),col(W),col(W)],
         out_specs=[col(R),col(R),pl.BlockSpec((1,R,L),lambda p,h:(2*p+h,0,0))],
         out_shape=[jax.ShapeDtypeStruct((R,F),bf),jax.ShapeDtypeStruct((R,F),f32),jax.ShapeDtypeStruct((2*pairs,R,L),bf)],
-        scratch_shapes=[pltpu.VMEM((R,L),f32),pltpu.VMEM((R,128),f32)],
+        scratch_shapes=[pltpu.VMEM((2,C,R),bf),pltpu.VMEM((R,L),bf),pltpu.VMEM((L,128),bf),pltpu.VMEM((2,C,R+C),f32),
+                        pltpu.VMEM((2,B,L),f32),pltpu.VMEM((2,B,L+B),f32),pltpu.VMEM((2,B,128),f32)],
         compiler_params=pltpu.CompilerParams(vmem_limit_bytes=48*1024*1024,dimension_semantics=("arbitrary","arbitrary")),
         cost_estimate=pl.CostEstimate(flops=flops,bytes_accessed=2*pairs*R*L*2+10*L*F,transcendentals=2*pairs*R*L),
         name="attend",
     )(mask,q,k,v,kt,qr)
 
 def bwd_kernel(R,L,B,C,q_ref,k_ref,v_ref,do_ref,ctx_ref,e_ref,kr_ref,qrel_ref,ox_ref,oy_ref,
-               dq_ref,dk_ref,dv_ref,dkr_ref,dqr_ref,ds_ref,dor_ref,qrev_ref,dqa_ref,dka_ref,dva_ref):
+               dq_ref,dk_ref,dv_ref,dkr_ref,dqr_ref,ds_ref,dor_ref,qrev_ref,dqa_ref,dka_ref,dva_ref,
+               delta_ref,dp_ref,wide_ref,dst_ref,wide2_ref):
     hh=pl.program_id(1)
     def lanes(n): return (lax.broadcasted_iota(jnp.int32,(n,128),1)//DH)==hh
     zero=jnp.zeros((),bf)
@@ -109,42 +138,46 @@
     ctx=dot_nn(J,ctx_ref[...])
     dor_ref[...]=do
     qrev_ref[...]=jnp.where(lanes(R),dot_nn(J,q_ref[...]).astype(bf),zero)
-    delta_all=jnp.sum(do.astype(f32)*ctx,axis=1,keepdims=True)
+    delta_ref[...]=jnp.broadcast_to(jnp.sum(do.astype(f32)*ctx,axis=1,keepdims=True),(R,128))
     own=lanes(B)
     for i in range(R//B):
         r0=i*B
-        do_s=dor_ref[r0:r0+B,:]
-        dp=dot_nt(do_s,v_ref[...])
-        ds=(e_ref[0,r0:r0+B,:].astype(f32)*(dp-delta_all[r0:r0+B])).astype(bf)
-        ds_ref[r0:r0+B,:]=ds
-        wide=jnp.concatenate([ds,jnp.zeros((B,B),bf)],axis=1)
-        wide=pltpu.roll(wide,0,1,stride=1,stride_axis=0)
-        db=dot_nn(wide,ox_ref[r0:r0+L+B,:]).astype(bf)
-        dq=dot_nn(ds,k_ref[...])+dot_nn(db,kr_ref[...])
+        dp,wide=dp_ref.at[i%2],wide_ref.at[i%2]
+        dp[...]=dot_nt(dor_ref[r0:r0+B,:],v_ref[...])
+        for g in range(B//16):
+            rows=slice(16*g,16*g+16)
+            at=slice(r0+16*g,r0+16*g+16)
+            delta=jnp.concatenate([delta_ref[at,:]]*(L//128),axis=1)
+            ds=(e_ref[0,at,:].astype(f32)*(dp[rows,:]-delta)).astype(bf)
+            ds_ref[at,:]=ds
+            part=jnp.concatenate([ds,jnp.zeros((16,B),bf)],axis=1)
+            wide[rows,:]=pltpu.roll(part,16*g,1,stride=1,stride_axis=0)
+        db=dot_nn(wide[...],ox_ref[r0:r0+L+B,:]).astype(bf)
+        dq=dot_nn(ds_ref[r0:r0+B,:],k_ref[...])+dot_nn(db,kr_ref[...])
         dqa_ref[r0:r0+B,:]=jnp.where(own,dq,dqa_ref[r0:r0+B,:])
         dkr_ref[...]+=dot_tn(db,qrev_ref[r0:r0+B,:])
     ownk=lanes(C)
     qrel=jnp.where(lanes(NB),qrel_ref[...],zero)
-    def jblock(i,_):
-        j0=pl.multiple_of(i*C,C)
-        dst=ds_ref[:,pl.ds(j0,C)].T
-        et=e_ref[0,:,pl.ds(j0,C)].T
-        wide=jnp.concatenate([dst,jnp.zeros((C,C),bf)],axis=1)
-        wide=pltpu.roll(wide,0,1,stride=1,stride_axis=0)
-        db=dot_nn(wide,oy_ref[pl.ds(j0,R+C),:]).astype(bf)
-        dka_ref[pl.ds(j0,C),:]+=dot_nn(dst,qrev_ref[...])+dot_nn(db,qrel)
-        dva_ref[pl.ds(j0,C),:]+=dot_nn(et,dor_ref[...])
-        kb=jnp.where(ownk,k_ref[pl.ds(j0,C),:],zero)
+    for i in range(L//C):
+        at=slice(i*C,i*C+C)
+        dst,wide=dst_ref.at[i%2],wide2_ref.at[i%2]
+        dst[...]=ds_ref[:,at].T
+        for g in range(C//16):
+            rows=slice(16*g,16*g+16)
+            part=jnp.concatenate([dst[rows,:],jnp.zeros((16,C),bf)],axis=1)
+            wide[rows,:]=pltpu.roll(part,16*g,1,stride=1,stride_axis=0)
+        db=dot_nn(wide[...],oy_ref[i*C:i*C+R+C,:]).astype(bf)
+        dka_ref[at,:]+=dot_nn(dst[...],qrev_ref[...])+dot_nn(db,qrel)
+        dva_ref[at,:]+=dot_tn(e_ref[0,:,at],dor_ref[...])
+        kb=jnp.where(ownk,k_ref[at,:],zero)
         dqr_ref[...]+=dot_tn(db,kb)
-        return 0
-    lax.fori_loop(0,L//C,jblock,0,unroll=2)
     @pl.when(hh==1)
     def _():
         dq_ref[...]=dot_nn(J,dqa_ref[...].astype(bf)).astype(bf)
         dk_ref[...]=dka_ref[...].astype(bf)
         dv_ref[...]=(dva_ref[...]*(1.0/SCALE)).astype(bf)
 
-def attention_backward(q,k,v,do,ctx,e,key_rel,query_rel,onehot_x,onehot_y,B=128,C=256):
+def attention_backward(q,k,v,do,ctx,e,key_rel,query_rel,onehot_x,onehot_y,B=128,C=128):
     R,F=q.shape; L=k.shape[0]; W=L+R; pairs=F//128
     col=lambda n: pl.BlockSpec((n,128),lambda p,h:(0,p))
     full=pl.BlockSpec((W,NB),lambda p,h:(0,0))
@@ -156,11 +189,157 @@
         out_shape=[jax.ShapeDtypeStruct((R,F),bf),jax.ShapeDtypeStruct((L,F),bf),jax.ShapeDtypeStruct((L,F),bf),
                    jax.ShapeDtypeStruct((NB,F),f32),jax.ShapeDtypeStruct((NB,F),f32)],
         scratch_shapes=[pltpu.VMEM((R,L),bf),pltpu.VMEM((R,128),bf),pltpu.VMEM((R,128),bf),
-                        pltpu.VMEM((R,128),f32),pltpu.VMEM((L,128),f32),pltpu.VMEM((L,128),f32)],
+                        pltpu.VMEM((R,128),f32),pltpu.VMEM((L,128),f32),pltpu.VMEM((L,128),f32),
+                        pltpu.VMEM((R,128),f32),pltpu.VMEM((2,B,L),f32),pltpu.VMEM((2,B,L+B),bf),pltpu.VMEM((2,C,R),bf),pltpu.VMEM((2,C,R+C),bf)],
         compiler_params=pltpu.CompilerParams(vmem_limit_bytes=48*1024*1024,dimension_semantics=("arbitrary","arbitrary")),
         cost_estimate=pl.CostEstimate(flops=flops,bytes_accessed=2*pairs*R*L*2+20*L*F,transcendentals=0),
         name="attend_back",
     )(q,k,v,do,ctx,e,key_rel,query_rel,onehot_x,onehot_y)
+
+EPS=1e-6
+
+def gelu_parts(v):
+    a=jnp.abs(v)
+    t=1.0/(1.0+(0.3275911/math.sqrt(2.0))*a)
+    bell=jnp.exp(-0.5*v*v)
+    poly=t*(0.127414796+t*(-0.142248368+t*(0.7107068705+t*(-0.7265760135+t*0.5307027145))))
+    tail=poly*bell
+    phi=jnp.where(v>0,1.0-tail,tail)
+    return v*phi, phi+v*bell*(1.0/math.sqrt(2.0*math.pi))
+
+def feed_kernel(R,D,tiles,per,rows_in,own_rows,ctx_ref,tok_ref,og_ref,scale_ref,wo_ref,late_ref,bias_ref,gain_ref,shift_ref,
+                res_ref,dres_ref,do_ref,sums_ref,bsum_ref,grad_ref,
+                u1_ref,r1_ref,low_ref,acc_ref,pre_ref,gated_ref,gp_ref,dfeed_ref,stage_ref,tail_ref,datt_ref,sem):
+    step=pl.program_id(0)
+    width=per*rows_in
+    CH=64
+    def chunks(f):
+        def body(i,c):
+            f(pl.ds(pl.multiple_of(i*CH,CH),CH))
+            return c
+        lax.fori_loop(0,R//CH,body,0)
+    mean=lambda x: jnp.mean(x,axis=1,keepdims=True)
+    gain=lambda i: gain_ref[i:i+1,:]
+    shift=lambda i: shift_ref[i:i+1,:]
+    def add_sum(i,x):
+        sums_ref[i:i+1,:]+=jnp.sum(x,axis=0,keepdims=True)
+    @pl.when(step==0)
+    def _():
+        sums_ref[...]=jnp.zeros_like(sums_ref)
+        acc_ref[...]=dot_nn(ctx_ref[...],wo_ref[...])
+        def norm(at):
+            v=tok_ref[at,:].astype(f32)+acc_ref[at,:]+shift(0)
+            c=v-mean(v)
+            r=lax.rsqrt(mean(c*c)+EPS)
+            u=c*r
+            u1_ref[at,:]=u
+            r1_ref[at,:]=jnp.broadcast_to(r,(CH,128))
+            h=u*gain(0)+shift(1)
+            low_ref[at,:]=h.astype(bf)
+            acc_ref[at,:]=h+shift(2)
+        chunks(norm)
+    w_in=late_ref[:,0:rows_in,:].reshape(width,D)
+    w_outer=late_ref[:,rows_in:2*rows_in,:].reshape(width,D)
+    @pl.when(step<tiles)
+    def _():
+        pre_ref[...]=dot_nt(low_ref[...],w_in)
+        def act(at):
+            g,gp=gelu_parts(pre_ref[at,:]+bias_ref[0])
+            gated_ref[step,at,:]=g.astype(bf)
+            gp_ref[step,at,:]=gp.astype(bf)
+        chunks(act)
+        acc_ref[...]+=dot_nn(gated_ref[step],w_outer)
+    @pl.when(step==tiles-1)
+    def _():
+        def norm(at):
+            v=acc_ref[at,:]
+            c=v-mean(v)
+            r=lax.rsqrt(mean(c*c)+EPS)
+            u=c*r
+            res_ref[at,:]=(u*gain(1)+shift(3)).astype(bf)
+            top=og_ref[at,:].astype(f32)
+            add_sum(1,top*u)
+            add_sum(5,top)
+            e=top*gain(1)
+            d=(e-mean(e)-u*mean(e*u))*r
+            add_sum(4,d)
+            dfeed_ref[at,:]=d.astype(bf)
+            acc_ref[at,:]=d
+        chunks(norm)
+    @pl.when(step>=tiles)
+    def _():
+        k=step-tiles
+        slot=lax.rem(k,2)
+        pre_ref[...]=dot_nt(dfeed_ref[...],w_outer)
+        def act(at):
+            d=(pre_ref[at,:]*gp_ref[k,at,:].astype(f32)).astype(bf)
+            gp_ref[k,at,:]=d
+        chunks(act)
+        bsum_ref[0]=jnp.sum(gp_ref[k].astype(f32),axis=0,keepdims=True)
+        def out(kk,s):
+            return pltpu.make_async_copy(stage_ref.at[s],grad_ref.at[pl.ds(kk*per,per),pl.ds(0,2*rows_in)],sem.at[s])
+        @pl.when(k>=2)
+        def _():
+            out(k-2,slot).wait()
+        stage_ref[slot,:,0:rows_in,:]=dot_tn(gp_ref[k],low_ref[...]).astype(bf).reshape(per,rows_in,D)
+        stage_ref[slot,:,rows_in:2*rows_in,:]=dot_tn(gated_ref[k],dfeed_ref[...]).astype(bf).reshape(per,rows_in,D)
+        out(k,slot).start()
+        acc_ref[...]+=dot_nn(gp_ref[k],w_in)
+        @pl.when(k==tiles-1)
+        def _():
+            def norm(at):
+                d=acc_ref[at,:]
+                u=u1_ref[at,:]
+                r=r1_ref[at,0:1]
+                add_sum(0,d*u)
+                add_sum(3,d)
+                e=d*gain(0)
+                g=(e-mean(e)-u*mean(e*u))*r
+                add_sum(2,g)
+                dres_ref[at,:]=g
+                datt_ref[at,:]=g.astype(bf)
+            chunks(norm)
+            do_ref[...]=(dot_nt(datt_ref[...],wo_ref[...])*scale_ref[...]).astype(bf)
+            outer=dot_tn(ctx_ref[...],datt_ref[...])
+            n=D//own_rows
+            gap=tail_ref.shape[1]-own_rows
+            for p in range(n):
+                piece=outer[p*own_rows:p*own_rows+own_rows,:]
+                if gap:
+                    piece=jnp.concatenate([piece,jnp.zeros((gap,D),f32)],axis=0)
+                tail_ref[p]=piece.astype(bf)
+            last=pltpu.make_async_copy(tail_ref,grad_ref.at[:,pl.ds(2*rows_in,tail_ref.shape[1])],sem.at[2])
+            last.start()
+            if tiles>1:
+                out(k-1,1-slot).wait()
+            out(k,slot).wait()
+            last.wait()
+
+def feed(ctx,tokens,out_grad,scale,out_rows,late,bias,gain,shift,rows_in,own_rows,tiles=4):
+    R,D=ctx.shape
+    n,rows_late,_=late.shape
+    per=n//tiles
+    width=per*rows_in
+    tail=rows_late-2*rows_in
+    vm=lambda s: pl.BlockSpec(s,lambda i: (0,)*len(s))
+    return pl.pallas_call(functools.partial(feed_kernel,R,D,tiles,per,rows_in,own_rows),
+        grid=(2*tiles,),
+        in_specs=[vm((R,D)),vm((R,D)),vm((R,D)),vm((R,D)),vm((D,D)),
+                  pl.BlockSpec((per,rows_late,D),lambda i:(lax.rem(i,tiles),0,0)),
+                  pl.BlockSpec((1,1,width),lambda i:(lax.rem(i,tiles),0,0)),vm((2,D)),vm((4,D))],
+        out_specs=[vm((R,D)),vm((R,D)),vm((R,D)),vm((8,D)),pl.BlockSpec((1,1,width),lambda i:(jnp.maximum(i-tiles,0),0,0)),
+                   pl.BlockSpec(memory_space=pl.ANY)],
+        out_shape=[jax.ShapeDtypeStruct((R,D),bf),jax.ShapeDtypeStruct((R,D),f32),jax.ShapeDtypeStruct((R,D),bf),
+                   jax.ShapeDtypeStruct((8,D),f32),jax.ShapeDtypeStruct((tiles,1,width),f32),
+                   jax.ShapeDtypeStruct((n,rows_late,D),bf)],
+        scratch_shapes=[pltpu.VMEM((R,D),f32),pltpu.VMEM((R,128),f32),pltpu.VMEM((R,D),bf),pltpu.VMEM((R,D),f32),
+                        pltpu.VMEM((R,width),f32),pltpu.VMEM((tiles,R,width),bf),pltpu.VMEM((tiles,R,width),bf),
+                        pltpu.VMEM((R,D),bf),pltpu.VMEM((2,per,2*rows_in,D),bf),pltpu.VMEM((n,tail,D),bf),pltpu.VMEM((R,D),bf),
+                        pltpu.SemaphoreType.DMA((3,))],
+        compiler_params=pltpu.CompilerParams(vmem_limit_bytes=58*1024*1024,dimension_semantics=("arbitrary",)),
+        cost_estimate=pl.CostEstimate(flops=2*R*D*n*rows_in*6+6*R*D*D,bytes_accessed=4*n*rows_late*D+20*R*D,transcendentals=2*R*n*rows_in),
+        name="feed",
+    )(ctx,tokens,out_grad,scale,out_rows,late,bias,gain,shift)
 
 MESH=pl.DeviceIdType.MESH
 
@@ -396,17 +575,8 @@
         name="reduce_end",
     )(spread, pack)
 
-EPS=1e-06
+GROUPS, TILES = 32, 4
 ALL=("tensor","dp")
-
-def layer_norm(values, gain, shift):
-    middle = jnp.mean(values, axis=-1, keepdims=True)
-    centered = values - middle
-    spread = jnp.mean(centered * centered, axis=-1, keepdims=True)
-    return centered * lax.rsqrt(spread + EPS) * gain + shift
-
-def exact_gelu(values):
-    return jax.nn.gelu(values, approximate=False)
 
 def project(inputs, weights, bias):
     return (jnp.einsum("td,fd->tf", inputs, weights, preferred_element_type=f32) + bias).astype(bf)
@@ -426,13 +596,16 @@
     used = misc.shape[0]
     misc = jnp.pad(misc, (0, D - used))[None]
     rel_part = lax.dynamic_slice_in_dim(rel_table, t * part, part, 0)
-    small = jnp.concatenate([misc, rel_part], axis=0)
+    small = jnp.concatenate([rel_part, misc], axis=0)
     early = jnp.concatenate([w_query, w_key, w_value, small], axis=0)
     own_rows = w_query.shape[0]
     late_rows = w_ff_in.shape[0]
     early_rows = early.shape[0]
     early = jnp.pad(early, ((0, -early_rows % 16), (0, 0)))
+    even = late_rows % 16 == 0 and own_rows % 8 == 0
     late = jnp.concatenate([w_ff_in, w_ff_out, w_out], axis=0)
+    late_own = late.shape[0]
+    late = jnp.pad(late, ((0, -late_own % 16), (0, 0)))
     gathered, early_all = gather_start(tokens, early, n_t, n_dp)
     late_all = lax.all_gather(late, ALL, axis=0, tiled=False)
     gathered = gathered.reshape(L, D)
@@ -440,9 +613,14 @@
     cut = lambda x, at, n: x[:, at:at + n].reshape(n_all * n, D)
     query_rows, key_rows, value_rows = [cut(early_all, i * own_rows, own_rows) for i in range(3)]
     small_all = early_all[:, 3 * own_rows:early_rows]
-    inner_rows, outer_rows = cut(late_all, 0, late_rows), cut(late_all, late_rows, late_rows)
     out_rows = cut(late_all, 2 * late_rows, own_rows)
-    misc_all = small_all[:, 0]
+    groups = n_all if even else GROUPS
+    group_rows, group_own = n_all * late_rows // groups, D // groups
+    if not even:
+        sections = [cut(late_all, 0, late_rows), cut(late_all, late_rows, late_rows)]
+        late_all = jnp.concatenate([x.reshape(groups, group_rows, D) for x in sections]
+                                   + [jnp.zeros((groups, -(-group_own // 16) * 16, D), bf)], axis=1)
+    misc_all = small_all[:, part]
     o1 = 3 * wide
     o2 = o1 + inner
     o3 = o2 + 2 * cols
@@ -451,7 +629,7 @@
     first = misc_all[:n_dp]
     gain = first[:, o2:o3].reshape(n_dp, 2, cols).transpose(1, 0, 2).reshape(2, D).astype(f32)
     shift = first[:, o3:used].reshape(n_dp, 4, cols).transpose(1, 0, 2).reshape(4, D).astype(f32)
-    table = small_all[:, 1:].reshape(n_t, n_dp, part, D).transpose(1, 0, 2, 3).reshape(NB, D)
+    table = small_all[:, :part].reshape(n_t, n_dp, part, D).transpose(1, 0, 2, 3).reshape(NB, D)
 
     query = project(tokens, query_rows, bias[0])
     key = project(gathered, key_rows, bias[1])
@@ -469,42 +647,23 @@
     pick_u = pick(back, R * t)
     key_table = jnp.dot(pick_x, key_rel, preferred_element_type=f32).astype(bf)
     query_table = jnp.dot(pick_u, query_rel, preferred_element_type=f32).astype(bf)
-    mask = jnp.where(jnp.arange(L, dtype=jnp.int32)[None, :] < lengths[0], 0.0, -1e9).astype(f32)
+    mask = jnp.where(jnp.arange(L, dtype=jnp.int32) < lengths[0], 0.0, -1e9).astype(bf)
+    mask = jnp.broadcast_to(mask[:, None], (L, 128))
 
     context, scale, shares = attention_forward(query, key, value, key_table, query_table, mask)
-    attended = jnp.dot(context, out_rows, preferred_element_type=f32)
-    resid_one = tokens.astype(f32) + attended + shift[0]
-    hidden_one, norm_one_back = jax.vjp(layer_norm, resid_one, gain[0], shift[1])
-    hidden_low = hidden_one.astype(bf)
-    pre = jnp.einsum("td,fd->tf", hidden_low, inner_rows, preferred_element_type=f32) + inner_bias
-    activated, gelu_back = jax.vjp(exact_gelu, pre)
-    gated = activated.astype(bf)
-    feed_out = jnp.dot(gated, outer_rows, preferred_element_type=f32)
-    resid_two = hidden_one + feed_out + shift[2]
-    final_value, norm_two_back = jax.vjp(layer_norm, resid_two, gain[1], shift[3])
-    layer_result_rows = final_value.astype(bf)
-    d_resid_two, d_gain_two, d_shift_three = norm_two_back(out_grad.astype(f32))
-    d_shift_two = jnp.sum(d_resid_two, axis=0)
-    d_feed = d_resid_two.astype(bf)
-    d_gated = jnp.einsum("td,fd->tf", d_feed, outer_rows, preferred_element_type=f32)
-    grad_outer = jnp.einsum("tf,td->fd", gated, d_feed, preferred_element_type=f32)
-    d_pre = gelu_back(d_gated)[0].astype(bf)
-    grad_inner = jnp.einsum("tf,td->fd", d_pre, hidden_low, preferred_element_type=f32)
-    grad_bias_inner = jnp.sum(d_pre.astype(f32), axis=0)
-    d_hidden_one = d_resid_two + jnp.dot(d_pre, inner_rows, preferred_element_type=f32)
-    d_resid_one, d_gain_one, d_shift_one = norm_one_back(d_hidden_one)
-    d_shift_zero = jnp.sum(d_resid_one, axis=0)
-    d_attended = d_resid_one.astype(bf)
-    grad_out = jnp.einsum("tf,td->fd", context, d_attended, preferred_element_type=f32)
-    d_context = jnp.einsum("td,fd->tf", d_attended, out_rows, preferred_element_type=f32)
-    d_scaled = (d_context * scale).astype(bf)
+    layer_result_rows, d_resid_one, d_scaled, sums, bias_sums, late_grad = feed(
+        context, tokens, out_grad, scale, out_rows, late_all, inner_bias.reshape(TILES, 1, -1), gain, shift, group_rows, group_own)
     d_query, d_key, d_value, d_key_rel, d_query_rel = attention_backward(
         query, key, value, d_scaled, context, shares, key_rel, query_rel, pick_x, pick_y)
 
     parted = lambda x: x.astype(bf).reshape(n_all, -1, D)
-    late_grad = jnp.concatenate([parted(grad_inner), parted(grad_outer), parted(grad_out)], axis=1)
+    if not even:
+        late_grad = jnp.concatenate([
+            parted(late_grad[:, :group_rows]), parted(late_grad[:, group_rows:2 * group_rows]),
+            parted(late_grad[:, 2 * group_rows:2 * group_rows + group_own]),
+            jnp.zeros((n_all, late.shape[0] - late_own, D), bf)], axis=1)
     late_sum = lax.psum_scatter(late_grad, ALL, scatter_dimension=0, tiled=True)[0].astype(f32)
-    g_inner, g_outer, g_out = late_sum[:late_rows], late_sum[late_rows:2 * late_rows], late_sum[2 * late_rows:]
+    g_inner, g_outer, g_out = late_sum[:late_rows], late_sum[late_rows:2 * late_rows], late_sum[2 * late_rows:late_own]
     dqr, dkr = d_query_rel.astype(bf), d_key_rel.astype(bf)
     grad_query = jnp.einsum("tf,td->fd", d_query, tokens, preferred_element_type=f32) + jnp.einsum(
         "tf,td->fd", dqr, table, preferred_element_type=f32)
@@ -519,15 +678,13 @@
     own = jnp.dot(d_query, query_rows, preferred_element_type=f32)
     spread = (jnp.dot(d_key, key_rows, preferred_element_type=f32)
               + jnp.dot(d_value, value_rows, preferred_element_type=f32)).astype(bf)
-    gain_grads = jnp.stack([d_gain_one, d_gain_two])
-    shift_grads = jnp.stack([d_shift_zero, d_shift_one, d_shift_two, d_shift_three])
     shape_dp = lambda x, k: jnp.broadcast_to(
         x.reshape(k, n_dp, cols).transpose(1, 0, 2).reshape(1, n_dp, k * cols), (n_t, n_dp, k * cols)).reshape(n_all, k * cols)
     line = jnp.concatenate([
         bias_gradient.reshape(3, n_all, wide).transpose(1, 0, 2).reshape(n_all, o1),
-        grad_bias_inner.reshape(n_all, inner),
-        shape_dp(gain_grads, 2), shape_dp(shift_grads, 4)], axis=1)
-    line = jnp.pad(line, ((0, 0), (0, D - used)))[:, None]
+        bias_sums.reshape(n_all, inner),
+        shape_dp(sums[:2], 2), shape_dp(sums[2:6], 4)], axis=1)
+    line = jnp.pad(line[:, None], ((0, 0), (0, 7), (0, D - used)))
     rel_rows = rel_table.shape[0]
     d_rel_all = jnp.broadcast_to(d_rel.reshape(1, n_dp, rel_rows, D), (n_t, n_dp, rel_rows, D)).reshape(n_all, rel_rows, D)
     early_grad = jnp.concatenate([parted(grad_query), parted(grad_key), parted(grad_value), line.astype(bf), d_rel_all.astype(bf)], axis=1)
@@ -537,7 +694,7 @@
     tokens_grad = d_resid_one + own + back_sum
     g_query, g_key, g_value = [early_sum[i * own_rows:(i + 1) * own_rows] for i in range(3)]
     row = early_sum[3 * own_rows]
-    g_rel = early_sum[3 * own_rows + 1:end_rows]
+    g_rel = early_sum[3 * own_rows + 8:end_rows]
     return (layer_result_rows, tokens_grad, g_query, g_key, g_value, g_out,
             row[:o1].reshape(3, wide), g_inner, g_outer, row[o1:o2], g_rel,
             row[o2:o3].reshape(2, cols), row[o3:used].reshape(4, cols))

time: 645 us -> 520 us (0.81)
  the two profiles are of different devices: /device:TPU:0 before, /device:TPU:13 now
where the time goes in v3:
time: 520 us; the launch traced here: 511 us
  Pallas kernels  394 us (76%)
  local copies, waits for them, and re-layouts  50.3 us (10%)
  matrix products  35.3 us (7%)
  other arithmetic  15.9 us (3%)
  between operations  15.3 us (3%)
    pallas_call x1, Pallas kernels, gather_start(): pl.pallas_call(functools.partial(gather_kernel, n_t, n_dp), out_shape=[ja...  105 us
    pallas_call x1, Pallas kernels, reduce_end(): pl.pallas_call(functools.partial(reduce_kernel, n_t, n_dp), out_shape=[ja...  92.7 us
    pallas_call x1, Pallas kernels, attention_backward(): pl.pallas_call(functools.partial(bwd_kernel, R, L, B, C), grid=(pairs, 2)...  88.2 us
    pallas_call x1, Pallas kernels, attention_forward(): pl.pallas_call(functools.partial(fwd_kernel, R, L, B, C), grid=(pairs, 2)...  64.3 us
    pallas_call x1, Pallas kernels, feed(): pl.pallas_call(functools.partial(feed_kernel, R, D, tiles, per, rows_in,...  43.9 us
    unnamed x53, local copies, waits for them, and re-layouts  12.7 us
  transfers between devices with their start and end apart: 2, of which 0 were waited for; matrix products, arithmetic and copies ran while one was open for 18% of the time, Pallas kernels for 69%

profile of v3, /device:TPU:13, one launch (start us, length us, event | category | flops | bytes accessed | tf_op | source)
XLA Modules:
  0.0 510.9 jit_solution(17982979120174030625)
XLA Ops:
  7.2 1.8 fusion.12
  9.1 0.8 reshape.224
  9.8 0.8 reshape.222
  10.6 0.7 reshape.223
  11.3 0.7 fusion.27
  12.1 0.8 constant_dynamic-update-slice_fusion.4
  12.8 0.8 constant_dynamic-update-slice_fusion.3
  13.6 0.8 constant_dynamic-update-slice_fusion.2
  14.4 0.7 constant_dynamic-update-slice_fusion.1
  15.8 105.0 %gather_start.1 = (bf16[4,512,768]{2,1,0:T(8,128)(2,1)}, bf16[4,4,2,96,768]{4,3,2,1,0:T(8,128)(2,1)}) custom-call(bf16[512,768]{1,0:T(8,128)(2,1)} %tok_ref.3, bf16[96,768]{1,0:T(8,128)(2,1)} %pad.18.pack_ref), custom_call_target="tpu_custom_call" | custom-call | tf_op jit(solution)/shard_map/gather_start/pallas_call | solution.py:444
  120.7 1.1 slice.146
  121.8 1.0 slice.153
  122.8 0.9 slice.156
  125.3 0.7 reshape.243.bias_ref
  127.8 2.4 fusion.28
  131.9 0.8 fusion.4.q_ref
  132.8 3.5 convolution_convert_fusion.1.kt_ref
  136.3 3.4 convolution_convert_fusion.qr_ref
  139.7 4.0 add_convert_fusion.2.k_ref
  143.7 4.0 add_convert_fusion.1.v_ref
  148.0 64.3 %attend.1 = (bf16[512,768]{1,0:T(8,128)(2,1)S(1)}, f32[512,768]{1,0:T(8,128)S(1)}, bf16[12,512,2048]{2,1,0:T(8,128)(2,1)}) custom-call(bf16[2048,128]{1,0:T(8,128)(2,1)S(1)} %broadcast_in_dim.46.mask_ref, bf16[512,768]{1,0:T(8,128)(2,1)S(1)} %fusion.4.q_ref, bf16[2048,768]{1,0:T(8,128)(2,1)} %add_convert_fusion.2.k_ref, ...), custom_call_target="tpu_custom_call" | custom-call | flops 12884901888 | bytes 40894464 | tf_op jit(solution)/shard_map/attend/pallas_call | solution.py:111
  212.3 1.1 copy-done.2
  213.4 0.9 copy-done.3
  214.4 2.4 slice.154
  216.7 43.9 %feed.1 = (bf16[512,768]{1,0:T(8,128)(2,1)}, f32[512,768]{1,0:T(8,128)}, bf16[512,768]{1,0:T(8,128)(2,1)}, f32[8,768]{1,0:T(8,128)}, f32[4,1,768]{2,1,0:T(1,128)}, /*index=5*/bf16[32,224,768]{2,1,0:T(8,128)(2,1)}) custom-call(bf16[512,768]{1,0:T(8,128)(2,1)} %copy-done.3, bf16[512,768]{1,0:T(8,128)(2,1)} %tok_ref.3, bf16[512,768]{1,0:T(8,128)(2,1)} %og_ref.1, ...), custom_call_target="tpu_custom_call" | custom-call | flops 16307453952 | bytes 29884416 | tf_op jit(solution)/shard_map/feed/pallas_call | solution.py:325
  260.7 2.8 fusion
  263.5 1.3 slice.176
  264.8 1.3 slice.177
  266.2 88.2 %attend_back.1 = (bf16[512,768]{1,0:T(8,128)(2,1)S(1)}, bf16[2048,768]{1,0:T(8,128)(2,1)}, bf16[2048,768]{1,0:T(8,128)(2,1)}, f32[256,768]{1,0:T(8,128)S(1)}, f32[256,768]{1,0:T(8,128)S(1)}) custom-call(bf16[512,768]{1,0:T(8,128)(2,1)S(1)} %copy-done.1, bf16[2048,768]{1,0:T(8,128)(2,1)} %add_convert_fusion.2.k_ref, ...), custom_call_target="tpu_custom_call" | custom-call | flops 25769803776 | bytes 56623104 | tf_op jit(solution)/shard_map/attend_back/pallas_call | solution.py:185
  354.7 2.5 convert_reduce_fusion
  357.9 0.8 add.137
  358.6 3.0 reduce
  361.6 1.4 stack.8
  363.0 1.3 maximum_bitcast_fusion.1
  364.3 1.4 copy.67
  365.7 1.4 copy.70
  367.1 0.8 reshape.252
  368.6 0.8 reshape.251
  370.1 0.7 convert_reduce_fusion.2
  370.9 0.7 broadcast_bitcast_fusion.1
  371.6 0.7 broadcast_bitcast_fusion
  372.3 0.8 maximum_bitcast_fusion
  373.2 0.8 fusion.32
  374.6 1.1 constant_dynamic-update-slice_fusion.8
  376.4 1.0 copy-done.19
  377.4 2.7 fusion.33
  380.7 1.1 constant_dynamic-update-slice_fusion.7
  381.8 0.7 copy-done.10
  382.5 2.8 convolution_convert_fusion.2
  385.3 1.1 constant_dynamic-update-slice_fusion.6
  386.4 0.9 constant_dynamic-update-slice_fusion.5
  388.3 1.4 broadcast_dynamic-update-slice_fusion.pack_ref
  389.7 2.9 fusion.31
  392.5 4.1 add_convert_fusion
  396.6 92.7 %reduce_end.1 = (f32[512,768]{1,0:T(8,128)}, f32[112,768]{1,0:T(8,128)}) custom-call(bf16[4,512,768]{2,1,0:T(8,128)(2,1)} %bitcast.102, bf16[4,4,2,112,768]{4,3,2,1,0:T(8,128)(2,1)} %broadcast_dynamic-update-slice_fusion.pack_ref), custom_call_target="tpu_custom_call" | custom-call | tf_op jit(solution)/shard_map/reduce_end/pallas_call | solution.py:564
  489.3 1.5 slice.142
  490.8 0.8 slice_reduce_fusion
  492.3 0.7 slice_reduce_fusion.2
  493.6 0.8 slice_reduce_fusion.1
  495.1 1.3 slice_bitcast_fusion.3
  496.4 1.6 fusion.29
  498.0 3.3 add_add_fusion
  501.3 1.0 convert_element_type.161
  502.4 0.8 slice_bitcast_fusion
  (94 shorter events, 13.4 us)
Async XLA Ops:
  7.2 116.9 %copy-start.17 = (s32[4095]{0:T(1024)S(1)}, s32[4095]{0:T(1024)}, u32[]{:S(2)}) copy-start(s32[4095]{0:T(1024)} %param.27) | copy-start | bytes 49144
  7.2 207.2 %all-gather.3.cloned.1.call-start = ((), (), s32[]{:S(2)}) async-start(), calls=%async_computation.2 | async-start | bytes 11354112 | tf_op jit(solution)/shard_map/all_gather | solution.py:610
  9.0 492.3 %reduce-scatter.2.cloned.1.call-start = ((), (), s32[]{:S(2)}) async-start(), calls=%async_computation.1 | async-start | bytes 11354112 | tf_op jit(solution)/shard_map/reduce_scatter | solution.py:665
  130.2 2.6 copy-start.6
  130.2 9.5 %copy-start.8 = (bf16[32,24,768]{2,1,0:T(8,128)(2,1)}, bf16[32,24,768]{2,1,0:T(8,128)(2,1)S(1)}, u32[]{:S(2)}) copy-start(bf16[32,24,768]{2,1,0:T(8,128)(2,1)S(1)} %get-tuple-element.50) | copy-start | bytes 3538948
  130.2 13.5 %copy-start.15 = (bf16[32,24,768]{2,1,0:T(8,128)(2,1)}, bf16[32,24,768]{2,1,0:T(8,128)(2,1)S(1)}, u32[]{:S(2)}) copy-start(bf16[32,24,768]{2,1,0:T(8,128)(2,1)S(1)} %get-tuple-element.49) | copy-start | bytes 3538948
  130.2 1.7 copy-start.12
  132.8 15.2 %copy-start = (bf16[512,768]{1,0:T(8,128)(2,1)}, bf16[512,768]{1,0:T(8,128)(2,1)S(1)}, u32[]{:S(2)}) copy-start(bf16[512,768]{1,0:T(8,128)(2,1)S(1)} %fusion.4.q_ref) | copy-start | bytes 2359300
  136.3 3.4 copy-start.18
  212.3 1.1 copy-start.2
  213.4 0.9 copy-start.3
  260.6 5.5 %copy-start.1 = (bf16[512,768]{1,0:T(8,128)(2,1)S(1)}, bf16[512,768]{1,0:T(8,128)(2,1)}, u32[]{:S(2)}) copy-start(bf16[512,768]{1,0:T(8,128)(2,1)} %copy-done) | copy-start | bytes 2359300
  260.6 5.5 %copy-start.4 = (bf16[512,768]{1,0:T(8,128)(2,1)S(1)}, bf16[512,768]{1,0:T(8,128)(2,1)}, u32[]{:S(2)}) copy-start(bf16[512,768]{1,0:T(8,128)(2,1)} %copy-done.3) | copy-start | bytes 2359300
  260.6 5.5 %copy-start.5 = (bf16[512,768]{1,0:T(8,128)(2,1)S(1)}, bf16[512,768]{1,0:T(8,128)(2,1)}, u32[]{:S(2)}) copy-start(bf16[512,768]{1,0:T(8,128)(2,1)} %get-tuple-element.37.do_ref) | copy-start | bytes 2359300
  357.3 16.0 %copy-start.13 = (bf16[512,768]{1,0:T(8,128)(2,1)S(1)}, bf16[512,768]{1,0:T(8,128)(2,1)}, u32[]{:S(2)}) copy-start(bf16[512,768]{1,0:T(8,128)(2,1)} %tok_ref.3) | copy-start | bytes 2359300
  374.1 2.3 copy-start.11
  374.1 3.3 copy-start.19
  380.1 2.4 copy-start.10
  385.2 2.1 copy-start.7
  385.3 2.5 copy-start.9
  389.7 2.9 copy-start.16
  396.6 101.4 %copy-start.14 = (f32[512,768]{1,0:T(8,128)S(1)}, f32[512,768]{1,0:T(8,128)}, u32[]{:S(2)}) copy-start(f32[512,768]{1,0:T(8,128)} %get-tuple-element.36) | copy-start | bytes 4718596
Sparse Core Ops, SparseCore 0:
  11.5 126.8 all-gather.2
  260.7 144.5 reduce-scatter.1

commit v4 on v3

--- a/solution.py
+++ b/solution.py
@@ -152,7 +152,7 @@
             ds_ref[at,:]=ds
             part=jnp.concatenate([ds,jnp.zeros((16,B),bf)],axis=1)
             wide[rows,:]=pltpu.roll(part,16*g,1,stride=1,stride_axis=0)
-        db=dot_nn(wide[...],ox_ref[r0:r0+L+B,:]).astype(bf)
+        db=dot_nt(wide[...],ox_ref[:,r0:r0+L+B]).astype(bf)
         dq=dot_nn(ds_ref[r0:r0+B,:],k_ref[...])+dot_nn(db,kr_ref[...])
         dqa_ref[r0:r0+B,:]=jnp.where(own,dq,dqa_ref[r0:r0+B,:])
         dkr_ref[...]+=dot_tn(db,qrev_ref[r0:r0+B,:])
@@ -166,7 +166,7 @@
             rows=slice(16*g,16*g+16)
             part=jnp.concatenate([dst[rows,:],jnp.zeros((16,C),bf)],axis=1)
             wide[rows,:]=pltpu.roll(part,16*g,1,stride=1,stride_axis=0)
-        db=dot_nn(wide[...],oy_ref[i*C:i*C+R+C,:]).astype(bf)
+        db=dot_nt(wide[...],oy_ref[:,i*C:i*C+R+C]).astype(bf)
         dka_ref[at,:]+=dot_nn(dst[...],qrev_ref[...])+dot_nn(db,qrel)
         dva_ref[at,:]+=dot_tn(e_ref[0,:,at],dor_ref[...])
         kb=jnp.where(ownk,k_ref[at,:],zero)
@@ -180,7 +180,7 @@
 def attention_backward(q,k,v,do,ctx,e,key_rel,query_rel,onehot_x,onehot_y,B=128,C=128):
     R,F=q.shape; L=k.shape[0]; W=L+R; pairs=F//128
     col=lambda n: pl.BlockSpec((n,128),lambda p,h:(0,p))
-    full=pl.BlockSpec((W,NB),lambda p,h:(0,0))
+    full=pl.BlockSpec((NB,W),lambda p,h:(0,0))
     flops=2*pairs*2*R*L*128*8
     return pl.pallas_call(functools.partial(bwd_kernel,R,L,B,C),
         grid=(pairs,2),
@@ -341,15 +341,13 @@
         name="feed",
     )(ctx,tokens,out_grad,scale,out_rows,late,bias,gain,shift)
 
-MESH=pl.DeviceIdType.MESH
-
-def places(n_t, n_dp):
-    dp, t = lax.axis_index("dp"), lax.axis_index("tensor")
-    high, core = dp // 2, dp % 2
-    bits = (n_dp // 2).bit_length() - 1
-    flips = [high + (1 - 2 * ((high // 2**i) % 2)) * 2**i for i in range(bits)]
-    right, left = lax.rem(t + 1, n_t), lax.rem(t + n_t - 1, n_t)
-    return dp, t, high, core, bits, flips, right, left
+MESH = pl.DeviceIdType.MESH
+ANY = pl.BlockSpec(memory_space=pl.ANY)
+VM = pl.BlockSpec(memory_space=pltpu.VMEM)
+
+def remote(src, dst, send, recv, peer):
+    return pltpu.make_async_remote_copy(src_ref=src, dst_ref=dst, send_sem=send, recv_sem=recv,
+                                        device_id=peer, device_id_type=MESH)
 
 def meet(peers):
     barrier = pltpu.get_barrier_semaphore()
@@ -357,229 +355,518 @@
         pl.semaphore_signal(barrier, inc=1, device_id=peer, device_id_type=MESH)
     pl.semaphore_wait(barrier, len(peers))
 
-def remote(src, dst, send, recv, peer):
-    return pltpu.make_async_remote_copy(src_ref=src, dst_ref=dst, send_sem=send, recv_sem=recv,
-                                        device_id=peer, device_id_type=MESH)
-
-def interleave(*lists):
-    out = []
-    for i in range(max(len(x) for x in lists)):
-        out += [x[i] for x in lists if i < len(x)]
-    return out
-
-def gather_kernel(n_t, n_dp, tok_ref, pack_ref, toks_ref, packs_ref, own_sem, tok_send, tok_recv, pack_send, pack_recv):
-    dp, t, high, core, bits, flips, right, left = places(n_t, n_dp)
-    peers = [{"tensor": right}, {"tensor": left}, {"dp": high * 2 + 1 - core}] + [{"dp": f * 2 + core} for f in flips]
-    meet(peers)
-    own_tok = pltpu.make_async_copy(tok_ref, toks_ref.at[t], own_sem.at[0])
-    own_pack = pltpu.make_async_copy(pack_ref, packs_ref.at[t, high, core], own_sem.at[1])
-    own_tok.start()
+class Place:
+    def __init__(self, n_t, n_dp):
+        self.n_t, self.n_dp = n_t, n_dp
+        bits = (n_dp // 2).bit_length() - 1
+        self.low = bits // 2
+        self.high = bits - self.low
+        dp, self.t = lax.axis_index("dp"), lax.axis_index("tensor")
+        self.core = dp % 2
+        self.down = (dp // 2) % 2**self.low
+        self.up = dp // 2 // 2**self.low
+        self.others = [lax.rem(self.t + 1 + i, n_t) for i in range(n_t - 1)]
+        self.twin = {"dp": dp - self.core + 1 - self.core}
+        self.steps = [("down", i) for i in range(self.low)] + [("up", i) for i in range(self.high)]
+
+    def bit(self, step):
+        kind, i = step
+        return (getattr(self, kind) // 2**i) % 2
+
+    def peer(self, step):
+        kind, i = step
+        turn = (1 - 2 * self.bit(step)) * 2**i
+        down = self.down + turn if kind == "down" else self.down
+        up = self.up + turn if kind == "up" else self.up
+        return {"dp": (up * 2**self.low + down) * 2 + self.core}
+
+    def peers(self):
+        return [{"tensor": o} for o in self.others] + [self.twin] + [self.peer(s) for s in self.steps]
+
+    def orders(self):
+        down = [s for s in self.steps if s[0] == "down"]
+        up = [s for s in self.steps if s[0] == "up"]
+        return [down + up, up + down]
+
+    def spans(self, done):
+        out = []
+        for kind in ("up", "down"):
+            n = sum(1 for s in done if s[0] == kind)
+            here = getattr(self, kind)
+            out.append(pl.ds((here // 2**n) * 2**n, 2**n))
+        return out
+
+    def parts(self):
+        half = self.n_t // 2
+        return [pl.ds(0, half), pl.ds(half, half)] if half else [pl.ds(0, 1)]
+
+def lanes_of(count, width, shape, tall):
+    wide_axis = 0 if tall else 1
+    f = lax.broadcasted_iota(jnp.int32, shape, wide_axis)
+    r = lax.broadcasted_iota(jnp.int32, shape, 1 - wide_axis)
+    return jnp.where(f % count == r, 1.0, 0.0).astype(bf)
+
+def spread_row(table, count, width, first):
+    n = table.shape[0]
+    full = dot_nn(table.astype(bf), lanes_of(count, width, (128, width), False))
+    p = lax.broadcasted_iota(jnp.int32, (n, width), 0)
+    f = lax.broadcasted_iota(jnp.int32, (n, width), 1)
+    return jnp.sum(jnp.where(first + f // count == p, full, 0.0), axis=0, keepdims=True)
+
+def fold_row(row, count, n, first):
+    width = row.shape[1]
+    p = lax.broadcasted_iota(jnp.int32, (n, width), 0)
+    f = lax.broadcasted_iota(jnp.int32, (n, width), 1)
+    full = jnp.where(first + f // count == p, jnp.broadcast_to(row, (n, width)), 0.0)
+    return dot_nn(full.astype(bf), lanes_of(count, width, (width, 128), True))
+
+def eight(n):
+    return -(-n // 8) * 8
+
+def begin_kernel(n_t, n_dp, own, part, cols, inner, tiles, L,
+                 tok_ref, wq_ref, wk_ref, wv_ref, rel_ref, qkvb_ref, ffb_ref, gains_ref, shifts_ref, ahead_ref, back_ref,
+                 q_out, k_out, v_out, krel_out, qrel_out, kt_out, qr_out, toks_out, w_out, ox_out, oy_out, table_out,
+                 ibias_ref, gain_ref, shift_ref,
+                 toks, packs, pack, packf, wf, w, kb, vb, qb, krel, qrel, kt, qr, table, tableb, miscf, ox, oy,
+                 tok_send, tok_recv, z_send, z_recv, x_send, x_recv, out_sem):
+    at = Place(n_t, n_dp)
+    t = at.t
+    R, D = tok_ref.shape
+    W = L + R
+    n_all = n_t * n_dp
+    S, S2 = eight(own), eight(part)
+    misc = 3 * S + S2
+    right = {"tensor": lax.rem(t + 1, n_t)}
+
+    packf[...] = jnp.zeros_like(packf)
+    for i, ref in enumerate((wq_ref, wk_ref, wv_ref)):
+        packf[i * S:i * S + own, :] = ref[...].astype(f32)
+    for i in range(n_t):
+        @pl.when(t == i)
+        def _():
+            packf[3 * S:3 * S + part, :] = rel_ref[...].astype(f32)[i * part:(i + 1) * part]
+    for i in range(3):
+        packf[misc:misc + 1, 128 * i:128 * i + own] = qkvb_ref[i:i + 1, :].astype(f32)
+    packf[misc:misc + 1, 384:384 + inner] = ffb_ref[...].astype(f32)
+    for i in range(2):
+        packf[misc + 1:misc + 2, 128 * i:128 * i + cols] = gains_ref[i:i + 1, :].astype(f32)
+    for i in range(4):
+        packf[misc + 1:misc + 2, 256 + 128 * i:256 + 128 * i + cols] = shifts_ref[i:i + 1, :].astype(f32)
+    pack[...] = packf[...].astype(bf)
+
+    meet(at.peers())
+    copies = []
+
+    def go(copy):
+        copy.start()
+        copies.append(copy)
+        return copy
+
+    here = packs.at[t, at.up, at.down, at.core]
+    ring = [go(remote(pack, here, z_send.at[i], z_recv.at[i], {"tensor": o})) for i, o in enumerate(at.others)]
+    half = R // 2
+    token = {}
+
+    def send_token(s):
+        b = lax.rem(t - s + n_t, n_t)
+        src = tok_ref if s == 0 else toks.at[b]
+        for j in range(2):
+            if s:
+                token[s - 1, j].wait_recv()
+            rows = pl.ds(j * half, half)
+            token[s, j] = go(remote(src.at[rows], toks.at[b, rows], tok_send.at[s, j], tok_recv.at[s, j], right))
+
+    send_token(0)
+    own_pack = pltpu.make_async_copy(pack, here, out_sem.at[0])
     own_pack.start()
-    rows = tok_ref.shape[0]
-    half = rows // 2
-    token = {}
-    pack = {}
-
-    def send_pack(s):
+    outs = []
+
+    def put(src, dst):
+        copy = pltpu.make_async_copy(src, dst, out_sem.at[1 + len(outs)])
+        copy.start()
+        outs.append(copy)
+
+    def pick(line, start):
+        rows = line[:, pl.ds(pl.multiple_of(start, 128), W)]
+        ids = lax.broadcasted_iota(jnp.int32, (NB, W), 0)
+        return jnp.where(ids == rows, 1.0, 0.0).astype(bf)
+
+    ox[...] = pick(back_ref, L - R - R * t)
+    oy[...] = pick(ahead_ref, L - R - R * t)
+    put(ox, ox_out)
+    put(oy, oy_out)
+
+    for copy in ring:
+        copy.wait_recv()
+    own_pack.wait()
+    parts, orders = at.parts(), at.orders()
+    n_steps = len(at.steps)
+    swaps = {}
+
+    def swap(h, k):
+        if k:
+            swaps[h, k - 1].wait_recv()
+        up, down = at.spans(orders[h][:k])
+        if k < n_steps:
+            piece, peer = packs.at[parts[h], up, down, at.core], at.peer(orders[h][k])
+        else:
+            piece, peer = packs.at[parts[h], :, :, at.core], at.twin
+        swaps[h, k] = go(remote(piece, piece, x_send.at[h, k], x_recv.at[h, k], peer))
+
+    hs = range(len(parts))
+    sent = 1
+    for k in range(n_steps + 1):
+        for h in hs:
+            swap(h, k)
+        if k and sent < n_t - 1:
+            send_token(sent)
+            sent += 1
+    for h in hs:
+        swaps[h, n_steps].wait_recv()
+
+    slots = [(a, u, d, c) for a in range(n_t) for u in range(2**at.high) for d in range(2**at.low) for c in range(2)]
+    for i in range(3):
+        for p, s in enumerate(slots):
+            wf[p * own:p * own + own, :] = packs[s[0], s[1], s[2], s[3], i * S:i * S + own, :].astype(f32)
+        w[i] = wf[...].astype(bf)
+    put(w, w_out)
+    for p, s in enumerate(slots):
+        rows = packs[s[0], s[1], s[2], s[3], misc:misc + 8, :].astype(f32)
+        miscf[0, p:p + 1, :] = rows[0:1]
+        miscf[1, p:p + 1, :] = rows[1:2]
+        a, dp = p // n_dp, p % n_dp
+        to = dp * n_t * part + a * part
+        table[to:to + part, :] = packs[s[0], s[1], s[2], s[3], 3 * S:3 * S + part, :].astype(f32)
+    bias = [spread_row(miscf[0, :, 128 * i:128 * i + 128], own, D, 0) for i in range(3)]
+    rel = table[...].astype(bf)
+    tableb[...] = rel
+    put(tableb, table_out)
+    krel[...] = (dot_nt(rel, w[1]) + bias[1]).astype(bf)
+    qrel[...] = (dot_nt(rel, w[0]) + bias[0]).astype(bf)
+    put(krel, krel_out)
+    put(qrel, qrel_out)
+    kt[...] = dot_tn(ox[...], krel[...]).astype(bf)
+    put(kt, kt_out)
+    qr[...] = dot_tn(pick(back_ref, R * t), qrel[...]).astype(bf)
+    put(qr, qr_out)
+    while sent < n_t - 1:
+        send_token(sent)
+        sent += 1
+
+    def project(tokens, i):
+        return (dot_nt(tokens, w[i]) + bias[i]).astype(bf)
+
+    qb[...] = project(tok_ref[...], 0)
+    put(qb, q_out)
+    width = n_all * inner // tiles
+    for i in range(tiles):
+        ibias_ref[i] = spread_row(miscf[0, :, 384:512], inner, width, i * (n_all // tiles))
+    for i in range(2):
+        gain_ref[i:i + 1, :] = spread_row(miscf[1, 0:n_dp, 128 * i:128 * i + 128], cols, D, 0)
+    for i in range(4):
+        shift_ref[i:i + 1, :] = spread_row(miscf[1, 0:n_dp, 256 + 128 * i:384 + 128 * i], cols, D, 0)
+
+    for s in range(n_t):
         b = lax.rem(t - s + n_t, n_t)
-        src = pack_ref if s == 0 else packs_ref.at[b, high, core]
-        pack[s] = remote(src, packs_ref.at[b, high, core], pack_send.at[s], pack_recv.at[s], {"tensor": right})
-        pack[s].start()
-
-    def send_token(s, j):
-        b = lax.rem(t - s + n_t, n_t)
-        src = (tok_ref if s == 0 else toks_ref.at[b]).at[pl.ds(j * half, half)]
-        token[s, j] = remote(src, toks_ref.at[b, pl.ds(j * half, half)], tok_send.at[s, j], tok_recv.at[s, j], {"tensor": right})
-        token[s, j].start()
-
-    def swap(i):
-        s = n_t - 1 + i
-        if i < bits:
-            base = (high // 2**i) * 2**i
-            part = packs_ref.at[:, pl.ds(base, 2**i), core]
-            peer = {"dp": flips[i] * 2 + core}
-        else:
-            part = packs_ref.at[:, :, core]
-            peer = {"dp": high * 2 + 1 - core}
-        pack[s] = remote(part, part, pack_send.at[s], pack_recv.at[s], peer)
-        pack[s].start()
-
-    send_pack(0)
-    send_token(0, 0)
-    send_token(0, 1)
-    for s in range(1, n_t - 1):
-        pack[s - 1].wait_recv()
-        send_pack(s)
-    pack[n_t - 2].wait_recv()
-    own_pack.wait()
-    swap(0)
-
-    def token_step(s):
-        def run():
+        rows = pl.ds(pl.multiple_of(b * R, R), R)
+        if s == n_t - 1:
             for j in range(2):
                 token[s - 1, j].wait_recv()
-                if s < n_t - 1:
-                    send_token(s, j)
-        return run
-
-    def pack_step(i):
-        def run():
-            pack[n_t - 1 + i - 1].wait_recv()
-            if i <= bits:
-                swap(i)
-        return run
-
-    for step in interleave([token_step(s) for s in range(1, n_t)], [pack_step(i) for i in range(1, bits + 2)]):
-        step()
-    own_tok.wait()
-    for copy in list(pack.values()) + list(token.values()):
+        src = tok_ref if s == 0 else toks.at[b]
+        put(src, toks_out.at[b])
+        kb[s] = project(src[...], 1)
+        put(kb.at[s], k_out.at[rows])
+        vb[s] = project(src[...], 2)
+        put(vb.at[s], v_out.at[rows])
+    for copy in outs:
+        copy.wait()
+    for copy in copies:
         copy.wait_send()
 
-def gather_start(tokens, pack, n_t, n_dp):
-    rows, D = tokens.shape
-    pr = pack.shape[0]
+def begin(tokens, w_query, w_key, w_value, rel_table, qkv_bias, ff_bias, gains, shifts, ahead, back, n_t, n_dp, tiles):
+    R, D = tokens.shape
+    L = ahead.shape[1] // 2
+    W = L + R
+    own, inner, cols = w_query.shape[0], ff_bias.shape[1], gains.shape[1]
+    part = rel_table.shape[0] // n_t
+    n_all = n_t * n_dp
+    width = n_all * inner // tiles
+    PR = -(-(3 * eight(own) + eight(part) + 8) // 16) * 16
     bits = (n_dp // 2).bit_length() - 1
-    n_pack = n_t + bits
-    hbm = pl.BlockSpec(memory_space=pl.ANY)
+    low = bits // 2
+    S = jax.ShapeDtypeStruct
+    big = [(R, D), (L, D), (L, D), (NB, D), (NB, D), (W, D), (W, D), (n_t, R, D), (3, D, D), (NB, W), (NB, W), (NB, D)]
+    v = lambda s, t=bf: pltpu.VMEM(s, t)
+    dma = lambda *s: pltpu.SemaphoreType.DMA(s)
     return pl.pallas_call(
-        functools.partial(gather_kernel, n_t, n_dp),
-        out_shape=[jax.ShapeDtypeStruct((n_t, rows, D), bf), jax.ShapeDtypeStruct((n_t, n_dp // 2, 2, pr, D), bf)],
-        in_specs=[hbm, hbm], out_specs=[hbm, hbm],
-        scratch_shapes=[pltpu.SemaphoreType.DMA((2,)), pltpu.SemaphoreType.DMA((n_t - 1, 2)), pltpu.SemaphoreType.DMA((n_t - 1, 2)),
-                        pltpu.SemaphoreType.DMA((n_pack,)), pltpu.SemaphoreType.DMA((n_pack,))],
-        compiler_params=pltpu.CompilerParams(collective_id=0, has_side_effects=True),
-        name="gather_start",
-    )(tokens, pack)
-
-def reduce_kernel(n_t, n_dp, tok_ref, pack_ref, tok_out, pack_out, tok_got, tok_acc, first, acc, ring_got, ring_acc, *rest):
-    dp, t, high, core, bits, flips, right, left = places(n_t, n_dp)
-    halves, (tok_send, tok_recv, send, recv) = rest[:bits], rest[bits:]
-    peers = [{"tensor": right}, {"tensor": left}, {"dp": high * 2 + 1 - core}] + [{"dp": f * 2 + core} for f in flips]
-    meet(peers)
-    n_hi = n_dp // 2
-    pr = pack_ref.shape[3]
-    rows = tok_ref.shape[1]
-    piece = 64 if rows % 64 == 0 else rows
-    copies = {}
+        functools.partial(begin_kernel, n_t, n_dp, own, part, cols, inner, tiles, L),
+        out_shape=[S(s, bf) for s in big] + [S((tiles, 1, width), f32), S((2, D), f32), S((4, D), f32)],
+        in_specs=[VM] * 11, out_specs=[ANY] * len(big) + [VM] * 3,
+        scratch_shapes=[v((n_t, R, D)), v((n_t, 2**(bits - low), 2**low, 2, PR, D)), v((PR, D)), v((PR, D), f32), v((D, D), f32),
+                        v((3, D, D)), v((n_t, R, D)), v((n_t, R, D)), v((R, D)), v((NB, D)), v((NB, D)), v((W, D)), v((W, D)),
+                        v((NB, D), f32), v((NB, D)), v((2, n_all, D), f32), v((NB, W)), v((NB, W)),
+                        dma(n_t - 1, 2), dma(n_t - 1, 2), dma(n_t - 1), dma(n_t - 1), dma(2, bits + 1), dma(2, bits + 1),
+                        dma(10 + 3 * n_t)],
+        compiler_params=pltpu.CompilerParams(collective_id=0, has_side_effects=True, vmem_limit_bytes=58 * 1024 * 1024),
+        name="begin",
+    )(tokens, w_query, w_key, w_value, rel_table, qkv_bias, ff_bias, gains, shifts, ahead, back)
+
+def finish_kernel(n_t, n_dp, own, rel_rows, cols, inner, tiles,
+                  dq_in, dk_in, dv_in, tok_in, toks_in, w_in, table_in, dqr_in, dkr_in, dres_in, sums_ref, bsum_ref,
+                  tg_ref, gq_ref, gk_ref, gv_ref, rel_ref, qkvb_ref, ffb_ref, gains_ref, shifts_ref,
+                  dq, dk, dv, tok, toks, w, table, dqr, dkr, dres, g, relf, m0, m1, miscs, pack, first, acc, got, total,
+                  tok_got, tok_acc, tok_own, base, *rest):
+    at = Place(n_t, n_dp)
+    t = at.t
+    n_steps = len(at.steps)
+    bufs, (in_sem, tok_send, tok_recv, x_send, x_recv, z_send, z_recv) = rest[:2 * n_steps], rest[2 * n_steps:]
+    R, D = tok.shape
+    L = n_t * R
+    n_all = n_t * n_dp
+    S, S3 = eight(own), eight(rel_rows)
+    misc = 3 * S
+    PR = pack.shape[4]
+    right = {"tensor": lax.rem(t + 1, n_t)}
+    loads = []
+
+    def load(src, dst):
+        copy = pltpu.make_async_copy(src, dst, in_sem.at[len(loads)])
+        copy.start()
+        loads.append(copy)
+        return copy
 
     def block(s):
         return lax.rem(t - 1 - s + 2 * n_t, n_t)
 
+    l_w = load(w_in, w)
+    l_kv = []
+    for s in range(n_t):
+        b = block(s)
+        l_kv.append((load(dk_in.at[b], dk.at[b]), load(dv_in.at[b], dv.at[b])))
+    l_toks = load(toks_in, toks)
+    l_rest = [load(tok_in, tok), load(dq_in, dq), load(table_in, table), load(dqr_in, dqr), load(dkr_in, dkr), load(dres_in, dres)]
+    meet(at.peers())
+    copies = []
+
+    def go(copy):
+        copy.start()
+        copies.append(copy)
+        return copy
+
+    half = R // 2
+    token = {}
+
+    def partial(s):
+        for copy in l_kv[s]:
+            copy.wait()
+        b = block(s)
+        return dot_nn(dk[b], w[1]) + dot_nn(dv[b], w[2])
+
     def send_token(s):
-        src = tok_ref.at[block(0)] if s == 0 else tok_acc.at[s - 1]
-        copies["t", s] = remote(src, tok_got.at[s], tok_send.at[s], tok_recv.at[s], {"tensor": right})
-        copies["t", s].start()
-
-    def token_step(s):
-        def run():
-            copies["t", s - 1].wait_recv()
-            last = s == n_t - 1
-            b = t if last else block(s)
-
-            @pl.loop(0, rows // piece)
-            def _(i):
-                at = pl.ds(pl.multiple_of(i * piece, piece), piece)
-                total = tok_got[s - 1, at].astype(f32) + tok_ref[b, at].astype(f32)
-                if last:
-                    tok_out[at] = total
-                else:
-                    tok_acc[s - 1, at] = total.astype(bf)
-            if not last:
-                send_token(s)
-        return run
-
-    def start(k, src, dst, peer):
-        copies["p", k] = remote(src, dst, send.at[k], recv.at[k], peer)
-        copies["p", k].start()
-
-    def swap(k):
+        for j in range(2):
+            rows = pl.ds(j * half, half)
+            if s:
+                token[s - 1, j].wait_recv()
+                tok_acc[s, rows] = (tok_own[rows].astype(f32) + tok_got[s - 1, rows].astype(f32)).astype(bf)
+            token[s, j] = go(remote(tok_acc.at[s, rows], tok_got.at[s, rows], tok_send.at[s, j], tok_recv.at[s, j], right))
+
+    l_w.wait()
+    tok_acc[0] = partial(0).astype(bf)
+    send_token(0)
+    blocks = [None] * n_t
+    tok_own[...] = partial(1).astype(bf)
+
+    for s in range(2, n_t):
+        for copy in l_kv[s]:
+            copy.wait()
+    l_kv = [()] * n_t
+    l_toks.wait()
+    for copy in l_rest:
+        copy.wait()
+    dqb, dkb = dqr[...].astype(bf), dkr[...].astype(bf)
+    rel_table = table[...]
+    g[0] = dot_tn(dq[...], tok[...]) + dot_tn(dqb, rel_table)
+    g[1] = dot_tn(dk[...].reshape(L, D), toks[...].reshape(L, D)) + dot_tn(dkb, rel_table)
+    g[2] = dot_tn(dv[...].reshape(L, D), toks[...].reshape(L, D))
+    relf[...] = dot_nn(dqb, w[0]) + dot_nn(dkb, w[1])
+    ones = lambda n: jnp.ones((8, n), bf)
+    columns = [dot_nn(ones(R), dq[...])[0:1] + jnp.sum(dqr[...], axis=0, keepdims=True),
+               dot_nn(ones(L), dk[...].reshape(L, D))[0:1] + jnp.sum(dkr[...], axis=0, keepdims=True),
+               dot_nn(ones(L), dv[...].reshape(L, D))[0:1]]
+    for i in range(3):
+        m0[:, 128 * i:128 * i + 128] = fold_row(columns[i], own, n_all, 0)
+    units = jnp.zeros((n_all, 128), f32)
+    for i in range(tiles):
+        units += fold_row(bsum_ref[i], inner, n_all, i * (n_all // tiles))
+    m0[:, 384:512] = units
+    for i in range(6):
+        m1[:, 128 * i:128 * i + 128] = fold_row(sums_ref[i:i + 1, :], cols, n_dp, 0)
+    miscs[...] = jnp.zeros_like(miscs)
+    slots = [(a, u, d, c) for a in range(n_t) for u in range(2**at.high) for d in range(2**at.low) for c in range(2)]
+
+    def padded(x, n):
+        return jnp.concatenate([x, jnp.zeros((n - x.shape[0], D), f32)], axis=0) if n > x.shape[0] else x
+
+    for p, s in enumerate(slots):
+        dp = p % n_dp
+        miscs[8 * p:8 * p + 1, 0:512] = m0[p:p + 1, :]
+        miscs[8 * p + 1:8 * p + 2, :] = m1[dp:dp + 1, :]
+        pieces = [padded(g[i, p * own:p * own + own, :], S) for i in range(3)]
+        pieces += [miscs[8 * p:8 * p + 8, :], padded(relf[dp * rel_rows:dp * rel_rows + rel_rows, :], S3)]
+        whole = padded(jnp.concatenate(pieces, axis=0), PR)
+        pack[s[0], s[1], s[2], s[3]] = whole.astype(bf)
+
+    parts = at.parts()
+    hs = range(len(parts))
+    per = n_t // len(parts)
+    orders = [list(reversed(o)) for o in at.orders()][:len(parts)]
+    swaps = {}
+    left = {h: {"up": at.high, "down": at.low} for h in hs}
+
+    def region(h, cut=None):
+        out = []
+        for kind in ("up", "down"):
+            n = left[h][kind]
+            here = getattr(at, kind)
+            if cut is not None and cut[0] == kind:
+                start = (here // 2**n) * 2**n + (1 - at.bit(cut)) * 2**(n - 1)
+                out.append((start, 2**(n - 1)))
+            else:
+                out.append(((here // 2**n) * 2**n, 2**n))
+        return out
+
+    def start(h, k):
         if k == 0:
-            start(0, pack_ref.at[:, :, 1 - core], first, {"dp": high * 2 + 1 - core})
+            src, dst, peer = pack.at[parts[h], :, :, 1 - at.core], first.at[parts[h]], at.twin
         else:
-            i = bits - k
-            base = (high // 2**(i + 1)) * 2**(i + 1)
-            other = base + (1 - (high // 2**i) % 2) * 2**i
-            start(k, acc.at[:, pl.ds(other, 2**i)], halves[i], {"dp": flips[i] * 2 + core})
-
-    def add_swap(k):
-        copies["p", k].wait_recv()
-        if k == 0:
-            @pl.loop(0, n_t * n_hi)
-            def _(m):
-                a, b = m // n_hi, m % n_hi
-                acc[a, b] = (pack_ref[a, b, core].astype(f32) + first[a, b].astype(f32)).astype(bf)
-        else:
-            i = bits - k
-            keep = (high // 2**i) * 2**i
-
-            @pl.loop(0, n_t * 2**i)
-            def _(m):
-                a, b = m // 2**i, m % 2**i
-                acc[a, keep + b] = (acc[a, keep + b].astype(f32) + halves[i][a, b].astype(f32)).astype(bf)
-
-    def ring(s):
-        src = acc.at[block(0), high] if s == 0 else ring_acc.at[s - 1]
-        start(bits + 1 + s, src, ring_got.at[s], {"tensor": right})
-
-    def ring_add(s):
-        copies["p", bits + s].wait_recv()
-        last = s == n_t - 1
-        b = t if last else block(s)
-        total = ring_got[s - 1].astype(f32) + acc[b, high].astype(f32)
-        if last:
-            pack_out[...] = total
-        else:
-            ring_acc[s - 1] = total.astype(bf)
-
-    swap(0)
-    send_token(0)
-
-    def pack_step(k):
-        def run():
-            if k <= bits:
-                add_swap(k)
-                if k < bits:
-                    swap(k + 1)
-                else:
-                    ring(0)
+            cut = orders[h][k - 1]
+            up, down = [pl.ds(*x) for x in region(h, cut)]
+            src, dst, peer = acc.at[parts[h], up, down], bufs[h * n_steps + k - 1], at.peer(cut)
+        swaps[h, k] = go(remote(src, dst, x_send.at[h, k], x_recv.at[h, k], peer))
+
+    def absorb(h, k):
+        swaps[h, k].wait_recv()
+        if k:
+            left[h][orders[h][k - 1][0]] -= 1
+        (u0, nu), (d0, nd) = region(h)
+        buf = first if k == 0 else bufs[h * n_steps + k - 1]
+
+        @pl.loop(0, per * nu * nd)
+        def _(m):
+            a, u, d = m // (nu * nd), m // nd % nu, m % nd
+            if k == 0:
+                x, y = pack[h * per + a, u, d, at.core], buf[h * per + a, u, d]
             else:
-                s = k - bits
-                ring_add(s)
-                if s < n_t - 1:
-                    ring(s)
-        return run
-
-    for step in interleave([pack_step(k) for k in range(bits + n_t)], [lambda: None] + [token_step(s) for s in range(1, n_t)]):
-        step()
-    for copy in copies.values():
+                x, y = acc[h * per + a, u0 + u, d0 + d], buf[a, u, d]
+            acc[h * per + a, u0 + u, d0 + d] = (x.astype(f32) + y.astype(f32)).astype(bf)
+
+    for h in hs:
+        start(h, 0)
+    sent = 1
+    if n_t > 2:
+        send_token(1)
+        sent = 2
+        tok_own[...] = partial(2).astype(bf)
+    base[...] = partial(n_t - 1) + dres[...] + dot_nn(dq[...], w[0])
+    for k in range(n_steps + 1):
+        for h in hs:
+            absorb(h, k)
+            if k < n_steps:
+                start(h, k + 1)
+        if k == n_steps:
+            ring = [go(remote(acc.at[o, at.up, at.down], got.at[i], z_send.at[i], z_recv.at[i], {"tensor": o}))
+                    for i, o in enumerate(at.others)]
+        if k and sent < n_t - 1:
+            send_token(sent)
+            sent += 1
+            if sent < n_t - 1:
+                tok_own[...] = partial(sent).astype(bf)
+    for copy in ring:
+        copy.wait_recv()
+    total[...] = acc[t, at.up, at.down].astype(f32)
+    for i in range(n_t - 1):
+        total[...] += got[i].astype(f32)
+    for i, ref in enumerate((gq_ref, gk_ref, gv_ref)):
+        ref[...] = total[i * S:i * S + own, :]
+    rel_ref[...] = total[misc + 8:misc + 8 + rel_rows, :]
+    for i in range(3):
+        qkvb_ref[i:i + 1, :] = total[misc:misc + 1, 128 * i:128 * i + own]
+    ffb_ref[...] = total[misc:misc + 1, 384:384 + inner]
+    for i in range(2):
+        gains_ref[i:i + 1, :] = total[misc + 1:misc + 2, 128 * i:128 * i + cols]
+    for i in range(4):
+        shifts_ref[i:i + 1, :] = total[misc + 1:misc + 2, 256 + 128 * i:256 + 128 * i + cols]
+    while sent < n_t - 1:
+        send_token(sent)
+        sent += 1
+        if sent < n_t - 1:
+            tok_own[...] = partial(sent).astype(bf)
+    for j in range(2):
+        rows = pl.ds(j * half, half)
+        token[n_t - 2, j].wait_recv()
+        tg_ref[rows, :] = base[rows, :] + tok_got[n_t - 2, rows].astype(f32)
+    for copy in copies:
         copy.wait_send()
 
-def reduce_end(spread, pack, n_t, n_dp):
-    _, rows, D = spread.shape
-    pr = pack.shape[3]
-    n_hi = n_dp // 2
-    bits = n_hi.bit_length() - 1
-    n_pack = bits + n_t
-    vm = pl.BlockSpec(memory_space=pltpu.VMEM)
+def finish(dq, dk, dv, tok, toks, w, table, dqr, dkr, dres, sums, bsum, own, rel_rows, cols, inner, n_t, n_dp):
+    R, D = tok.shape
+    L = n_t * R
+    n_all = n_t * n_dp
+    tiles = bsum.shape[0]
+    S3 = eight(rel_rows)
+    PR = -(-(3 * eight(own) + 8 + S3) // 16) * 16
+    bits = (n_dp // 2).bit_length() - 1
+    low = bits // 2
+    high = bits - low
+    per = n_t // 2
+    v = lambda s, x=bf: pltpu.VMEM(s, x)
+    dma = lambda *s: pltpu.SemaphoreType.DMA(s)
+    bufs = []
+    for order in ([("up", high), ("down", low)], [("down", low), ("up", high)]):
+        left = {"up": high, "down": low}
+        for kind, n in order:
+            for _ in range(n):
+                left[kind] -= 1
+                bufs.append(v((per, 2**left["up"], 2**left["down"], PR, D)))
+    S = jax.ShapeDtypeStruct
+    outs = [(R, D), (own, D), (own, D), (own, D), (rel_rows, D), (3, own), (1, inner), (2, cols), (4, cols)]
+    blocks = lambda x: x.reshape(n_t, R, D)
     return pl.pallas_call(
-        functools.partial(reduce_kernel, n_t, n_dp),
-        out_shape=[jax.ShapeDtypeStruct((rows, D), f32), jax.ShapeDtypeStruct((pr, D), f32)],
-        in_specs=[vm, vm], out_specs=[vm, vm],
-        scratch_shapes=[pltpu.VMEM((n_t - 1, rows, D), bf), pltpu.VMEM((max(n_t - 2, 1), rows, D), bf),
-                        pltpu.VMEM((n_t, n_hi, pr, D), bf), pltpu.VMEM((n_t, n_hi, pr, D), bf),
-                        pltpu.VMEM((n_t - 1, pr, D), bf), pltpu.VMEM((max(n_t - 2, 1), pr, D), bf)]
-                       + [pltpu.VMEM((n_t, 2**i, pr, D), bf) for i in range(bits)]
-                       + [pltpu.SemaphoreType.DMA((n_t - 1,)), pltpu.SemaphoreType.DMA((n_t - 1,)),
-                          pltpu.SemaphoreType.DMA((n_pack,)), pltpu.SemaphoreType.DMA((n_pack,))],
-        compiler_params=pltpu.CompilerParams(collective_id=1, has_side_effects=True, vmem_limit_bytes=56 * 1024 * 1024),
-        name="reduce_end",
-    )(spread, pack)
+        functools.partial(finish_kernel, n_t, n_dp, own, rel_rows, cols, inner, tiles),
+        out_shape=[S(s, f32) for s in outs],
+        in_specs=[ANY] * 10 + [VM] * 2, out_specs=[VM] * len(outs),
+        scratch_shapes=[v((R, D)), v((n_t, R, D)), v((n_t, R, D)), v((R, D)), v((n_t, R, D)), v((3, D, D)), v((NB, D)),
+                        v((NB, D), f32), v((NB, D), f32), v((R, D), f32), v((3, D, D), f32), v((NB, D), f32),
+                        v((n_all, 512), f32), v((n_dp, D), f32), v((8 * n_all, D), f32),
+                        v((n_t, 2**high, 2**low, 2, PR, D)), v((n_t, 2**high, 2**low, PR, D)), v((n_t, 2**high, 2**low, PR, D)),
+                        v((n_t - 1, PR, D)), v((PR, D), f32),
+                        v((n_t - 1, R, D)), v((n_t - 1, R, D)), v((R, D)), v((R, D), f32)] + bufs
+                       + [dma(2 * n_t + 8), dma(n_t - 1, 2), dma(n_t - 1, 2), dma(2, bits + 1), dma(2, bits + 1), dma(n_t - 1), dma(n_t - 1)],
+        compiler_params=pltpu.CompilerParams(collective_id=1, has_side_effects=True, vmem_limit_bytes=60 * 1024 * 1024),
+        name="finish",
+    )(dq, blocks(dk), blocks(dv), tok, blocks(toks), w, table, dqr, dkr, dres, sums, bsum)
 
 GROUPS, TILES = 32, 4
 ALL=("tensor","dp")
 
-def project(inputs, weights, bias):
-    return (jnp.einsum("td,fd->tf", inputs, weights, preferred_element_type=f32) + bias).astype(bf)
+def finish_plain(dq, dk, dv, tok, toks, w, table, dqr, dkr, dres, sums, bsum, own, rel_rows, cols, inner, n_t, n_dp):
+    times = lambda s, a, b: jnp.einsum(s, a.astype(bf), b.astype(bf), preferred_element_type=f32)
+    scatter = lambda x: lax.psum_scatter(x, ALL, scatter_dimension=0, tiled=True)
+    grads = [times("tf,td->fd", dq, tok) + times("tf,td->fd", dqr, table),
+             times("tf,td->fd", dk, toks) + times("tf,td->fd", dkr, table), times("tf,td->fd", dv, toks)]
+    rel = times("bf,fd->bd", dqr, w[0]) + times("bf,fd->bd", dkr, w[1])
+    spread = (times("tf,fd->td", dk, w[1]) + times("tf,fd->td", dv, w[2])).astype(bf)
+    back_sum = lax.psum_scatter(spread, "tensor", scatter_dimension=0, tiled=True).astype(f32)
+    tokens_grad = dres + times("tf,fd->td", dq, w[0]) + back_sum
+    column = lambda x: jnp.sum(x.astype(f32), axis=0)
+    bias = jnp.stack([column(dq) + column(dqr), column(dk) + column(dkr), column(dv)])
+    every = lambda x: lax.psum(x, ALL)
+    dp = lax.axis_index("dp")
+    place = lax.axis_index("tensor") * n_dp + dp
+    cut = lambda x, i, n: lax.dynamic_slice_in_dim(x, i * n, n, 1)
+    rel = lax.dynamic_slice_in_dim(every(rel), dp * rel_rows, rel_rows, 0)
+    return [tokens_grad] + [scatter(x) for x in grads] + [rel, cut(every(bias), place, own), cut(every(bsum.reshape(1, -1)), place, inner),
+            cut(every(sums[:2]), dp, cols), cut(every(sums[2:6]), dp, cols)]
 
 def local(tokens, w_query, w_key, w_value, w_out, qkv_bias, w_ff_in, w_ff_out, ff_bias, rel_table,
           gains, shifts, rel_bucket, lengths, out_grad):
@@ -590,29 +877,21 @@
     R = tokens.shape[0]
     L = (rel_bucket.shape[0] + 1) // 2
     W = L + R
-    part = rel_table.shape[0] // n_t
-    wide, inner, cols = qkv_bias.shape[1], ff_bias.shape[0], gains.shape[1]
-    misc = jnp.concatenate([qkv_bias.reshape(-1), ff_bias, gains.reshape(-1), shifts.reshape(-1)])
-    used = misc.shape[0]
-    misc = jnp.pad(misc, (0, D - used))[None]
-    rel_part = lax.dynamic_slice_in_dim(rel_table, t * part, part, 0)
-    small = jnp.concatenate([rel_part, misc], axis=0)
-    early = jnp.concatenate([w_query, w_key, w_value, small], axis=0)
-    own_rows = w_query.shape[0]
+    own_rows, cols, inner = w_query.shape[0], gains.shape[1], ff_bias.shape[0]
+    none = jnp.full((1,), -1, jnp.int32)
+    ahead = jnp.concatenate([rel_bucket, none])[None]
+    back = jnp.concatenate([rel_bucket[::-1], none])[None]
+    (query, key, value, key_rel, query_rel, key_table, query_table, gathered, weights, pick_x, pick_y, table,
+     inner_bias, gain, shift) = begin(tokens, w_query, w_key, w_value, rel_table, qkv_bias, ff_bias.reshape(1, -1), gains, shifts,
+                                      ahead, back, n_t, n_dp, TILES)
+    gathered = gathered.reshape(L, D)
     late_rows = w_ff_in.shape[0]
-    early_rows = early.shape[0]
-    early = jnp.pad(early, ((0, -early_rows % 16), (0, 0)))
     even = late_rows % 16 == 0 and own_rows % 8 == 0
     late = jnp.concatenate([w_ff_in, w_ff_out, w_out], axis=0)
     late_own = late.shape[0]
     late = jnp.pad(late, ((0, -late_own % 16), (0, 0)))
-    gathered, early_all = gather_start(tokens, early, n_t, n_dp)
     late_all = lax.all_gather(late, ALL, axis=0, tiled=False)
-    gathered = gathered.reshape(L, D)
-    early_all = early_all.reshape(n_all, early.shape[0], D)
     cut = lambda x, at, n: x[:, at:at + n].reshape(n_all * n, D)
-    query_rows, key_rows, value_rows = [cut(early_all, i * own_rows, own_rows) for i in range(3)]
-    small_all = early_all[:, 3 * own_rows:early_rows]
     out_rows = cut(late_all, 2 * late_rows, own_rows)
     groups = n_all if even else GROUPS
     group_rows, group_own = n_all * late_rows // groups, D // groups
@@ -620,39 +899,12 @@
         sections = [cut(late_all, 0, late_rows), cut(late_all, late_rows, late_rows)]
         late_all = jnp.concatenate([x.reshape(groups, group_rows, D) for x in sections]
                                    + [jnp.zeros((groups, -(-group_own // 16) * 16, D), bf)], axis=1)
-    misc_all = small_all[:, part]
-    o1 = 3 * wide
-    o2 = o1 + inner
-    o3 = o2 + 2 * cols
-    bias = misc_all[:, :o1].reshape(n_all, 3, wide).transpose(1, 0, 2).reshape(3, D).astype(f32)
-    inner_bias = misc_all[:, o1:o2].reshape(-1).astype(f32)
-    first = misc_all[:n_dp]
-    gain = first[:, o2:o3].reshape(n_dp, 2, cols).transpose(1, 0, 2).reshape(2, D).astype(f32)
-    shift = first[:, o3:used].reshape(n_dp, 4, cols).transpose(1, 0, 2).reshape(4, D).astype(f32)
-    table = small_all[:, :part].reshape(n_t, n_dp, part, D).transpose(1, 0, 2, 3).reshape(NB, D)
-
-    query = project(tokens, query_rows, bias[0])
-    key = project(gathered, key_rows, bias[1])
-    value = project(gathered, value_rows, bias[2])
-    key_rel = project(table, key_rows, bias[1])
-    query_rel = project(table, query_rows, bias[0])
-
-    none = jnp.full((1,), -1, jnp.int32)
-    ahead = jnp.concatenate([rel_bucket, none])
-    back = jnp.concatenate([rel_bucket[::-1], none])
-    buckets = jnp.arange(NB, dtype=jnp.int32)[None, :]
-    pick = lambda line, start: (lax.dynamic_slice_in_dim(line, start, W, 0)[:, None] == buckets).astype(bf)
-    pick_x = pick(back, L - R - R * t)
-    pick_y = pick(ahead, L - R - R * t)
-    pick_u = pick(back, R * t)
-    key_table = jnp.dot(pick_x, key_rel, preferred_element_type=f32).astype(bf)
-    query_table = jnp.dot(pick_u, query_rel, preferred_element_type=f32).astype(bf)
     mask = jnp.where(jnp.arange(L, dtype=jnp.int32) < lengths[0], 0.0, -1e9).astype(bf)
     mask = jnp.broadcast_to(mask[:, None], (L, 128))
 
     context, scale, shares = attention_forward(query, key, value, key_table, query_table, mask)
     layer_result_rows, d_resid_one, d_scaled, sums, bias_sums, late_grad = feed(
-        context, tokens, out_grad, scale, out_rows, late_all, inner_bias.reshape(TILES, 1, -1), gain, shift, group_rows, group_own)
+        context, tokens, out_grad, scale, out_rows, late_all, inner_bias, gain, shift, group_rows, group_own)
     d_query, d_key, d_value, d_key_rel, d_query_rel = attention_backward(
         query, key, value, d_scaled, context, shares, key_rel, query_rel, pick_x, pick_y)
 
@@ -664,40 +916,12 @@
             jnp.zeros((n_all, late.shape[0] - late_own, D), bf)], axis=1)
     late_sum = lax.psum_scatter(late_grad, ALL, scatter_dimension=0, tiled=True)[0].astype(f32)
     g_inner, g_outer, g_out = late_sum[:late_rows], late_sum[late_rows:2 * late_rows], late_sum[2 * late_rows:late_own]
-    dqr, dkr = d_query_rel.astype(bf), d_key_rel.astype(bf)
-    grad_query = jnp.einsum("tf,td->fd", d_query, tokens, preferred_element_type=f32) + jnp.einsum(
-        "tf,td->fd", dqr, table, preferred_element_type=f32)
-    grad_key = jnp.einsum("tf,td->fd", d_key, gathered, preferred_element_type=f32) + jnp.einsum(
-        "tf,td->fd", dkr, table, preferred_element_type=f32)
-    grad_value = jnp.einsum("tf,td->fd", d_value, gathered, preferred_element_type=f32)
-    bias_gradient = jnp.stack([
-        jnp.sum(d_query.astype(f32), axis=0) + jnp.sum(d_query_rel, axis=0),
-        jnp.sum(d_key.astype(f32), axis=0) + jnp.sum(d_key_rel, axis=0),
-        jnp.sum(d_value.astype(f32), axis=0)])
-    d_rel = jnp.dot(dqr, query_rows, preferred_element_type=f32) + jnp.dot(dkr, key_rows, preferred_element_type=f32)
-    own = jnp.dot(d_query, query_rows, preferred_element_type=f32)
-    spread = (jnp.dot(d_key, key_rows, preferred_element_type=f32)
-              + jnp.dot(d_value, value_rows, preferred_element_type=f32)).astype(bf)
-    shape_dp = lambda x, k: jnp.broadcast_to(
-        x.reshape(k, n_dp, cols).transpose(1, 0, 2).reshape(1, n_dp, k * cols), (n_t, n_dp, k * cols)).reshape(n_all, k * cols)
-    line = jnp.concatenate([
-        bias_gradient.reshape(3, n_all, wide).transpose(1, 0, 2).reshape(n_all, o1),
-        bias_sums.reshape(n_all, inner),
-        shape_dp(sums[:2], 2), shape_dp(sums[2:6], 4)], axis=1)
-    line = jnp.pad(line[:, None], ((0, 0), (0, 7), (0, D - used)))
+    ends = (d_query, d_key, d_value, tokens, gathered, weights, table, d_query_rel, d_key_rel, d_resid_one, sums, bias_sums)
     rel_rows = rel_table.shape[0]
-    d_rel_all = jnp.broadcast_to(d_rel.reshape(1, n_dp, rel_rows, D), (n_t, n_dp, rel_rows, D)).reshape(n_all, rel_rows, D)
-    early_grad = jnp.concatenate([parted(grad_query), parted(grad_key), parted(grad_value), line.astype(bf), d_rel_all.astype(bf)], axis=1)
-    end_rows = early_grad.shape[1]
-    early_grad = jnp.pad(early_grad, ((0, 0), (0, -end_rows % 16), (0, 0)))
-    back_sum, early_sum = reduce_end(spread.reshape(n_t, R, D), early_grad.reshape(n_t, n_dp // 2, 2, -1, D), n_t, n_dp)
-    tokens_grad = d_resid_one + own + back_sum
-    g_query, g_key, g_value = [early_sum[i * own_rows:(i + 1) * own_rows] for i in range(3)]
-    row = early_sum[3 * own_rows]
-    g_rel = early_sum[3 * own_rows + 8:end_rows]
+    finished = (finish if even else finish_plain)(*ends, own_rows, rel_rows, cols, inner, n_t, n_dp)
+    tokens_grad, g_query, g_key, g_value, g_rel, g_qkv_bias, g_ff_bias, g_gains, g_shifts = finished
     return (layer_result_rows, tokens_grad, g_query, g_key, g_value, g_out,
-            row[:o1].reshape(3, wide), g_inner, g_outer, row[o1:o2], g_rel,
-            row[o2:o3].reshape(2, cols), row[o3:used].reshape(4, cols))
+            g_qkv_bias, g_inner, g_outer, g_ff_bias.reshape(inner), g_rel, g_gains, g_shifts)
 
 def solution(mesh):
     rows, params = P(("dp", "tensor"), None), P(ALL, None)

time: 520 us -> 522 us (level)
  Pallas kernels: 394 us -> 476 us
  matrix products: 35.3 us -> 0 us
  local copies, waits for them, and re-layouts: 50.3 us -> 18.6 us
  other arithmetic: 15.9 us -> 4.31 us
    pallas_call x2, Pallas kernels: 198 us -> 245 us  [the longest x1 155 us: begin(): pl.pallas_call(functools.partial(begin_kernel, n_t, n_dp, own, part, cols...]
    dot_general x17 -> x0, matrix products: 35.3 us -> none  [the longest x5 9.79 us: project(): jnp.einsum('td,fd->tf', inputs, weights, preferred_element_type=f32) + bias]
    pallas_call x1, Pallas kernels: 88.2 us -> 122 us  [attention_backward(): pl.pallas_call(functools.partial(bwd_kernel, R, L, B, C), grid=(pairs, 2)...]
    slice x15 -> x0, local copies, waits for them, and re-layouts: 12.6 us -> none  [the longest x1 1.64 us: local(): early_sum[i * own_rows:(i + 1) * own_rows]]
    reshape x10 -> x0, local copies, waits for them, and re-layouts: 7.11 us -> none  [the longest x1 1.4 us: local(): bias_gradient.reshape(3, n_all, wide).transpose(1, 0, 2).reshape(n_all, o1)]
    reduce_sum x5 -> x0, other arithmetic: 5.82 us -> none  [the longest x1 2.99 us: local(): jnp.sum(d_value.astype(f32), axis=0)]
    unnamed x53 -> x51, local copies, waits for them, and re-layouts: 12.7 us -> 14.4 us
  transfers between devices with their start and end apart: 2 -> 2, of which waited for: 0 -> 0; matrix products, arithmetic and copies ran while one was open for 18% -> 1% of each run, Pallas kernels for 69% -> 84%
where the time goes in v4:
time: 522 us; the launch traced here: 514 us
  Pallas kernels  476 us (91%)
  local copies, waits for them, and re-layouts  18.6 us (4%)
  between operations  15.3 us (3%)
    pallas_call x1, Pallas kernels, begin(): pl.pallas_call(functools.partial(begin_kernel, n_t, n_dp, own, part, cols...  155 us
    pallas_call x1, Pallas kernels, attention_backward(): pl.pallas_call(functools.partial(bwd_kernel, R, L, B, C), grid=(pairs, 2)...  122 us
    pallas_call x1, Pallas kernels, finish(): pl.pallas_call(functools.partial(finish_kernel, n_t, n_dp, own, rel_rows,...  90.5 us
    pallas_call x1, Pallas kernels, attention_forward(): pl.pallas_call(functools.partial(fwd_kernel, R, L, B, C), grid=(pairs, 2)...  64.5 us
    pallas_call x1, Pallas kernels, feed(): pl.pallas_call(functools.partial(feed_kernel, R, D, tiles, per, rows_in,...  43.8 us
    unnamed x51, local copies, waits for them, and re-layouts  14.4 us
  transfers between devices with their start and end apart: 2, of which 0 were waited for; matrix products, arithmetic and copies ran while one was open for 1% of the time, Pallas kernels for 84%

profile of v4, /device:TPU:13, one launch (start us, length us, event | category | flops | bytes accessed | tf_op | source)
XLA Modules:
  0.0 514.4 jit_solution(16595204352930045260)
XLA Ops:
  7.2 0.0 all-gather.3.cloned.1.call-start
  7.2 1.8 fusion.4
  9.0 0.0 all-gather.3.cloned.1.call-update
  9.0 0.0 reduce-scatter.2.cloned.1.call-start
  9.7 0.8 reverse
  10.5 0.1 slice.35
  10.6 1.4 pad_add_fusion
  12.0 154.9 %begin.1 = (bf16[512,768]{1,0:T(8,128)(2,1)}, bf16[2048,768]{1,0:T(8,128)(2,1)}, bf16[2048,768]{1,0:T(8,128)(2,1)}, bf16[256,768]{1,0:T(8,128)(2,1)}, bf16[256,7...) custom-call(bf16[512,768]{1,0:T(8,128)(2,1)} %tok_in.1, ...), custom_call_target="tpu_custom_call" | custom-call | tf_op jit(solution)/shard_map/begin/pallas_call | solution.py:601
  166.9 0.3 broadcast_in_dim.22.mask_ref
  167.3 0.0 copy-start.3
  167.3 1.1 copy-done.3
  168.4 64.5 %attend.1 = (bf16[512,768]{1,0:T(8,128)(2,1)S(1)}, f32[512,768]{1,0:T(8,128)S(1)}, bf16[12,512,2048]{2,1,0:T(8,128)(2,1)}) custom-call(bf16[2048,128]{1,0:T(8,128)(2,1)S(1)} %broadcast_in_dim.22.mask_ref, bf16[512,768]{1,0:T(8,128)(2,1)S(1)} %copy-done.3, bf16[2048,768]{1,0:T(8,128)(2,1)} %get-tuple-element.52.k_ref, ...), custom_call_target="tpu_custom_call" | custom-call | flops 12884901888 | bytes 40894464 | tf_op jit(solution)/shard_map/attend/pallas_call | solution.py:111
  232.9 1.1 copy-done.7
  234.1 0.9 copy-done.8
  234.9 2.4 slice.28
  237.3 43.8 %feed.1 = (bf16[512,768]{1,0:T(8,128)(2,1)}, f32[512,768]{1,0:T(8,128)}, bf16[512,768]{1,0:T(8,128)(2,1)}, f32[8,768]{1,0:T(8,128)}, f32[4,1,768]{2,1,0:T(1,128)}, /*index=5*/bf16[32,224,768]{2,1,0:T(8,128)(2,1)}) custom-call(bf16[512,768]{1,0:T(8,128)(2,1)} %copy-done.8, bf16[512,768]{1,0:T(8,128)(2,1)} %tok_in.1, bf16[512,768]{1,0:T(8,128)(2,1)} %og_ref.1, ...), custom_call_target="tpu_custom_call" | custom-call | flops 16307453952 | bytes 29884416 | tf_op jit(solution)/shard_map/feed/pallas_call | solution.py:325
  281.1 0.0 copy-start.4
  281.1 0.0 copy-start.5
  281.1 0.0 copy-start.6
  281.2 0.0 copy-start.9
  281.2 0.0 copy-start.10
  281.2 0.0 reduce-scatter.2.cloned.1.call-update
  281.2 1.1 copy-done.4
  282.3 0.1 copy-done.5
  282.4 0.1 copy-done.6
  282.5 0.3 copy-done.9
  282.7 0.2 copy-done.10
  283.0 122.2 %attend_back.1 = (bf16[512,768]{1,0:T(8,128)(2,1)S(1)}, bf16[2048,768]{1,0:T(8,128)(2,1)}, bf16[2048,768]{1,0:T(8,128)(2,1)}, f32[256,768]{1,0:T(8,128)S(1)}, f32[256,768]{1,0:T(8,128)S(1)}) custom-call(bf16[512,768]{1,0:T(8,128)(2,1)S(1)} %copy-done.4, bf16[2048,768]{1,0:T(8,128)(2,1)} %get-tuple-element.52.k_ref, ...), custom_call_target="tpu_custom_call" | custom-call | flops 25769803776 | bytes 56623104 | tf_op jit(solution)/shard_map/attend_back/pallas_call | solution.py:185
  405.2 0.0 copy-start
  405.2 0.9 copy-done
  406.1 0.9 copy-done.1
  407.0 0.9 copy-done.2
  407.8 90.5 %finish.1 = (f32[512,768]{1,0:T(8,128)}, f32[24,768]{1,0:T(8,128)}, f32[24,768]{1,0:T(8,128)}, f32[24,768]{1,0:T(8,128)}, f32[32,768]{1,0:T(8,128)}, /*index=5*/...) custom-call(bf16[512,768]{1,0:T(8,128)(2,1)} %copy-done, bf16[4,512,768]{2,1,0:T(8,128)(2,1)} %bitcast.17, ...), custom_call_target="tpu_custom_call" | custom-call | tf_op jit(solution)/shard_map/finish/pallas_call | solution.py:834
  498.4 0.0 copy-start.11
  498.4 0.0 copy-start.15
  498.4 0.0 copy-start.14
  498.4 0.0 copy-start.13
  498.4 0.0 copy-start.17
  498.4 0.0 copy-start.19
  498.5 0.0 copy-start.12
  498.5 0.0 copy-start.18
  498.5 0.0 copy-start.16
  498.5 0.0 reduce-scatter.2.cloned.1.call-done
  498.5 1.1 convert_element_type.14
  499.7 0.6 slice_bitcast_fusion.2
  500.3 0.8 slice_bitcast_fusion
  501.1 0.0 copy-done.11
  501.1 1.1 copy.38
  502.3 0.0 copy-done.15
  502.3 0.6 copy.39
  502.9 0.0 copy-done.14
  502.9 0.6 copy.40
  503.6 0.0 copy-done.13
  503.6 0.6 copy.41
  504.2 0.0 copy-done.17
  504.2 0.6 copy.42
  504.8 0.0 copy-done.19
  504.8 0.5 copy.43
  505.3 0.0 copy-done.12
  505.3 0.6 copy.44
  505.9 0.0 copy-done.18
  505.9 0.6 copy.45
  506.5 0.0 copy-done.16
  506.5 0.6 copy.46
  (6 shorter events, 0.0 us)
Async XLA Ops:
  7.2 227.8 %all-gather.3.cloned.1.call-start = ((), (), s32[]{:S(2)}) async-start(), calls=%async_computation.2 | async-start | bytes 11354112 | tf_op jit(solution)/shard_map/all_gather | solution.py:893
  9.0 489.5 %reduce-scatter.2.cloned.1.call-start = ((), (), s32[]{:S(2)}) async-start(), calls=%async_computation.1 | async-start | bytes 11354112 | tf_op jit(solution)/shard_map/reduce_scatter | solution.py:917
  167.3 1.1 copy-start.3
  232.9 1.1 copy-start.7
  234.1 0.9 copy-start.8
  281.1 1.1 copy-start.4
  281.1 1.2 copy-start.5
  281.1 1.3 copy-start.6
  281.2 1.6 copy-start.9
  281.2 1.8 copy-start.10
  405.2 0.9 copy-start
  406.1 0.9 copy-start.1
  407.0 0.9 copy-start.2
  498.4 2.8 copy-start.11
  498.4 3.9 copy-start.15
  498.4 4.5 copy-start.14
  498.4 5.1 copy-start.13
  498.4 5.8 %copy-start.17 = (f32[3,24]{1,0:T(4,128)S(1)}, f32[3,24]{1,0:T(4,128)}, u32[]{:S(2)}) copy-start(f32[3,24]{1,0:T(4,128)} %get-tuple-element.112) | copy-start | bytes 868
  498.4 6.3 %copy-start.19 = (f32[1,96]{1,0:T(1,128)S(1)}, f32[1,96]{1,0:T(1,128)}, u32[]{:S(2)}) copy-start(f32[1,96]{1,0:T(1,128)} %get-tuple-element.85) | copy-start | bytes 1156
  498.5 6.8 %copy-start.12 = (f32[32,768]{1,0:T(8,128)S(1)}, f32[32,768]{1,0:T(8,128)}, u32[]{:S(2)}) copy-start(f32[32,768]{1,0:T(8,128)} %get-tuple-element.116) | copy-start | bytes 294916
  498.5 7.5 %copy-start.18 = (f32[2,96]{1,0:T(2,128)S(1)}, f32[2,96]{1,0:T(2,128)}, u32[]{:S(2)}) copy-start(f32[2,96]{1,0:T(2,128)} %get-tuple-element.117) | copy-start | bytes 2308
  498.5 8.0 %copy-start.16 = (f32[4,96]{1,0:T(4,128)S(1)}, f32[4,96]{1,0:T(4,128)}, u32[]{:S(2)}) copy-start(f32[4,96]{1,0:T(4,128)} %get-tuple-element.118) | copy-start | bytes 4612
Sparse Core Ops, SparseCore 0:
  11.5 157.9 all-gather.2
  281.3 154.7 reduce-scatter.1

commit v5 on v4

--- a/solution.py
+++ b/solution.py
@@ -152,7 +152,7 @@
             ds_ref[at,:]=ds
             part=jnp.concatenate([ds,jnp.zeros((16,B),bf)],axis=1)
             wide[rows,:]=pltpu.roll(part,16*g,1,stride=1,stride_axis=0)
-        db=dot_nt(wide[...],ox_ref[:,r0:r0+L+B]).astype(bf)
+        db=dot_nn(wide[...],ox_ref[r0:r0+L+B,:]).astype(bf)
         dq=dot_nn(ds_ref[r0:r0+B,:],k_ref[...])+dot_nn(db,kr_ref[...])
         dqa_ref[r0:r0+B,:]=jnp.where(own,dq,dqa_ref[r0:r0+B,:])
         dkr_ref[...]+=dot_tn(db,qrev_ref[r0:r0+B,:])
@@ -166,7 +166,7 @@
             rows=slice(16*g,16*g+16)
             part=jnp.concatenate([dst[rows,:],jnp.zeros((16,C),bf)],axis=1)
             wide[rows,:]=pltpu.roll(part,16*g,1,stride=1,stride_axis=0)
-        db=dot_nt(wide[...],oy_ref[:,i*C:i*C+R+C]).astype(bf)
+        db=dot_nn(wide[...],oy_ref[i*C:i*C+R+C,:]).astype(bf)
         dka_ref[at,:]+=dot_nn(dst[...],qrev_ref[...])+dot_nn(db,qrel)
         dva_ref[at,:]+=dot_tn(e_ref[0,:,at],dor_ref[...])
         kb=jnp.where(ownk,k_ref[at,:],zero)
@@ -177,24 +177,37 @@
         dk_ref[...]=dka_ref[...].astype(bf)
         dv_ref[...]=(dva_ref[...]*(1.0/SCALE)).astype(bf)
 
-def attention_backward(q,k,v,do,ctx,e,key_rel,query_rel,onehot_x,onehot_y,B=128,C=128):
+def attention_backward(q,k,v,do,ctx,e,key_rel,query_rel,onehot_x,onehot_y,p0=0,count=None,before=None,after=None,through=None,B=128,C=128):
     R,F=q.shape; L=k.shape[0]; W=L+R; pairs=F//128
-    col=lambda n: pl.BlockSpec((n,128),lambda p,h:(0,p))
-    full=pl.BlockSpec((NB,W),lambda p,h:(0,0))
-    flops=2*pairs*2*R*L*128*8
-    return pl.pallas_call(functools.partial(bwd_kernel,R,L,B,C),
-        grid=(pairs,2),
-        in_specs=[col(R),col(L),col(L),col(R),col(R),pl.BlockSpec((1,R,L),lambda p,h:(2*p+h,0,0)),col(NB),col(NB),full,full],
-        out_specs=[col(R),col(L),col(L),col(NB),col(NB)],
+    count=pairs if count is None else count
+    B=min(B,R)
+    col=lambda n: pl.BlockSpec((n,128),lambda p,h:(0,p0+p))
+    full=pl.BlockSpec((W,NB),lambda p,h:(0,0))
+    flops=2*count*2*R*L*128*8
+    args=[q,k,v,do,ctx,e,key_rel,query_rel,onehot_x,onehot_y]
+    specs=[col(R),col(L),col(L),col(R),col(R),pl.BlockSpec((1,R,L),lambda p,h:(2*(p0+p)+h,0,0)),col(NB),col(NB),full,full]
+    n_in=len(args)
+    through=list(through or [])
+    extra=list(before or [])+through+list(after or [])
+    n_before=len(before or [])
+    body=functools.partial(bwd_kernel,R,L,B,C)
+    def kernel(*refs):
+        rest=refs[n_in+len(extra):]
+        body(*refs[:n_in],*rest[:5],*rest[5+len(through):])
+    return pl.pallas_call(kernel,
+        grid=(count,2),
+        in_specs=specs+[pl.BlockSpec(memory_space=pl.ANY)]*len(extra),
+        out_specs=[col(R),col(L),col(L),col(NB),col(NB)]+[pl.BlockSpec(memory_space=pl.ANY)]*len(through),
         out_shape=[jax.ShapeDtypeStruct((R,F),bf),jax.ShapeDtypeStruct((L,F),bf),jax.ShapeDtypeStruct((L,F),bf),
-                   jax.ShapeDtypeStruct((NB,F),f32),jax.ShapeDtypeStruct((NB,F),f32)],
+                   jax.ShapeDtypeStruct((NB,F),f32),jax.ShapeDtypeStruct((NB,F),f32)]+[jax.ShapeDtypeStruct(x.shape,x.dtype) for x in through],
+        input_output_aliases={**({n_in+i:i for i in range(5)} if before else {}),**{n_in+n_before+i:5+i for i in range(len(through))}},
         scratch_shapes=[pltpu.VMEM((R,L),bf),pltpu.VMEM((R,128),bf),pltpu.VMEM((R,128),bf),
                         pltpu.VMEM((R,128),f32),pltpu.VMEM((L,128),f32),pltpu.VMEM((L,128),f32),
                         pltpu.VMEM((R,128),f32),pltpu.VMEM((2,B,L),f32),pltpu.VMEM((2,B,L+B),bf),pltpu.VMEM((2,C,R),bf),pltpu.VMEM((2,C,R+C),bf)],
         compiler_params=pltpu.CompilerParams(vmem_limit_bytes=48*1024*1024,dimension_semantics=("arbitrary","arbitrary")),
-        cost_estimate=pl.CostEstimate(flops=flops,bytes_accessed=2*pairs*R*L*2+20*L*F,transcendentals=0),
+        cost_estimate=pl.CostEstimate(flops=flops,bytes_accessed=2*count*R*L*2+20*L*128*count,transcendentals=0),
         name="attend_back",
-    )(q,k,v,do,ctx,e,key_rel,query_rel,onehot_x,onehot_y)
+    )(*args,*extra)
 
 EPS=1e-6
 
@@ -207,10 +220,24 @@
     phi=jnp.where(v>0,1.0-tail,tail)
     return v*phi, phi+v*bell*(1.0/math.sqrt(2.0*math.pi))
 
+class Both:
+    def __init__(self,*copies):
+        self.copies=copies
+
+    def start(self):
+        for copy in self.copies:
+            copy.start()
+
+    def wait(self):
+        for copy in self.copies:
+            copy.wait()
+
 def feed_kernel(R,D,tiles,per,rows_in,own_rows,ctx_ref,tok_ref,og_ref,scale_ref,wo_ref,late_ref,bias_ref,gain_ref,shift_ref,
-                res_ref,dres_ref,do_ref,sums_ref,bsum_ref,grad_ref,
+                res_ref,dres_ref,do_ref,sums_ref,bsum_ref,keep_ref,give_ref,
                 u1_ref,r1_ref,low_ref,acc_ref,pre_ref,gated_ref,gp_ref,dfeed_ref,stage_ref,tail_ref,datt_ref,sem):
     step=pl.program_id(0)
+    core=lax.axis_index("dp")%2
+    pairs=per//2
     width=per*rows_in
     CH=64
     def chunks(f):
@@ -277,12 +304,14 @@
         chunks(act)
         bsum_ref[0]=jnp.sum(gp_ref[k].astype(f32),axis=0,keepdims=True)
         def out(kk,s):
-            return pltpu.make_async_copy(stage_ref.at[s],grad_ref.at[pl.ds(kk*per,per),pl.ds(0,2*rows_in)],sem.at[s])
+            to=(pl.ds(kk*pairs,pairs),pl.ds(0,2*rows_in))
+            return Both(pltpu.make_async_copy(stage_ref.at[s,:,core],keep_ref.at[to],sem.at[s,0]),
+                        pltpu.make_async_copy(stage_ref.at[s,:,1-core],give_ref.at[to],sem.at[s,1]))
         @pl.when(k>=2)
         def _():
             out(k-2,slot).wait()
-        stage_ref[slot,:,0:rows_in,:]=dot_tn(gp_ref[k],low_ref[...]).astype(bf).reshape(per,rows_in,D)
-        stage_ref[slot,:,rows_in:2*rows_in,:]=dot_tn(gated_ref[k],dfeed_ref[...]).astype(bf).reshape(per,rows_in,D)
+        stage_ref[slot,:,:,0:rows_in,:]=dot_tn(gp_ref[k],low_ref[...]).astype(bf).reshape(pairs,2,rows_in,D)
+        stage_ref[slot,:,:,rows_in:2*rows_in,:]=dot_tn(gated_ref[k],dfeed_ref[...]).astype(bf).reshape(pairs,2,rows_in,D)
         out(k,slot).start()
         acc_ref[...]+=dot_nn(gp_ref[k],w_in)
         @pl.when(k==tiles-1)
@@ -302,13 +331,15 @@
             do_ref[...]=(dot_nt(datt_ref[...],wo_ref[...])*scale_ref[...]).astype(bf)
             outer=dot_tn(ctx_ref[...],datt_ref[...])
             n=D//own_rows
-            gap=tail_ref.shape[1]-own_rows
+            gap=tail_ref.shape[2]-own_rows
             for p in range(n):
                 piece=outer[p*own_rows:p*own_rows+own_rows,:]
                 if gap:
                     piece=jnp.concatenate([piece,jnp.zeros((gap,D),f32)],axis=0)
-                tail_ref[p]=piece.astype(bf)
-            last=pltpu.make_async_copy(tail_ref,grad_ref.at[:,pl.ds(2*rows_in,tail_ref.shape[1])],sem.at[2])
+                tail_ref[p//2,p%2]=piece.astype(bf)
+            to=(slice(None),pl.ds(2*rows_in,tail_ref.shape[2]))
+            last=Both(pltpu.make_async_copy(tail_ref.at[:,core],keep_ref.at[to],sem.at[2,0]),
+                      pltpu.make_async_copy(tail_ref.at[:,1-core],give_ref.at[to],sem.at[2,1]))
             last.start()
             if tiles>1:
                 out(k-1,1-slot).wait()
@@ -328,14 +359,14 @@
                   pl.BlockSpec((per,rows_late,D),lambda i:(lax.rem(i,tiles),0,0)),
                   pl.BlockSpec((1,1,width),lambda i:(lax.rem(i,tiles),0,0)),vm((2,D)),vm((4,D))],
         out_specs=[vm((R,D)),vm((R,D)),vm((R,D)),vm((8,D)),pl.BlockSpec((1,1,width),lambda i:(jnp.maximum(i-tiles,0),0,0)),
-                   pl.BlockSpec(memory_space=pl.ANY)],
+                   pl.BlockSpec(memory_space=pl.ANY),pl.BlockSpec(memory_space=pl.ANY)],
         out_shape=[jax.ShapeDtypeStruct((R,D),bf),jax.ShapeDtypeStruct((R,D),f32),jax.ShapeDtypeStruct((R,D),bf),
                    jax.ShapeDtypeStruct((8,D),f32),jax.ShapeDtypeStruct((tiles,1,width),f32),
-                   jax.ShapeDtypeStruct((n,rows_late,D),bf)],
+                   jax.ShapeDtypeStruct((n//2,rows_late,D),bf),jax.ShapeDtypeStruct((n//2,rows_late,D),bf)],
         scratch_shapes=[pltpu.VMEM((R,D),f32),pltpu.VMEM((R,128),f32),pltpu.VMEM((R,D),bf),pltpu.VMEM((R,D),f32),
                         pltpu.VMEM((R,width),f32),pltpu.VMEM((tiles,R,width),bf),pltpu.VMEM((tiles,R,width),bf),
-                        pltpu.VMEM((R,D),bf),pltpu.VMEM((2,per,2*rows_in,D),bf),pltpu.VMEM((n,tail,D),bf),pltpu.VMEM((R,D),bf),
-                        pltpu.SemaphoreType.DMA((3,))],
+                        pltpu.VMEM((R,D),bf),pltpu.VMEM((2,per//2,2,2*rows_in,D),bf),pltpu.VMEM((n//2,2,tail,D),bf),pltpu.VMEM((R,D),bf),
+                        pltpu.SemaphoreType.DMA((3,2))],
         compiler_params=pltpu.CompilerParams(vmem_limit_bytes=58*1024*1024,dimension_semantics=("arbitrary",)),
         cost_estimate=pl.CostEstimate(flops=2*R*D*n*rows_in*6+6*R*D*D,bytes_accessed=4*n*rows_late*D+20*R*D,transcendentals=2*R*n*rows_in),
         name="feed",
@@ -400,6 +431,54 @@
         half = self.n_t // 2
         return [pl.ds(0, half), pl.ds(half, half)] if half else [pl.ds(0, 1)]
 
+class Line:
+    def __init__(self, t, n, own, slot, rows, pieces, send, recv):
+        self.t, self.n, self.own, self.slot = t, n, own, slot
+        self.rows, self.pieces, self.send, self.recv = rows, pieces, send, recv
+
+    def piece(self, ref, j):
+        size = self.rows // self.pieces
+        return ref.at[pl.ds(j * size, size)]
+
+    def copy(self, d, s, j, b, own):
+        at = self.piece(self.slot(b), j)
+        src = self.piece(self.own, j) if own else at
+        peer = {"tensor": self.t + 1 - 2 * d}
+        return remote(src, at, self.send.at[d, s, j], self.recv.at[d, s, j], peer)
+
+    def post(self, s, j):
+        for d in range(2):
+            b = self.t - s + 2 * d * s
+            go_on = (b >= 0) & (self.t + 1 < self.n) if d == 0 else (b < self.n) & (self.t > 0)
+
+            @pl.when(go_on)
+            def _():
+                self.copy(d, s, j, b, s == 0).start()
+
+    def take(self, s, j):
+        for d in range(2):
+            b = self.t - 1 - s if d == 0 else self.t + 1 + s
+
+            @pl.when(b >= 0 if d == 0 else b < self.n)
+            def _():
+                self.copy(d, s, j, b, False).wait_recv()
+
+    def step(self, s):
+        for j in range(self.pieces):
+            self.take(s, j)
+            if s + 1 < self.n - 1:
+                self.post(s + 1, j)
+
+    def drain(self):
+        for s in range(self.n - 1):
+            for j in range(self.pieces):
+                for d in range(2):
+                    b = self.t - s + 2 * d * s
+
+                    @pl.when((b >= 0) & (self.t + 1 < self.n) if d == 0 else (b < self.n) & (self.t > 0))
+                    def _():
+                        self.copy(d, s, j, b, s == 0).wait_send()
+
 def lanes_of(count, width, shape, tall):
     wide_axis = 0 if tall else 1
     f = lax.broadcasted_iota(jnp.int32, shape, wide_axis)
@@ -427,7 +506,7 @@
                  tok_ref, wq_ref, wk_ref, wv_ref, rel_ref, qkvb_ref, ffb_ref, gains_ref, shifts_ref, ahead_ref, back_ref,
                  q_out, k_out, v_out, krel_out, qrel_out, kt_out, qr_out, toks_out, w_out, ox_out, oy_out, table_out,
                  ibias_ref, gain_ref, shift_ref,
-                 toks, packs, pack, packf, wf, w, kb, vb, qb, krel, qrel, kt, qr, table, tableb, miscf, ox, oy,
+                 toks, packs, pack, packf, wf, w, kb, vb, qb, krel, qrel, kt, qr, table, tableb, miscf, ox, ox_tall, oy_tall,
                  tok_send, tok_recv, z_send, z_recv, x_send, x_recv, out_sem):
     at = Place(n_t, n_dp)
     t = at.t
@@ -436,7 +515,6 @@
     n_all = n_t * n_dp
     S, S2 = eight(own), eight(part)
     misc = 3 * S + S2
-    right = {"tensor": lax.rem(t + 1, n_t)}
 
     packf[...] = jnp.zeros_like(packf)
     for i, ref in enumerate((wq_ref, wk_ref, wv_ref)):
@@ -463,20 +541,11 @@
         return copy
 
     here = packs.at[t, at.up, at.down, at.core]
-    ring = [go(remote(pack, here, z_send.at[i], z_recv.at[i], {"tensor": o})) for i, o in enumerate(at.others)]
-    half = R // 2
-    token = {}
-
-    def send_token(s):
-        b = lax.rem(t - s + n_t, n_t)
-        src = tok_ref if s == 0 else toks.at[b]
-        for j in range(2):
-            if s:
-                token[s - 1, j].wait_recv()
-            rows = pl.ds(j * half, half)
-            token[s, j] = go(remote(src.at[rows], toks.at[b, rows], tok_send.at[s, j], tok_recv.at[s, j], right))
-
-    send_token(0)
+    column = Line(t, n_t, pack, lambda i: packs.at[i, at.up, at.down, at.core], pack.shape[0], 1, z_send, z_recv)
+    tokens = Line(t, n_t, tok_ref, lambda i: toks.at[i], R, 2, tok_send, tok_recv)
+    column.post(0, 0)
+    for j in range(2):
+        tokens.post(0, j)
     own_pack = pltpu.make_async_copy(pack, here, out_sem.at[0])
     own_pack.start()
     outs = []
@@ -492,12 +561,13 @@
         return jnp.where(ids == rows, 1.0, 0.0).astype(bf)
 
     ox[...] = pick(back_ref, L - R - R * t)
-    oy[...] = pick(ahead_ref, L - R - R * t)
-    put(ox, ox_out)
-    put(oy, oy_out)
-
-    for copy in ring:
-        copy.wait_recv()
+    ox_tall[...] = ox[...].T
+    oy_tall[...] = pick(ahead_ref, L - R - R * t).T
+    put(ox_tall, ox_out)
+    put(oy_tall, oy_out)
+
+    for s in range(n_t - 1):
+        column.step(s)
     own_pack.wait()
     parts, orders = at.parts(), at.orders()
     n_steps = len(at.steps)
@@ -514,13 +584,13 @@
         swaps[h, k] = go(remote(piece, piece, x_send.at[h, k], x_recv.at[h, k], peer))
 
     hs = range(len(parts))
-    sent = 1
+    passed = 0
     for k in range(n_steps + 1):
         for h in hs:
             swap(h, k)
-        if k and sent < n_t - 1:
-            send_token(sent)
-            sent += 1
+        if k and passed < n_t - 2:
+            tokens.step(passed)
+            passed += 1
     for h in hs:
         swaps[h, n_steps].wait_recv()
 
@@ -549,9 +619,6 @@
     put(kt, kt_out)
     qr[...] = dot_tn(pick(back_ref, R * t), qrel[...]).astype(bf)
     put(qr, qr_out)
-    while sent < n_t - 1:
-        send_token(sent)
-        sent += 1
 
     def project(tokens, i):
         return (dot_nt(tokens, w[i]) + bias[i]).astype(bf)
@@ -569,9 +636,9 @@
     for s in range(n_t):
         b = lax.rem(t - s + n_t, n_t)
         rows = pl.ds(pl.multiple_of(b * R, R), R)
-        if s == n_t - 1:
-            for j in range(2):
-                token[s - 1, j].wait_recv()
+        if s == 1:
+            for i in range(passed, n_t - 1):
+                tokens.step(i)
         src = tok_ref if s == 0 else toks.at[b]
         put(src, toks_out.at[b])
         kb[s] = project(src[...], 1)
@@ -582,6 +649,8 @@
         copy.wait()
     for copy in copies:
         copy.wait_send()
+    column.drain()
+    tokens.drain()
 
 def begin(tokens, w_query, w_key, w_value, rel_table, qkv_bias, ff_bias, gains, shifts, ahead, back, n_t, n_dp, tiles):
     R, D = tokens.shape
@@ -595,7 +664,7 @@
     bits = (n_dp // 2).bit_length() - 1
     low = bits // 2
     S = jax.ShapeDtypeStruct
-    big = [(R, D), (L, D), (L, D), (NB, D), (NB, D), (W, D), (W, D), (n_t, R, D), (3, D, D), (NB, W), (NB, W), (NB, D)]
+    big = [(R, D), (L, D), (L, D), (NB, D), (NB, D), (W, D), (W, D), (n_t, R, D), (3, D, D), (W, NB), (W, NB), (NB, D)]
     v = lambda s, t=bf: pltpu.VMEM(s, t)
     dma = lambda *s: pltpu.SemaphoreType.DMA(s)
     return pl.pallas_call(
@@ -604,8 +673,8 @@
         in_specs=[VM] * 11, out_specs=[ANY] * len(big) + [VM] * 3,
         scratch_shapes=[v((n_t, R, D)), v((n_t, 2**(bits - low), 2**low, 2, PR, D)), v((PR, D)), v((PR, D), f32), v((D, D), f32),
                         v((3, D, D)), v((n_t, R, D)), v((n_t, R, D)), v((R, D)), v((NB, D)), v((NB, D)), v((W, D)), v((W, D)),
-                        v((NB, D), f32), v((NB, D)), v((2, n_all, D), f32), v((NB, W)), v((NB, W)),
-                        dma(n_t - 1, 2), dma(n_t - 1, 2), dma(n_t - 1), dma(n_t - 1), dma(2, bits + 1), dma(2, bits + 1),
+                        v((NB, D), f32), v((NB, D)), v((2, n_all, D), f32), v((NB, W)), v((W, NB)), v((W, NB)),
+                        dma(2, n_t - 1, 2), dma(2, n_t - 1, 2), dma(2, n_t - 1, 1), dma(2, n_t - 1, 1), dma(2, bits + 1), dma(2, bits + 1),
                         dma(10 + 3 * n_t)],
         compiler_params=pltpu.CompilerParams(collective_id=0, has_side_effects=True, vmem_limit_bytes=58 * 1024 * 1024),
         name="begin",
@@ -849,6 +918,28 @@
 GROUPS, TILES = 32, 4
 ALL=("tensor","dp")
 
+def fold(name, grid, place, terms, shapes, out_maps):
+    tail = terms[0][0].shape[-2:]
+    block = lambda x, where: pl.BlockSpec((1,) * (len(x.shape) - 2) + tail, lambda *i: tuple(where(*i)) + (0, 0))
+    n = len(terms)
+
+    def kernel(place_ref, *refs):
+        for k in range(n):
+            x, y, out = refs[2 * k], refs[2 * k + 1], refs[2 * n + k]
+            out[...] = (x[...].astype(f32) + y[...].astype(f32)).reshape(out.shape).astype(bf)
+
+    outs = [jax.ShapeDtypeStruct(s + tail, bf) for s in shapes]
+    return pl.pallas_call(
+        kernel, out_shape=outs,
+        grid_spec=pltpu.PrefetchScalarGridSpec(
+            num_scalar_prefetch=1, grid=grid,
+            in_specs=[block(z, where) for x, y, where in terms for z in (x, y)],
+            out_specs=[block(o, where) for o, where in zip(outs, out_maps)]),
+        compiler_params=pltpu.CompilerParams(vmem_limit_bytes=32 * 1024 * 1024, dimension_semantics=("arbitrary",) * len(grid)),
+        cost_estimate=pl.CostEstimate(flops=0, bytes_accessed=sum(6 * math.prod(o.shape) for o in outs), transcendentals=0),
+        name=name,
+    )(place, *[z for x, y, _ in terms for z in (x, y)])
+
 def finish_plain(dq, dk, dv, tok, toks, w, table, dqr, dkr, dres, sums, bsum, own, rel_rows, cols, inner, n_t, n_dp):
     times = lambda s, a, b: jnp.einsum(s, a.astype(bf), b.astype(bf), preferred_element_type=f32)
     scatter = lambda x: lax.psum_scatter(x, ALL, scatter_dimension=0, tiled=True)
@@ -903,18 +994,55 @@
     mask = jnp.broadcast_to(mask[:, None], (L, 128))
 
     context, scale, shares = attention_forward(query, key, value, key_table, query_table, mask)
-    layer_result_rows, d_resid_one, d_scaled, sums, bias_sums, late_grad = feed(
+    layer_result_rows, d_resid_one, d_scaled, sums, bias_sums, keep, give = feed(
         context, tokens, out_grad, scale, out_rows, late_all, inner_bias, gain, shift, group_rows, group_own)
-    d_query, d_key, d_value, d_key_rel, d_query_rel = attention_backward(
-        query, key, value, d_scaled, context, shares, key_rel, query_rel, pick_x, pick_y)
-
-    parted = lambda x: x.astype(bf).reshape(n_all, -1, D)
-    if not even:
-        late_grad = jnp.concatenate([
-            parted(late_grad[:, :group_rows]), parted(late_grad[:, group_rows:2 * group_rows]),
-            parted(late_grad[:, 2 * group_rows:2 * group_rows + group_own]),
-            jnp.zeros((n_all, late.shape[0] - late_own, D), bf)], axis=1)
-    late_sum = lax.psum_scatter(late_grad, ALL, scatter_dimension=0, tiled=True)[0].astype(f32)
+    back_args = (query, key, value, d_scaled, context, shares, key_rel, query_rel, pick_x, pick_y)
+    pairs = D // 128
+    if even and n_dp == 8 and n_t % 2 == 0 and pairs >= 4:
+        dp = lax.axis_index("dp")
+        place = jnp.stack([dp // 4, dp // 2 % 2]).astype(jnp.int32)
+        swap = lambda x, mask: lax.ppermute(x, "dp", [(i, i ^ mask) for i in range(n_dp)])
+        shape = (n_t, 2, 2, late.shape[0], D)
+        keep, give = keep.reshape(shape), give.reshape(shape)
+        got = swap(give, 1)
+        half = n_t // 2
+        *grads, keep = attention_backward(*back_args, p0=0, count=pairs - 4, through=[keep])
+        stay_one, away_one, stay_two, away_two = fold(
+            "fold", (half, 2), place,
+            [(keep, got, lambda i, j, s: (i, s[0], j)), (keep, got, lambda i, j, s: (i, 1 - s[0], j)),
+             (keep, got, lambda i, j, s: (half + i, j, s[1])), (keep, got, lambda i, j, s: (half + i, j, 1 - s[1]))],
+            [(half, 2)] * 4, [lambda i, j, s: (i, j)] * 4)
+        got_one, got_two = swap(away_one, 4), swap(away_two, 2)
+        *grads, stay_one, stay_two = attention_backward(
+            *back_args, p0=pairs - 4, count=2, before=grads, after=[away_one, away_two], through=[stay_one, stay_two])
+        stay_one, away_one, stay_two, away_two = fold(
+            "fold", (half,), place,
+            [(stay_one, got_one, lambda i, s: (i, s[1])), (stay_one, got_one, lambda i, s: (i, 1 - s[1])),
+             (stay_two, got_two, lambda i, s: (i, s[0])), (stay_two, got_two, lambda i, s: (i, 1 - s[0]))],
+            [(half,)] * 4, [lambda i, s: (i,)] * 4)
+        got_one, got_two = swap(away_one, 2), swap(away_two, 4)
+        *grads, stay_one, stay_two = attention_backward(
+            *back_args, p0=pairs - 2, count=1, before=grads, after=[away_one, away_two], through=[stay_one, stay_two])
+        column = jnp.concatenate(fold(
+            "fold", (half,), place,
+            [(stay_one, got_one, lambda i, s: (i,)), (stay_two, got_two, lambda i, s: (i,))],
+            [(half,)] * 2, [lambda i, s: (i,)] * 2), axis=0)
+        late_sum = lax.psum_scatter(column, "tensor", scatter_dimension=0, tiled=True)[0]
+        grads = attention_backward(*back_args, p0=pairs - 1, count=1, before=grads, after=[column])
+    else:
+        grads = attention_backward(*back_args)
+        core = lax.axis_index("dp") % 2
+        late_grad = jnp.where(core == 0, jnp.stack([keep, give], axis=1), jnp.stack([give, keep], axis=1))
+        late_grad = late_grad.reshape(groups, -1, D)
+        parted = lambda x: x.reshape(n_all, -1, D)
+        if not even:
+            late_grad = jnp.concatenate([
+                parted(late_grad[:, :group_rows]), parted(late_grad[:, group_rows:2 * group_rows]),
+                parted(late_grad[:, 2 * group_rows:2 * group_rows + group_own]),
+                jnp.zeros((n_all, late.shape[0] - late_own, D), bf)], axis=1)
+        late_sum = lax.psum_scatter(late_grad, ALL, scatter_dimension=0, tiled=True)[0]
+    d_query, d_key, d_value, d_key_rel, d_query_rel = grads
+    late_sum = late_sum.astype(f32)
     g_inner, g_outer, g_out = late_sum[:late_rows], late_sum[late_rows:2 * late_rows], late_sum[2 * late_rows:late_own]
     ends = (d_query, d_key, d_value, tokens, gathered, weights, table, d_query_rel, d_key_rel, d_resid_one, sums, bias_sums)
     rel_rows = rel_table.shape[0]

time: 522 us -> 482 us (0.923)
  Pallas kernels: 476 us -> 414 us
  local copies, waits for them, and re-layouts: 18.6 us -> 33.9 us
  starting transfers between devices: 0.08 us -> 5.39 us
    pallas_call x1, Pallas kernels: 155 us -> 116 us  [begin(): pl.pallas_call(functools.partial(begin_kernel, n_t, n_dp, own, part, cols...]
    pallas_call x1 -> x7, Pallas kernels: 122 us -> 106 us  [the longest x4 99.8 us: attention_backward(): pl.pallas_call(kernel, grid=(count, 2), in_specs=specs + [pl.BlockSpec(me...]
    unnamed x51 -> x74, local copies, waits for them, and re-layouts: 14.4 us -> 28.8 us
    pallas_call x1, Pallas kernels: 90.5 us -> 83.4 us  [finish(): pl.pallas_call(functools.partial(finish_kernel, n_t, n_dp, own, rel_rows,...]
    ppermute x0 -> x5, starting transfers between devices: none -> 5.31 us  [local(): lax.ppermute(x, 'dp', [(i, i ^ mask) for i in range(n_dp)])]
  transfers between devices with their start and end apart: 2 -> 7, of which waited for: 0 -> 0; matrix products, arithmetic and copies ran while one was open for 1% -> 1% of each run, Pallas kernels for 84% -> 77%
where the time goes in v5:
time: 482 us; the launch traced here: 473 us
  Pallas kernels  414 us (86%)
  local copies, waits for them, and re-layouts  33.9 us (7%)
  between operations  15.4 us (3%)
  starting transfers between devices  5.39 us (1%)
    pallas_call x1, Pallas kernels, begin(): pl.pallas_call(functools.partial(begin_kernel, n_t, n_dp, own, part, cols...  116 us
    pallas_call x4, Pallas kernels, attention_backward(): pl.pallas_call(kernel, grid=(count, 2), in_specs=specs + [pl.BlockSpec(me...  99.8 us
    pallas_call x1, Pallas kernels, finish(): pl.pallas_call(functools.partial(finish_kernel, n_t, n_dp, own, rel_rows,...  83.4 us
    pallas_call x1, Pallas kernels, attention_forward(): pl.pallas_call(functools.partial(fwd_kernel, R, L, B, C), grid=(pairs, 2)...  64.5 us
    pallas_call x1, Pallas kernels, feed(): pl.pallas_call(functools.partial(feed_kernel, R, D, tiles, per, rows_in,...  43.9 us
    unnamed x74, local copies, waits for them, and re-layouts  28.8 us
  transfers between devices with their start and end apart: 7, of which 0 were waited for; matrix products, arithmetic and copies ran while one was open for 1% of the time, Pallas kernels for 77%

profile of v5, /device:TPU:13, one launch (start us, length us, event | category | flops | bytes accessed | tf_op | source)
XLA Modules:
  0.0 473.2 jit_solution(12101349188632082930)
XLA Ops:
  7.2 0.0 all-gather.3.cloned.1.call-start
  7.2 1.8 fusion.4
  9.0 0.0 all-gather.3.cloned.1.call-update
  9.0 0.0 reduce-scatter.2.cloned.1.call-start
  9.7 0.8 reverse
  10.5 0.1 slice.35
  10.6 1.4 pad_add_fusion
  12.0 116.0 %begin.1 = (bf16[512,768]{1,0:T(8,128)(2,1)}, bf16[2048,768]{1,0:T(8,128)(2,1)}, bf16[2048,768]{1,0:T(8,128)(2,1)}, bf16[256,768]{1,0:T(8,128)(2,1)}, bf16[256,7...) custom-call(bf16[512,768]{1,0:T(8,128)(2,1)} %tok_in.1, ...), custom_call_target="tpu_custom_call" | custom-call | tf_op jit(solution)/shard_map/begin/pallas_call | solution.py:670
  128.0 0.3 broadcast_in_dim.22.mask_ref
  128.4 1.1 copy-done.4
  129.5 64.5 %attend.1 = (bf16[512,768]{1,0:T(8,128)(2,1)S(1)}, f32[512,768]{1,0:T(8,128)S(1)}, bf16[12,512,2048]{2,1,0:T(8,128)(2,1)}) custom-call(bf16[2048,128]{1,0:T(8,128)(2,1)S(1)} %broadcast_in_dim.22.mask_ref, bf16[512,768]{1,0:T(8,128)(2,1)S(1)} %copy-done.4, bf16[2048,768]{1,0:T(8,128)(2,1)} %get-tuple-element.83.k_ref.refs_1_, ...), custom_call_target="tpu_custom_call" | custom-call | flops 12884901888 | bytes 40894464 | tf_op jit(solution)/shard_map/attend/pallas_call | solution.py:111
  194.0 0.9 copy-done.7
  194.9 1.1 copy-done.21
  196.1 2.3 slice.28
  198.4 43.9 %feed.1 = (bf16[512,768]{1,0:T(8,128)(2,1)}, f32[512,768]{1,0:T(8,128)}, bf16[512,768]{1,0:T(8,128)(2,1)}, f32[8,768]{1,0:T(8,128)}, f32[4,1,768]{2,1,0:T(1,128)...) custom-call(bf16[512,768]{1,0:T(8,128)(2,1)} %copy-done.7, bf16[512,768]{1,0:T(8,128)(2,1)} %tok_in.1, ...), custom_call_target="tpu_custom_call" | custom-call | flops 16307453952 | bytes 29884416 | tf_op jit(solution)/shard_map/feed/pallas_call | solution.py:356
  242.3 3.2 collective-permute-start
  245.5 0.1 pad_add_fusion.2.place_ref
  245.6 1.1 copy-done.8
  246.7 1.1 copy-done.10
  247.8 1.0 copy-done.17
  248.8 31.9 %attend_back.4 = (bf16[512,768]{1,0:T(8,128)(2,1)S(1)}, bf16[2048,768]{1,0:T(8,128)(2,1)}, bf16[2048,768]{1,0:T(8,128)(2,1)}, f32[256,768]{1,0:T(8,128)S(1)}, f3...) custom-call(bf16[512,768]{1,0:T(8,128)(2,1)S(1)} %copy-done.5, ...), custom_call_target="tpu_custom_call", output_to_operand_aliasing={{5}: (10, {})} | custom-call | flops 8589934592 | bytes 18874368 | tf_op jit(solution)/shard_map/attend_back/pallas_call | solution.py:197
  280.7 2.6 copy-done
  283.3 4.4 fold.3
  287.7 0.0 copy-start.12
  287.7 1.1 copy-done.12
  288.8 1.1 copy-done.14
  289.8 0.2 collective-permute-start.1
  290.1 0.4 collective-permute-start.2
  290.5 0.5 copy-done.19
  291.0 0.4 copy-done.20
  291.4 32.1 %attend_back.5 = (bf16[512,768]{1,0:T(8,128)(2,1)S(1)}, bf16[2048,768]{1,0:T(8,128)(2,1)}, bf16[2048,768]{1,0:T(8,128)(2,1)}, f32[256,768]{1,0:T(8,128)S(1)}, f3...) custom-call(bf16[512,768]{1,0:T(8,128)(2,1)S(1)} %copy-done.5, ...), custom_call_target="tpu_custom_call", output_to_operand_aliasing={{0}: (10, {}), {1}: (11, {}), {2}: (12, {}), {3}: (13, {}),... | custom-call | flops 8589934592 | bytes 18874368 | tf_op jit(solution)/shard_map/attend_back/pallas_call | solution.py:197
  323.5 0.0 copy-start.13
  323.5 1.3 copy-done.13
  324.8 1.3 copy-done.15
  326.2 1.2 fold.4
  327.4 0.3 collective-permute-start.3
  327.7 1.1 collective-permute-start.4
  328.9 17.8 %attend_back.6 = (bf16[512,768]{1,0:T(8,128)(2,1)S(1)}, bf16[2048,768]{1,0:T(8,128)(2,1)}, bf16[2048,768]{1,0:T(8,128)(2,1)}, f32[256,768]{1,0:T(8,128)S(1)}, f3...) custom-call(bf16[512,768]{1,0:T(8,128)(2,1)} %get-tuple-element.82.q, ...), custom_call_target="tpu_custom_call", output_to_operand_aliasing={{0}: (10, {}), {1}: (11, {}), {2}: (12, {}), {3}: (13, {}),... | custom-call | flops 4294967296 | bytes 9437184 | tf_op jit(solution)/shard_map/attend_back/pallas_call | solution.py:197
  346.7 0.9 fold.5
  347.6 0.9 constant_dynamic-update-slice_fusion.1
  348.5 0.9 constant_dynamic-update-slice_fusion.refs_15_
  349.4 0.0 reduce-scatter.2.cloned.1.call-update
  349.4 0.5 copy-done.6
  349.9 1.1 copy-done.9
  351.0 1.1 copy-done.11
  352.2 1.0 copy-done.18
  353.2 18.0 %attend_back.7 = (bf16[512,768]{1,0:T(8,128)(2,1)S(1)}, bf16[2048,768]{1,0:T(8,128)(2,1)}, bf16[2048,768]{1,0:T(8,128)(2,1)}, f32[256,768]{1,0:T(8,128)S(1)}, f32[256,768]{1,0:T(8,128)S(1)}) custom-call(bf16[512,768]{1,0:T(8,128)(2,1)S(1)} %copy-done.6, ...), custom_call_target="tpu_custom_call", output_to_operand_aliasing={{0}: (10, {}), {1}: (11, {}), {2}: (12, {}), {3}: (13, {}),... | custom-call | flops 4294967296 | bytes 9437184 | tf_op jit(solution)/shard_map/attend_back/pallas_call | solution.py:197
  371.2 0.9 copy-done.1
  372.1 0.9 copy-done.2
  373.0 0.9 copy-done.3
  373.8 83.4 %finish.1 = (f32[512,768]{1,0:T(8,128)}, f32[24,768]{1,0:T(8,128)}, f32[24,768]{1,0:T(8,128)}, f32[24,768]{1,0:T(8,128)}, f32[32,768]{1,0:T(8,128)}, /*index=5*/...) custom-call(bf16[512,768]{1,0:T(8,128)(2,1)} %copy-done.1, bf16[4,512,768]{2,1,0:T(8,128)(2,1)} %bitcast.22, ...), custom_call_target="tpu_custom_call" | custom-call | tf_op jit(solution)/shard_map/finish/pallas_call | solution.py:903
  457.3 0.0 reduce-scatter.2.cloned.1.call-done
  457.3 1.1 convert_element_type.14
  458.4 0.6 slice_bitcast_fusion.2
  459.1 0.8 slice_bitcast_fusion
  460.0 1.1 copy.79
  461.1 0.6 copy.80
  461.8 0.6 copy.81
  462.4 0.6 copy.82
  463.0 0.6 copy.83
  463.6 0.5 copy.84
  464.1 0.6 copy.85
  464.8 0.6 copy.86
  465.3 0.6 copy.87
  (47 shorter events, 0.1 us)
Async XLA Ops:
  7.2 188.9 %all-gather.3.cloned.1.call-start = ((), (), s32[]{:S(2)}) async-start(), calls=%async_computation.2 | async-start | bytes 11354112 | tf_op jit(solution)/shard_map/all_gather | solution.py:984
  9.0 448.3 %reduce-scatter.2.cloned.1.call-start = ((), (), s32[]{:S(2)}) async-start(), calls=%async_computation.1 | async-start | bytes 1720320 | tf_op jit(solution)/shard_map/reduce_scatter | solution.py:1030
  128.4 1.1 copy-start.4
  194.0 0.9 copy-start.7
  194.9 1.1 copy-start.21
  198.4 47.2 %copy-start.5 = (bf16[512,768]{1,0:T(8,128)(2,1)S(1)}, bf16[512,768]{1,0:T(8,128)(2,1)}, u32[]{:S(2)}) copy-start(bf16[512,768]{1,0:T(8,128)(2,1)} %get-tuple-element.82.q_ref.refs_0_) | copy-start | bytes 2359300
  198.4 47.2 %copy-start.16 = (bf16[256,768]{1,0:T(8,128)(2,1)S(1)}, bf16[256,768]{1,0:T(8,128)(2,1)}, u32[]{:S(2)}) copy-start(bf16[256,768]{1,0:T(8,128)(2,1)} %get-tuple-element.95.refs_6_) | copy-start | bytes 1179652
  242.3 38.4 %collective-permute-start = (bf16[4,2,2,224,768]{4,3,2,1,0:T(8,128)(2,1)}, bf16[4,2,2,224,768]{4,3,2,1,0:T(8,128)(2,1)}, u32[]{:S(2)}, u32[]{:S(2)}) collective-permute-start(bf16[4,2,2,224,768]{4,3,2,1,0:T(8,128)(2,1)} %bitcast.31), channel_id=1, source_target_pairs={{0,4},{4,0},{8,12},{12,8},{16,20},{20,16},{24,28},{28,24},{1,5},{5... | collective-permute-start | bytes 16515080 | tf_op jit(solution)/shard_map/ppermute | solution.py:1004
  245.6 1.1 copy-start.8
  246.7 1.1 copy-start.10
  247.8 1.0 copy-start.17
  280.7 2.6 copy-start
  287.7 1.1 copy-start.12
  288.8 1.1 copy-start.14
  289.8 1.2 copy-start.19
  289.8 1.6 copy-start.20
  289.8 33.7 %collective-permute-start.1 = (bf16[2,2,224,768]{3,2,1,0:T(8,128)(2,1)S(1)}, bf16[2,2,224,768]{3,2,1,0:T(8,128)(2,1)S(1)}, u32[]{:S(2)}, u32[]{:S(2)}) collective-permute-start(bf16[2,2,224,768]{3,2,1,0:T(8,128)(2,1)S(1)} %get-tuple-element.109.refs_17_), channel_id=1, source_target_pairs={{0,16},{4,20},{8,24},{12,28},{16,0},{20,4},{24,8},{28,12},{1,17},{... | collective-permute-start | bytes 4128776 | tf_op jit(solution)/shard_map/ppermute | solution.py:1004
  290.1 33.4 %collective-permute-start.2 = (bf16[2,2,224,768]{3,2,1,0:T(8,128)(2,1)S(1)}, bf16[2,2,224,768]{3,2,1,0:T(8,128)(2,1)S(1)}, u32[]{:S(2)}, u32[]{:S(2)}) collective-permute-start(bf16[2,2,224,768]{3,2,1,0:T(8,128)(2,1)S(1)} %get-tuple-element.110.refs_18_), channel_id=1, source_target_pairs={{0,8},{4,12},{8,0},{12,4},{16,24},{20,28},{24,16},{28,20},{1,9},{5... | collective-permute-start | bytes 4128776 | tf_op jit(solution)/shard_map/ppermute | solution.py:1004
  323.5 1.3 copy-start.13
  324.8 1.3 copy-start.15
  327.4 19.3 %collective-permute-start.3 = (bf16[2,224,768]{2,1,0:T(8,128)(2,1)S(1)}, bf16[2,224,768]{2,1,0:T(8,128)(2,1)S(1)}, u32[]{:S(2)}, u32[]{:S(2)}) collective-permute-start(bf16[2,224,768]{2,1,0:T(8,128)(2,1)S(1)} %get-tuple-element.120.refs_17_), channel_id=1, source_target_pairs={{0,8},{4,12},{8,0},{12,4},{16,24},{20,28},{24,16},{28,20},{1,9},{5... | collective-permute-start | bytes 2064392 | tf_op jit(solution)/shard_map/ppermute | solution.py:1004
  327.7 19.0 %collective-permute-start.4 = (bf16[2,224,768]{2,1,0:T(8,128)(2,1)S(1)}, bf16[2,224,768]{2,1,0:T(8,128)(2,1)S(1)}, u32[]{:S(2)}, u32[]{:S(2)}) collective-permute-start(bf16[2,224,768]{2,1,0:T(8,128)(2,1)S(1)} %get-tuple-element.121.refs_18_), channel_id=1, source_target_pairs={{0,16},{4,20},{8,24},{12,28},{16,0},{20,4},{24,8},{28,12},{1,17},{... | collective-permute-start | bytes 2064392 | tf_op jit(solution)/shard_map/ppermute | solution.py:1004
  348.5 1.4 copy-start.6
  349.9 1.1 copy-start.9
  351.0 1.1 copy-start.11
  352.2 1.0 copy-start.18
  371.2 0.9 copy-start.1
  372.1 0.9 copy-start.2
  372.9 0.9 copy-start.3
  457.2 2.7 copy-start.22
  459.9 1.2 copy-start.26
  459.9 1.8 copy-start.25
  459.9 2.5 copy-start.24
  459.9 3.1 copy-start.28
  459.9 3.7 copy-start.30
  459.9 4.2 copy-start.23
  460.0 4.8 %copy-start.29 = (f32[2,96]{1,0:T(2,128)S(1)}, f32[2,96]{1,0:T(2,128)}, u32[]{:S(2)}) copy-start(f32[2,96]{1,0:T(2,128)} %get-tuple-element.179) | copy-start | bytes 2308
  460.0 5.4 %copy-start.27 = (f32[4,96]{1,0:T(4,128)S(1)}, f32[4,96]{1,0:T(4,128)}, u32[]{:S(2)}) copy-start(f32[4,96]{1,0:T(4,128)} %get-tuple-element.180) | copy-start | bytes 4612
Sparse Core Ops, SparseCore 0:
  11.5 109.9 all-gather.2
  349.6 36.0 reduce-scatter.1

commit v6 on v5

--- a/solution.py
+++ b/solution.py
@@ -503,11 +503,11 @@
     return -(-n // 8) * 8
 
 def begin_kernel(n_t, n_dp, own, part, cols, inner, tiles, L,
-                 tok_ref, wq_ref, wk_ref, wv_ref, rel_ref, qkvb_ref, ffb_ref, gains_ref, shifts_ref, ahead_ref, back_ref,
-                 q_out, k_out, v_out, krel_out, qrel_out, kt_out, qr_out, toks_out, w_out, ox_out, oy_out, table_out,
+                 tok_ref, wq_ref, wk_ref, wv_ref, rel_ref, qkvb_ref, ffb_ref, gains_ref, shifts_ref, ahead_ref, back_ref, late_ref,
+                 q_out, k_out, v_out, krel_out, qrel_out, kt_out, qr_out, toks_out, w_out, ox_out, oy_out, table_out, late_all,
                  ibias_ref, gain_ref, shift_ref,
                  toks, packs, pack, packf, wf, w, kb, vb, qb, krel, qrel, kt, qr, table, tableb, miscf, ox, ox_tall, oy_tall,
-                 tok_send, tok_recv, z_send, z_recv, x_send, x_recv, out_sem):
+                 tok_send, tok_recv, z_send, z_recv, x_send, x_recv, out_sem, lz_send, lz_recv, lx_send, lx_recv, lc_send, lc_recv):
     at = Place(n_t, n_dp)
     t = at.t
     R, D = tok_ref.shape
@@ -543,9 +543,11 @@
     here = packs.at[t, at.up, at.down, at.core]
     column = Line(t, n_t, pack, lambda i: packs.at[i, at.up, at.down, at.core], pack.shape[0], 1, z_send, z_recv)
     tokens = Line(t, n_t, tok_ref, lambda i: toks.at[i], R, 2, tok_send, tok_recv)
+    late = Line(t, n_t, late_ref, lambda i: late_all.at[i, at.up, at.down, at.core], late_ref.shape[0], 1, lz_send, lz_recv)
     column.post(0, 0)
-    for j in range(2):
-        tokens.post(0, j)
+    late.post(0, 0)
+    own_late = pltpu.make_async_copy(late_ref, late_all.at[t, at.up, at.down, at.core], out_sem.at[out_sem.shape[0] - 1])
+    own_late.start()
     own_pack = pltpu.make_async_copy(pack, here, out_sem.at[0])
     own_pack.start()
     outs = []
@@ -568,6 +570,11 @@
 
     for s in range(n_t - 1):
         column.step(s)
+        if s < n_t - 2:
+            late.step(s)
+        if s == n_t - 3 or n_t < 3:
+            for j in range(2):
+                tokens.post(0, j)
     own_pack.wait()
     parts, orders = at.parts(), at.orders()
     n_steps = len(at.steps)
@@ -584,13 +591,40 @@
         swaps[h, k] = go(remote(piece, piece, x_send.at[h, k], x_recv.at[h, k], peer))
 
     hs = range(len(parts))
+    moves = {}
+
+    def late_twin(h, k):
+        up, down = at.spans(orders[h][:k])
+        if k:
+            kind, i = orders[h][k - 1]
+            base = (getattr(at, kind) // 2**(i + 1)) * 2**(i + 1)
+            other = pl.ds(base + (1 - at.bit((kind, i))) * 2**i, 2**i)
+            up, down = (other, down) if kind == "up" else (up, other)
+        piece = late_all.at[parts[h], up, down, at.core]
+        moves[h, k, "twin"] = go(remote(piece, piece, lc_send.at[h, k], lc_recv.at[h, k], at.twin))
+
+    def late_swap(k):
+        for h in hs:
+            if k:
+                moves[h, k - 1, "swap"].wait_recv()
+            if k < n_steps:
+                up, down = at.spans(orders[h][:k])
+                piece = late_all.at[parts[h], up, down, at.core]
+                moves[h, k, "swap"] = go(remote(piece, piece, lx_send.at[h, k], lx_recv.at[h, k], at.peer(orders[h][k])))
+            late_twin(h, k)
+
+    for h in hs:
+        swap(h, 0)
+    late.step(n_t - 2)
+    own_late.wait()
+    late_swap(0)
     passed = 0
-    for k in range(n_steps + 1):
+    for k in range(1, n_steps + 1):
         for h in hs:
             swap(h, k)
-        if k and passed < n_t - 2:
-            tokens.step(passed)
-            passed += 1
+    if n_t > 2:
+        tokens.step(0)
+        passed = 1
     for h in hs:
         swaps[h, n_steps].wait_recv()
 
@@ -607,6 +641,8 @@
         a, dp = p // n_dp, p % n_dp
         to = dp * n_t * part + a * part
         table[to:to + part, :] = packs[s[0], s[1], s[2], s[3], 3 * S:3 * S + part, :].astype(f32)
+    if n_steps:
+        late_swap(1)
     bias = [spread_row(miscf[0, :, 128 * i:128 * i + 128], own, D, 0) for i in range(3)]
     rel = table[...].astype(bf)
     tableb[...] = rel
@@ -619,6 +655,9 @@
     put(kt, kt_out)
     qr[...] = dot_tn(pick(back_ref, R * t), qrel[...]).astype(bf)
     put(qr, qr_out)
+    if n_t > 3:
+        tokens.step(1)
+        passed = 2
 
     def project(tokens, i):
         return (dot_nt(tokens, w[i]) + bias[i]).astype(bf)
@@ -637,6 +676,8 @@
         b = lax.rem(t - s + n_t, n_t)
         rows = pl.ds(pl.multiple_of(b * R, R), R)
         if s == 1:
+            for k in range(2, n_steps + 1):
+                late_swap(k)
             for i in range(passed, n_t - 1):
                 tokens.step(i)
         src = tok_ref if s == 0 else toks.at[b]
@@ -645,14 +686,18 @@
         put(kb.at[s], k_out.at[rows])
         vb[s] = project(src[...], 2)
         put(vb.at[s], v_out.at[rows])
+    for h in hs:
+        for k in range(n_steps + 1):
+            moves[h, k, "twin"].wait_recv()
     for copy in outs:
         copy.wait()
     for copy in copies:
         copy.wait_send()
     column.drain()
+    late.drain()
     tokens.drain()
 
-def begin(tokens, w_query, w_key, w_value, rel_table, qkv_bias, ff_bias, gains, shifts, ahead, back, n_t, n_dp, tiles):
+def begin(tokens, w_query, w_key, w_value, rel_table, qkv_bias, ff_bias, gains, shifts, ahead, back, late, n_t, n_dp, tiles):
     R, D = tokens.shape
     L = ahead.shape[1] // 2
     W = L + R
@@ -664,21 +709,22 @@
     bits = (n_dp // 2).bit_length() - 1
     low = bits // 2
     S = jax.ShapeDtypeStruct
-    big = [(R, D), (L, D), (L, D), (NB, D), (NB, D), (W, D), (W, D), (n_t, R, D), (3, D, D), (W, NB), (W, NB), (NB, D)]
+    big = [(R, D), (L, D), (L, D), (NB, D), (NB, D), (W, D), (W, D), (n_t, R, D), (3, D, D), (W, NB), (W, NB), (NB, D),
+           (n_t, 2**(bits - low), 2**low, 2, late.shape[0], D)]
     v = lambda s, t=bf: pltpu.VMEM(s, t)
     dma = lambda *s: pltpu.SemaphoreType.DMA(s)
     return pl.pallas_call(
         functools.partial(begin_kernel, n_t, n_dp, own, part, cols, inner, tiles, L),
         out_shape=[S(s, bf) for s in big] + [S((tiles, 1, width), f32), S((2, D), f32), S((4, D), f32)],
-        in_specs=[VM] * 11, out_specs=[ANY] * len(big) + [VM] * 3,
+        in_specs=[VM] * 11 + [ANY], out_specs=[ANY] * len(big) + [VM] * 3,
         scratch_shapes=[v((n_t, R, D)), v((n_t, 2**(bits - low), 2**low, 2, PR, D)), v((PR, D)), v((PR, D), f32), v((D, D), f32),
                         v((3, D, D)), v((n_t, R, D)), v((n_t, R, D)), v((R, D)), v((NB, D)), v((NB, D)), v((W, D)), v((W, D)),
                         v((NB, D), f32), v((NB, D)), v((2, n_all, D), f32), v((NB, W)), v((W, NB)), v((W, NB)),
                         dma(2, n_t - 1, 2), dma(2, n_t - 1, 2), dma(2, n_t - 1, 1), dma(2, n_t - 1, 1), dma(2, bits + 1), dma(2, bits + 1),
-                        dma(10 + 3 * n_t)],
+                        dma(11 + 3 * n_t), dma(2, n_t - 1, 1), dma(2, n_t - 1, 1), dma(2, max(bits, 1)), dma(2, max(bits, 1)), dma(2, bits + 1), dma(2, bits + 1)],
         compiler_params=pltpu.CompilerParams(collective_id=0, has_side_effects=True, vmem_limit_bytes=58 * 1024 * 1024),
         name="begin",
-    )(tokens, w_query, w_key, w_value, rel_table, qkv_bias, ff_bias, gains, shifts, ahead, back)
+    )(tokens, w_query, w_key, w_value, rel_table, qkv_bias, ff_bias, gains, shifts, ahead, back, late)
 
 def finish_kernel(n_t, n_dp, own, rel_rows, cols, inner, tiles,
                   dq_in, dk_in, dv_in, tok_in, toks_in, w_in, table_in, dqr_in, dkr_in, dres_in, sums_ref, bsum_ref,
@@ -972,16 +1018,16 @@
     none = jnp.full((1,), -1, jnp.int32)
     ahead = jnp.concatenate([rel_bucket, none])[None]
     back = jnp.concatenate([rel_bucket[::-1], none])[None]
-    (query, key, value, key_rel, query_rel, key_table, query_table, gathered, weights, pick_x, pick_y, table,
-     inner_bias, gain, shift) = begin(tokens, w_query, w_key, w_value, rel_table, qkv_bias, ff_bias.reshape(1, -1), gains, shifts,
-                                      ahead, back, n_t, n_dp, TILES)
-    gathered = gathered.reshape(L, D)
     late_rows = w_ff_in.shape[0]
     even = late_rows % 16 == 0 and own_rows % 8 == 0
     late = jnp.concatenate([w_ff_in, w_ff_out, w_out], axis=0)
     late_own = late.shape[0]
     late = jnp.pad(late, ((0, -late_own % 16), (0, 0)))
-    late_all = lax.all_gather(late, ALL, axis=0, tiled=False)
+    (query, key, value, key_rel, query_rel, key_table, query_table, gathered, weights, pick_x, pick_y, table,
+     late_all, inner_bias, gain, shift) = begin(tokens, w_query, w_key, w_value, rel_table, qkv_bias, ff_bias.reshape(1, -1), gains, shifts,
+                                      ahead, back, late, n_t, n_dp, TILES)
+    gathered = gathered.reshape(L, D)
+    late_all = late_all.reshape(n_all, -1, D)
     cut = lambda x, at, n: x[:, at:at + n].reshape(n_all * n, D)
     out_rows = cut(late_all, 2 * late_rows, own_rows)
     groups = n_all if even else GROUPS

time: 482 us -> 461 us (0.956)
  the two profiles are of different devices: /device:TPU:13 before, /device:TPU:26 now
where the time goes in v6:
time: 461 us; the launch traced here: 453 us
  Pallas kernels  397 us (86%)
  local copies, waits for them, and re-layouts  31.9 us (7%)
  between operations  15.4 us (3%)
    pallas_call x1, Pallas kernels, begin(): pl.pallas_call(functools.partial(begin_kernel, n_t, n_dp, own, part, cols...  103 us
    pallas_call x4, Pallas kernels, attention_backward(): pl.pallas_call(kernel, grid=(count, 2), in_specs=specs + [pl.BlockSpec(me...  99.8 us
    pallas_call x1, Pallas kernels, finish(): pl.pallas_call(functools.partial(finish_kernel, n_t, n_dp, own, rel_rows,...  78.7 us
    pallas_call x1, Pallas kernels, attention_forward(): pl.pallas_call(functools.partial(fwd_kernel, R, L, B, C), grid=(pairs, 2)...  64.6 us
    pallas_call x1, Pallas kernels, feed(): pl.pallas_call(functools.partial(feed_kernel, R, D, tiles, per, rows_in,...  43.8 us
    unnamed x72, local copies, waits for them, and re-layouts  26.8 us
  transfers between devices with their start and end apart: 6, of which 0 were waited for; matrix products, arithmetic and copies ran while one was open for 0% of the time, Pallas kernels for 39%

profile of v6, /device:TPU:26, one launch (start us, length us, event | category | flops | bytes accessed | tf_op | source)
XLA Modules:
  0.0 452.9 jit_solution(6005494836160563812)
XLA Ops:
  7.2 0.0 reduce-scatter.2.cloned.1.call-start
  7.9 0.8 reverse
  8.7 0.1 slice.35
  8.7 1.4 pad_add_fusion
  10.2 1.8 fusion.4.late_ref
  11.9 103.5 %begin.1 = (bf16[512,768]{1,0:T(8,128)(2,1)}, bf16[2048,768]{1,0:T(8,128)(2,1)}, bf16[2048,768]{1,0:T(8,128)(2,1)}, bf16[256,768]{1,0:T(8,128)(2,1)}, bf16[256,7...) custom-call(bf16[512,768]{1,0:T(8,128)(2,1)} %tok_in.1, ...), custom_call_target="tpu_custom_call" | custom-call | tf_op jit(solution)/shard_map/begin/pallas_call | solution.py:716
  115.4 2.4 slice.28
  117.8 0.3 broadcast_in_dim.22.mask_ref
  118.2 64.6 %attend.1 = (bf16[512,768]{1,0:T(8,128)(2,1)S(1)}, f32[512,768]{1,0:T(8,128)S(1)}, bf16[12,512,2048]{2,1,0:T(8,128)(2,1)}) custom-call(bf16[2048,128]{1,0:T(8,128)(2,1)S(1)} %broadcast_in_dim.22.mask_ref, bf16[512,768]{1,0:T(8,128)(2,1)S(1)} %copy-done.4, bf16[2048,768]{1,0:T(8,128)(2,1)} %get-tuple-element.84.k_ref.refs_1_, ...), custom_call_target="tpu_custom_call" | custom-call | flops 12884901888 | bytes 40894464 | tf_op jit(solution)/shard_map/attend/pallas_call | solution.py:111
  182.8 0.9 copy-done.6
  183.7 1.1 copy-done.20
  184.8 43.8 %feed.1 = (bf16[512,768]{1,0:T(8,128)(2,1)}, f32[512,768]{1,0:T(8,128)}, bf16[512,768]{1,0:T(8,128)(2,1)}, f32[8,768]{1,0:T(8,128)}, f32[4,1,768]{2,1,0:T(1,128)...) custom-call(bf16[512,768]{1,0:T(8,128)(2,1)} %copy-done.6, bf16[512,768]{1,0:T(8,128)(2,1)} %tok_in.1, ...), custom_call_target="tpu_custom_call" | custom-call | flops 16307453952 | bytes 29884416 | tf_op jit(solution)/shard_map/feed/pallas_call | solution.py:356
  228.6 0.1 collective-permute-start
  228.7 0.1 pad_add_fusion.2.place_ref
  228.8 1.1 copy-done.7
  230.0 1.1 copy-done.9
  231.1 1.0 copy-done.16
  232.1 32.1 %attend_back.4 = (bf16[512,768]{1,0:T(8,128)(2,1)S(1)}, bf16[2048,768]{1,0:T(8,128)(2,1)}, bf16[2048,768]{1,0:T(8,128)(2,1)}, f32[256,768]{1,0:T(8,128)S(1)}, f3...) custom-call(bf16[512,768]{1,0:T(8,128)(2,1)S(1)} %copy-done.4, ...), custom_call_target="tpu_custom_call", output_to_operand_aliasing={{5}: (10, {})} | custom-call | flops 8589934592 | bytes 18874368 | tf_op jit(solution)/shard_map/attend_back/pallas_call | solution.py:197
  264.1 0.0 collective-permute-done.refs_1_.refs_3_.refs_5_.refs_7_
  264.1 2.6 copy-done
  266.7 4.4 fold.3
  271.1 0.0 copy-start.11
  271.1 1.1 copy-done.11
  272.2 1.1 copy-done.13
  273.2 1.5 collective-permute-start.1
  274.7 0.5 collective-permute-start.2
  275.3 31.8 %attend_back.5 = (bf16[512,768]{1,0:T(8,128)(2,1)S(1)}, bf16[2048,768]{1,0:T(8,128)(2,1)}, bf16[2048,768]{1,0:T(8,128)(2,1)}, f32[256,768]{1,0:T(8,128)S(1)}, f3...) custom-call(bf16[512,768]{1,0:T(8,128)(2,1)S(1)} %copy-done.4, ...), custom_call_target="tpu_custom_call", output_to_operand_aliasing={{0}: (10, {}), {1}: (11, {}), {2}: (12, {}), {3}: (13, {}),... | custom-call | flops 8589934592 | bytes 18874368 | tf_op jit(solution)/shard_map/attend_back/pallas_call | solution.py:197
  307.1 0.0 collective-permute-done.1.refs_1_.refs_3_
  307.1 0.0 collective-permute-done.2.refs_5_.refs_7_
  307.1 0.0 copy-start.12
  307.2 1.3 copy-done.12
  308.5 1.3 copy-done.14
  309.8 1.3 fold.4
  311.1 1.5 collective-permute-start.3
  312.6 0.5 collective-permute-start.4
  313.1 17.9 %attend_back.6 = (bf16[512,768]{1,0:T(8,128)(2,1)S(1)}, bf16[2048,768]{1,0:T(8,128)(2,1)}, bf16[2048,768]{1,0:T(8,128)(2,1)}, f32[256,768]{1,0:T(8,128)S(1)}, f3...) custom-call(bf16[512,768]{1,0:T(8,128)(2,1)} %get-tuple-element.83.q, ...), custom_call_target="tpu_custom_call", output_to_operand_aliasing={{0}: (10, {}), {1}: (11, {}), {2}: (12, {}), {3}: (13, {}),... | custom-call | flops 4294967296 | bytes 9437184 | tf_op jit(solution)/shard_map/attend_back/pallas_call | solution.py:197
  331.0 0.0 collective-permute-done.3.refs_1_
  331.0 0.0 collective-permute-done.4.refs_3_
  331.1 0.9 fold.5
  332.0 0.9 constant_dynamic-update-slice_fusion.1
  332.9 0.9 constant_dynamic-update-slice_fusion.refs_15_
  333.8 0.0 reduce-scatter.2.cloned.1.call-update
  333.8 0.5 copy-done.5
  334.3 1.1 copy-done.8
  335.4 1.1 copy-done.10
  336.5 1.0 copy-done.17
  337.5 18.0 %attend_back.7 = (bf16[512,768]{1,0:T(8,128)(2,1)S(1)}, bf16[2048,768]{1,0:T(8,128)(2,1)}, bf16[2048,768]{1,0:T(8,128)(2,1)}, f32[256,768]{1,0:T(8,128)S(1)}, f32[256,768]{1,0:T(8,128)S(1)}) custom-call(bf16[512,768]{1,0:T(8,128)(2,1)S(1)} %copy-done.5, ...), custom_call_target="tpu_custom_call", output_to_operand_aliasing={{0}: (10, {}), {1}: (11, {}), {2}: (12, {}), {3}: (13, {}),... | custom-call | flops 4294967296 | bytes 9437184 | tf_op jit(solution)/shard_map/attend_back/pallas_call | solution.py:197
  355.6 0.9 copy-done.1
  356.5 0.9 copy-done.2
  357.4 0.9 copy-done.3
  358.2 78.7 %finish.1 = (f32[512,768]{1,0:T(8,128)}, f32[24,768]{1,0:T(8,128)}, f32[24,768]{1,0:T(8,128)}, f32[24,768]{1,0:T(8,128)}, f32[32,768]{1,0:T(8,128)}, /*index=5*/...) custom-call(bf16[512,768]{1,0:T(8,128)(2,1)} %copy-done.1, bf16[4,512,768]{2,1,0:T(8,128)(2,1)} %bitcast.22, ...), custom_call_target="tpu_custom_call" | custom-call | tf_op jit(solution)/shard_map/finish/pallas_call | solution.py:949
  436.9 0.0 reduce-scatter.2.cloned.1.call-done
  437.0 1.1 convert_element_type.14
  438.1 0.6 slice_bitcast_fusion.2
  438.7 0.8 slice_bitcast_fusion
  439.7 1.1 copy.79
  440.8 0.6 copy.80
  441.4 0.6 copy.81
  442.1 0.6 copy.82
  442.7 0.6 copy.83
  443.3 0.5 copy.84
  443.8 0.6 copy.85
  444.5 0.6 copy.86
  445.0 0.6 copy.87
  (42 shorter events, 0.1 us)
Async XLA Ops:
  7.2 429.8 %reduce-scatter.2.cloned.1.call-start = ((), (), s32[]{:S(2)}) async-start(), calls=%async_computation.1 | async-start | bytes 1720320 | tf_op jit(solution)/shard_map/reduce_scatter | solution.py:1076
  115.4 2.8 copy-start.4
  182.8 0.9 copy-start.6
  183.7 1.1 copy-start.20
  184.8 44.0 %copy-start.15 = (bf16[256,768]{1,0:T(8,128)(2,1)S(1)}, bf16[256,768]{1,0:T(8,128)(2,1)}, u32[]{:S(2)}) copy-start(bf16[256,768]{1,0:T(8,128)(2,1)} %get-tuple-element.97.refs_6_) | copy-start | bytes 1179652
  228.6 35.5 %collective-permute-start = (bf16[4,2,2,224,768]{4,3,2,1,0:T(8,128)(2,1)}, bf16[4,2,2,224,768]{4,3,2,1,0:T(8,128)(2,1)}, u32[]{:S(2)}, u32[]{:S(2)}) collective-permute-start(bf16[4,2,2,224,768]{4,3,2,1,0:T(8,128)(2,1)} %bitcast.31), channel_id=1, source_target_pairs={{0,4},{4,0},{8,12},{12,8},{16,20},{20,16},{24,28},{28,24},{1,5},{5... | collective-permute-start | bytes 16515080 | tf_op jit(solution)/shard_map/ppermute | solution.py:1050
  228.8 1.1 copy-start.7
  229.9 1.1 copy-start.9
  231.1 1.0 copy-start.16
  264.1 2.6 copy-start
  271.1 1.1 copy-start.11
  272.2 1.1 copy-start.13
  273.2 2.1 copy-start.18
  273.2 2.1 copy-start.19
  273.2 33.9 %collective-permute-start.1 = (bf16[2,2,224,768]{3,2,1,0:T(8,128)(2,1)S(1)}, bf16[2,2,224,768]{3,2,1,0:T(8,128)(2,1)S(1)}, u32[]{:S(2)}, u32[]{:S(2)}) collective-permute-start(bf16[2,2,224,768]{3,2,1,0:T(8,128)(2,1)S(1)} %get-tuple-element.111.refs_17_), channel_id=1, source_target_pairs={{0,16},{4,20},{8,24},{12,28},{16,0},{20,4},{24,8},{28,12},{1,17},{... | collective-permute-start | bytes 4128776 | tf_op jit(solution)/shard_map/ppermute | solution.py:1050
  274.7 32.4 %collective-permute-start.2 = (bf16[2,2,224,768]{3,2,1,0:T(8,128)(2,1)S(1)}, bf16[2,2,224,768]{3,2,1,0:T(8,128)(2,1)S(1)}, u32[]{:S(2)}, u32[]{:S(2)}) collective-permute-start(bf16[2,2,224,768]{3,2,1,0:T(8,128)(2,1)S(1)} %get-tuple-element.112.refs_18_), channel_id=1, source_target_pairs={{0,8},{4,12},{8,0},{12,4},{16,24},{20,28},{24,16},{28,20},{1,9},{5... | collective-permute-start | bytes 4128776 | tf_op jit(solution)/shard_map/ppermute | solution.py:1050
  307.1 1.3 copy-start.12
  308.5 1.3 copy-start.14
  311.1 20.0 %collective-permute-start.3 = (bf16[2,224,768]{2,1,0:T(8,128)(2,1)S(1)}, bf16[2,224,768]{2,1,0:T(8,128)(2,1)S(1)}, u32[]{:S(2)}, u32[]{:S(2)}) collective-permute-start(bf16[2,224,768]{2,1,0:T(8,128)(2,1)S(1)} %get-tuple-element.122.refs_17_), channel_id=1, source_target_pairs={{0,8},{4,12},{8,0},{12,4},{16,24},{20,28},{24,16},{28,20},{1,9},{5... | collective-permute-start | bytes 2064392 | tf_op jit(solution)/shard_map/ppermute | solution.py:1050
  312.6 18.4 %collective-permute-start.4 = (bf16[2,224,768]{2,1,0:T(8,128)(2,1)S(1)}, bf16[2,224,768]{2,1,0:T(8,128)(2,1)S(1)}, u32[]{:S(2)}, u32[]{:S(2)}) collective-permute-start(bf16[2,224,768]{2,1,0:T(8,128)(2,1)S(1)} %get-tuple-element.123.refs_18_), channel_id=1, source_target_pairs={{0,16},{4,20},{8,24},{12,28},{16,0},{20,4},{24,8},{28,12},{1,17},{... | collective-permute-start | bytes 2064392 | tf_op jit(solution)/shard_map/ppermute | solution.py:1050
  332.9 1.4 copy-start.5
  334.3 1.1 copy-start.8
  335.4 1.1 copy-start.10
  336.5 1.0 copy-start.17
  355.6 0.9 copy-start.1
  356.5 0.9 copy-start.2
  357.4 0.9 copy-start.3
  436.9 2.7 copy-start.21
  439.6 1.2 copy-start.25
  439.6 1.8 copy-start.24
  439.6 2.5 copy-start.23
  439.6 3.1 copy-start.27
  439.6 3.7 copy-start.29
  439.6 4.2 copy-start.22
  439.6 4.8 %copy-start.28 = (f32[2,96]{1,0:T(2,128)S(1)}, f32[2,96]{1,0:T(2,128)}, u32[]{:S(2)}) copy-start(f32[2,96]{1,0:T(2,128)} %get-tuple-element.181) | copy-start | bytes 2308
  439.6 5.4 %copy-start.26 = (f32[4,96]{1,0:T(4,128)S(1)}, f32[4,96]{1,0:T(4,128)}, u32[]{:S(2)}) copy-start(f32[4,96]{1,0:T(4,128)} %get-tuple-element.182) | copy-start | bytes 4612
Sparse Core Ops, SparseCore 0:
  333.9 31.0 reduce-scatter.1

commit v7 on v6

--- a/solution.py
+++ b/solution.py
@@ -115,7 +115,7 @@
         out_shape=[jax.ShapeDtypeStruct((R,F),bf),jax.ShapeDtypeStruct((R,F),f32),jax.ShapeDtypeStruct((2*pairs,R,L),bf)],
         scratch_shapes=[pltpu.VMEM((2,C,R),bf),pltpu.VMEM((R,L),bf),pltpu.VMEM((L,128),bf),pltpu.VMEM((2,C,R+C),f32),
                         pltpu.VMEM((2,B,L),f32),pltpu.VMEM((2,B,L+B),f32),pltpu.VMEM((2,B,128),f32)],
-        compiler_params=pltpu.CompilerParams(vmem_limit_bytes=48*1024*1024,dimension_semantics=("arbitrary","arbitrary")),
+        compiler_params=pltpu.CompilerParams(vmem_limit_bytes=60*1024*1024,dimension_semantics=("arbitrary","arbitrary")),
         cost_estimate=pl.CostEstimate(flops=flops,bytes_accessed=2*pairs*R*L*2+10*L*F,transcendentals=2*pairs*R*L),
         name="attend",
     )(mask,q,k,v,kt,qr)
@@ -232,9 +232,9 @@
         for copy in self.copies:
             copy.wait()
 
-def feed_kernel(R,D,tiles,per,rows_in,own_rows,ctx_ref,tok_ref,og_ref,scale_ref,wo_ref,late_ref,bias_ref,gain_ref,shift_ref,
+def feed_kernel(R,D,tiles,per,rows_in,own_rows,ctx_ref,tok_ref,og_ref,scale_ref,wl_ref,late_ref,bias_ref,gain_ref,shift_ref,
                 res_ref,dres_ref,do_ref,sums_ref,bsum_ref,keep_ref,give_ref,
-                u1_ref,r1_ref,low_ref,acc_ref,pre_ref,gated_ref,gp_ref,dfeed_ref,stage_ref,tail_ref,datt_ref,sem):
+                u1_ref,r1_ref,low_ref,acc_ref,pre_ref,gated_ref,gp_ref,dfeed_ref,stage_ref,tail_ref,datt_ref,wf_ref,wo_ref,sem):
     step=pl.program_id(0)
     core=lax.axis_index("dp")%2
     pairs=per//2
@@ -244,7 +244,7 @@
         def body(i,c):
             f(pl.ds(pl.multiple_of(i*CH,CH),CH))
             return c
-        lax.fori_loop(0,R//CH,body,0)
+        lax.fori_loop(0,R//CH,body,0,unroll=4)
     mean=lambda x: jnp.mean(x,axis=1,keepdims=True)
     gain=lambda i: gain_ref[i:i+1,:]
     shift=lambda i: shift_ref[i:i+1,:]
@@ -253,6 +253,9 @@
     @pl.when(step==0)
     def _():
         sums_ref[...]=jnp.zeros_like(sums_ref)
+        for p in range(D//own_rows):
+            wf_ref[p*own_rows:(p+1)*own_rows,:]=wl_ref[p].astype(f32)[0:own_rows]
+        wo_ref[...]=wf_ref[...].astype(bf)
         acc_ref[...]=dot_nn(ctx_ref[...],wo_ref[...])
         def norm(at):
             v=tok_ref[at,:].astype(f32)+acc_ref[at,:]+shift(0)
@@ -346,7 +349,7 @@
             out(k,slot).wait()
             last.wait()
 
-def feed(ctx,tokens,out_grad,scale,out_rows,late,bias,gain,shift,rows_in,own_rows,tiles=4):
+def feed(ctx,tokens,out_grad,scale,late,bias,gain,shift,rows_in,own_rows,tiles=4):
     R,D=ctx.shape
     n,rows_late,_=late.shape
     per=n//tiles
@@ -355,7 +358,7 @@
     vm=lambda s: pl.BlockSpec(s,lambda i: (0,)*len(s))
     return pl.pallas_call(functools.partial(feed_kernel,R,D,tiles,per,rows_in,own_rows),
         grid=(2*tiles,),
-        in_specs=[vm((R,D)),vm((R,D)),vm((R,D)),vm((R,D)),vm((D,D)),
+        in_specs=[vm((R,D)),vm((R,D)),vm((R,D)),vm((R,D)),pl.BlockSpec((n,tail,D),lambda i:(0,2*rows_in//tail,0)),
                   pl.BlockSpec((per,rows_late,D),lambda i:(lax.rem(i,tiles),0,0)),
                   pl.BlockSpec((1,1,width),lambda i:(lax.rem(i,tiles),0,0)),vm((2,D)),vm((4,D))],
         out_specs=[vm((R,D)),vm((R,D)),vm((R,D)),vm((8,D)),pl.BlockSpec((1,1,width),lambda i:(jnp.maximum(i-tiles,0),0,0)),
@@ -365,12 +368,12 @@
                    jax.ShapeDtypeStruct((n//2,rows_late,D),bf),jax.ShapeDtypeStruct((n//2,rows_late,D),bf)],
         scratch_shapes=[pltpu.VMEM((R,D),f32),pltpu.VMEM((R,128),f32),pltpu.VMEM((R,D),bf),pltpu.VMEM((R,D),f32),
                         pltpu.VMEM((R,width),f32),pltpu.VMEM((tiles,R,width),bf),pltpu.VMEM((tiles,R,width),bf),
-                        pltpu.VMEM((R,D),bf),pltpu.VMEM((2,per//2,2,2*rows_in,D),bf),pltpu.VMEM((n//2,2,tail,D),bf),pltpu.VMEM((R,D),bf),
+                        pltpu.VMEM((R,D),bf),pltpu.VMEM((2,per//2,2,2*rows_in,D),bf),pltpu.VMEM((n//2,2,tail,D),bf),pltpu.VMEM((R,D),bf),pltpu.VMEM((D,D),f32),pltpu.VMEM((D,D),bf),
                         pltpu.SemaphoreType.DMA((3,2))],
         compiler_params=pltpu.CompilerParams(vmem_limit_bytes=58*1024*1024,dimension_semantics=("arbitrary",)),
         cost_estimate=pl.CostEstimate(flops=2*R*D*n*rows_in*6+6*R*D*D,bytes_accessed=4*n*rows_late*D+20*R*D,transcendentals=2*R*n*rows_in),
         name="feed",
-    )(ctx,tokens,out_grad,scale,out_rows,late,bias,gain,shift)
+    )(ctx,tokens,out_grad,scale,late,late,bias,gain,shift)
 
 MESH = pl.DeviceIdType.MESH
 ANY = pl.BlockSpec(memory_space=pl.ANY)
@@ -503,11 +506,11 @@
     return -(-n // 8) * 8
 
 def begin_kernel(n_t, n_dp, own, part, cols, inner, tiles, L,
-                 tok_ref, wq_ref, wk_ref, wv_ref, rel_ref, qkvb_ref, ffb_ref, gains_ref, shifts_ref, ahead_ref, back_ref, late_ref,
+                 tok_ref, wq_ref, wk_ref, wv_ref, rel_ref, qkvb_ref, ffb_ref, gains_ref, shifts_ref, ahead_ref, back_ref, fin_ref, fout_ref, wo_ref,
                  q_out, k_out, v_out, krel_out, qrel_out, kt_out, qr_out, toks_out, w_out, ox_out, oy_out, table_out, late_all,
                  ibias_ref, gain_ref, shift_ref,
                  toks, packs, pack, packf, wf, w, kb, vb, qb, krel, qrel, kt, qr, table, tableb, miscf, ox, ox_tall, oy_tall,
-                 tok_send, tok_recv, z_send, z_recv, x_send, x_recv, out_sem, lz_send, lz_recv, lx_send, lx_recv, lc_send, lc_recv):
+                 tok_send, tok_recv, z_send, z_recv, x_send, x_recv, out_sem, lz_send, lz_recv, lx_send, lx_recv, lc_send, lc_recv, late_ref, latef):
     at = Place(n_t, n_dp)
     t = at.t
     R, D = tok_ref.shape
@@ -531,6 +534,12 @@
     for i in range(4):
         packf[misc + 1:misc + 2, 256 + 128 * i:256 + 128 * i + cols] = shifts_ref[i:i + 1, :].astype(f32)
     pack[...] = packf[...].astype(bf)
+    latef[...] = jnp.zeros_like(latef)
+    at_row = 0
+    for ref in (fin_ref, fout_ref, wo_ref):
+        latef[at_row:at_row + ref.shape[0], :] = ref[...].astype(f32)
+        at_row += ref.shape[0]
+    late_ref[...] = latef[...].astype(bf)
 
     meet(at.peers())
     copies = []
@@ -697,7 +706,7 @@
     late.drain()
     tokens.drain()
 
-def begin(tokens, w_query, w_key, w_value, rel_table, qkv_bias, ff_bias, gains, shifts, ahead, back, late, n_t, n_dp, tiles):
+def begin(tokens, w_query, w_key, w_value, rel_table, qkv_bias, ff_bias, gains, shifts, ahead, back, w_ff_in, w_ff_out, w_out, n_t, n_dp, tiles):
     R, D = tokens.shape
     L = ahead.shape[1] // 2
     W = L + R
@@ -706,25 +715,27 @@
     n_all = n_t * n_dp
     width = n_all * inner // tiles
     PR = -(-(3 * eight(own) + eight(part) + 8) // 16) * 16
+    LR = -(-(2 * w_ff_in.shape[0] + own) // 16) * 16
     bits = (n_dp // 2).bit_length() - 1
     low = bits // 2
     S = jax.ShapeDtypeStruct
     big = [(R, D), (L, D), (L, D), (NB, D), (NB, D), (W, D), (W, D), (n_t, R, D), (3, D, D), (W, NB), (W, NB), (NB, D),
-           (n_t, 2**(bits - low), 2**low, 2, late.shape[0], D)]
+           (n_t, 2**(bits - low), 2**low, 2, LR, D)]
     v = lambda s, t=bf: pltpu.VMEM(s, t)
     dma = lambda *s: pltpu.SemaphoreType.DMA(s)
     return pl.pallas_call(
         functools.partial(begin_kernel, n_t, n_dp, own, part, cols, inner, tiles, L),
         out_shape=[S(s, bf) for s in big] + [S((tiles, 1, width), f32), S((2, D), f32), S((4, D), f32)],
-        in_specs=[VM] * 11 + [ANY], out_specs=[ANY] * len(big) + [VM] * 3,
+        in_specs=[VM] * 14, out_specs=[ANY] * len(big) + [VM] * 3,
         scratch_shapes=[v((n_t, R, D)), v((n_t, 2**(bits - low), 2**low, 2, PR, D)), v((PR, D)), v((PR, D), f32), v((D, D), f32),
                         v((3, D, D)), v((n_t, R, D)), v((n_t, R, D)), v((R, D)), v((NB, D)), v((NB, D)), v((W, D)), v((W, D)),
                         v((NB, D), f32), v((NB, D)), v((2, n_all, D), f32), v((NB, W)), v((W, NB)), v((W, NB)),
                         dma(2, n_t - 1, 2), dma(2, n_t - 1, 2), dma(2, n_t - 1, 1), dma(2, n_t - 1, 1), dma(2, bits + 1), dma(2, bits + 1),
-                        dma(11 + 3 * n_t), dma(2, n_t - 1, 1), dma(2, n_t - 1, 1), dma(2, max(bits, 1)), dma(2, max(bits, 1)), dma(2, bits + 1), dma(2, bits + 1)],
+                        dma(11 + 3 * n_t), dma(2, n_t - 1, 1), dma(2, n_t - 1, 1), dma(2, max(bits, 1)), dma(2, max(bits, 1)), dma(2, bits + 1), dma(2, bits + 1),
+                        v((LR, D)), v((LR, D), f32)],
         compiler_params=pltpu.CompilerParams(collective_id=0, has_side_effects=True, vmem_limit_bytes=58 * 1024 * 1024),
         name="begin",
-    )(tokens, w_query, w_key, w_value, rel_table, qkv_bias, ff_bias, gains, shifts, ahead, back, late)
+    )(tokens, w_query, w_key, w_value, rel_table, qkv_bias, ff_bias, gains, shifts, ahead, back, w_ff_in, w_ff_out, w_out)
 
 def finish_kernel(n_t, n_dp, own, rel_rows, cols, inner, tiles,
                   dq_in, dk_in, dv_in, tok_in, toks_in, w_in, table_in, dqr_in, dkr_in, dres_in, sums_ref, bsum_ref,
@@ -788,10 +799,7 @@
     l_w.wait()
     tok_acc[0] = partial(0).astype(bf)
     send_token(0)
-    blocks = [None] * n_t
-    tok_own[...] = partial(1).astype(bf)
-
-    for s in range(2, n_t):
+    for s in range(1, n_t):
         for copy in l_kv[s]:
             copy.wait()
     l_kv = [()] * n_t
@@ -822,15 +830,6 @@
     def padded(x, n):
         return jnp.concatenate([x, jnp.zeros((n - x.shape[0], D), f32)], axis=0) if n > x.shape[0] else x
 
-    for p, s in enumerate(slots):
-        dp = p % n_dp
-        miscs[8 * p:8 * p + 1, 0:512] = m0[p:p + 1, :]
-        miscs[8 * p + 1:8 * p + 2, :] = m1[dp:dp + 1, :]
-        pieces = [padded(g[i, p * own:p * own + own, :], S) for i in range(3)]
-        pieces += [miscs[8 * p:8 * p + 8, :], padded(relf[dp * rel_rows:dp * rel_rows + rel_rows, :], S3)]
-        whole = padded(jnp.concatenate(pieces, axis=0), PR)
-        pack[s[0], s[1], s[2], s[3]] = whole.astype(bf)
-
     parts = at.parts()
     hs = range(len(parts))
     per = n_t // len(parts)
@@ -875,8 +874,17 @@
                 x, y = acc[h * per + a, u0 + u, d0 + d], buf[a, u, d]
             acc[h * per + a, u0 + u, d0 + d] = (x.astype(f32) + y.astype(f32)).astype(bf)
 
-    for h in hs:
-        start(h, 0)
+    for p, s in enumerate(slots):
+        dp = p % n_dp
+        miscs[8 * p:8 * p + 1, 0:512] = m0[p:p + 1, :]
+        miscs[8 * p + 1:8 * p + 2, :] = m1[dp:dp + 1, :]
+        pieces = [padded(g[i, p * own:p * own + own, :], S) for i in range(3)]
+        pieces += [miscs[8 * p:8 * p + 8, :], padded(relf[dp * rel_rows:dp * rel_rows + rel_rows, :], S3)]
+        whole = padded(jnp.concatenate(pieces, axis=0), PR)
+        pack[s[0], s[1], s[2], s[3]] = whole.astype(bf)
+        if (p + 1) % (per * n_dp) == 0:
+            start(p // (per * n_dp), 0)
+    tok_own[...] = partial(1).astype(bf)
     sent = 1
     if n_t > 2:
         send_token(1)
@@ -1020,39 +1028,37 @@
     back = jnp.concatenate([rel_bucket[::-1], none])[None]
     late_rows = w_ff_in.shape[0]
     even = late_rows % 16 == 0 and own_rows % 8 == 0
-    late = jnp.concatenate([w_ff_in, w_ff_out, w_out], axis=0)
-    late_own = late.shape[0]
-    late = jnp.pad(late, ((0, -late_own % 16), (0, 0)))
+    late_own = 2 * late_rows + own_rows
+    late_all_rows = late_own + -late_own % 16
     (query, key, value, key_rel, query_rel, key_table, query_table, gathered, weights, pick_x, pick_y, table,
      late_all, inner_bias, gain, shift) = begin(tokens, w_query, w_key, w_value, rel_table, qkv_bias, ff_bias.reshape(1, -1), gains, shifts,
-                                      ahead, back, late, n_t, n_dp, TILES)
+                                      ahead, back, w_ff_in, w_ff_out, w_out, n_t, n_dp, TILES)
     gathered = gathered.reshape(L, D)
     late_all = late_all.reshape(n_all, -1, D)
     cut = lambda x, at, n: x[:, at:at + n].reshape(n_all * n, D)
-    out_rows = cut(late_all, 2 * late_rows, own_rows)
     groups = n_all if even else GROUPS
     group_rows, group_own = n_all * late_rows // groups, D // groups
     if not even:
-        sections = [cut(late_all, 0, late_rows), cut(late_all, late_rows, late_rows)]
-        late_all = jnp.concatenate([x.reshape(groups, group_rows, D) for x in sections]
-                                   + [jnp.zeros((groups, -(-group_own // 16) * 16, D), bf)], axis=1)
+        sections = [cut(late_all, 0, late_rows), cut(late_all, late_rows, late_rows), cut(late_all, 2 * late_rows, own_rows)]
+        late_all = jnp.concatenate([x.reshape(groups, -1, D) for x in sections]
+                                   + [jnp.zeros((groups, -group_own % 16, D), bf)], axis=1)
     mask = jnp.where(jnp.arange(L, dtype=jnp.int32) < lengths[0], 0.0, -1e9).astype(bf)
     mask = jnp.broadcast_to(mask[:, None], (L, 128))
 
     context, scale, shares = attention_forward(query, key, value, key_table, query_table, mask)
     layer_result_rows, d_resid_one, d_scaled, sums, bias_sums, keep, give = feed(
-        context, tokens, out_grad, scale, out_rows, late_all, inner_bias, gain, shift, group_rows, group_own)
+        context, tokens, out_grad, scale, late_all, inner_bias, gain, shift, group_rows, group_own)
     back_args = (query, key, value, d_scaled, context, shares, key_rel, query_rel, pick_x, pick_y)
     pairs = D // 128
-    if even and n_dp == 8 and n_t % 2 == 0 and pairs >= 4:
+    if even and n_dp == 8 and n_t % 2 == 0 and pairs >= 6:
         dp = lax.axis_index("dp")
         place = jnp.stack([dp // 4, dp // 2 % 2]).astype(jnp.int32)
         swap = lambda x, mask: lax.ppermute(x, "dp", [(i, i ^ mask) for i in range(n_dp)])
-        shape = (n_t, 2, 2, late.shape[0], D)
+        shape = (n_t, 2, 2, late_all_rows, D)
         keep, give = keep.reshape(shape), give.reshape(shape)
         got = swap(give, 1)
         half = n_t // 2
-        *grads, keep = attention_backward(*back_args, p0=0, count=pairs - 4, through=[keep])
+        *grads, keep = attention_backward(*back_args, p0=0, count=pairs - 5, through=[keep])
         stay_one, away_one, stay_two, away_two = fold(
             "fold", (half, 2), place,
             [(keep, got, lambda i, j, s: (i, s[0], j)), (keep, got, lambda i, j, s: (i, 1 - s[0], j)),
@@ -1060,7 +1066,7 @@
             [(half, 2)] * 4, [lambda i, j, s: (i, j)] * 4)
         got_one, got_two = swap(away_one, 4), swap(away_two, 2)
         *grads, stay_one, stay_two = attention_backward(
-            *back_args, p0=pairs - 4, count=2, before=grads, after=[away_one, away_two], through=[stay_one, stay_two])
+            *back_args, p0=pairs - 5, count=2, before=grads, after=[away_one, away_two], through=[stay_one, stay_two])
         stay_one, away_one, stay_two, away_two = fold(
             "fold", (half,), place,
             [(stay_one, got_one, lambda i, s: (i, s[1])), (stay_one, got_one, lambda i, s: (i, 1 - s[1])),
@@ -1068,13 +1074,13 @@
             [(half,)] * 4, [lambda i, s: (i,)] * 4)
         got_one, got_two = swap(away_one, 2), swap(away_two, 4)
         *grads, stay_one, stay_two = attention_backward(
-            *back_args, p0=pairs - 2, count=1, before=grads, after=[away_one, away_two], through=[stay_one, stay_two])
+            *back_args, p0=pairs - 3, count=1, before=grads, after=[away_one, away_two], through=[stay_one, stay_two])
         column = jnp.concatenate(fold(
             "fold", (half,), place,
             [(stay_one, got_one, lambda i, s: (i,)), (stay_two, got_two, lambda i, s: (i,))],
             [(half,)] * 2, [lambda i, s: (i,)] * 2), axis=0)
         late_sum = lax.psum_scatter(column, "tensor", scatter_dimension=0, tiled=True)[0]
-        grads = attention_backward(*back_args, p0=pairs - 1, count=1, before=grads, after=[column])
+        grads = attention_backward(*back_args, p0=pairs - 2, count=2, before=grads, after=[column])
     else:
         grads = attention_backward(*back_args)
         core = lax.axis_index("dp") % 2
@@ -1085,7 +1091,7 @@
             late_grad = jnp.concatenate([
                 parted(late_grad[:, :group_rows]), parted(late_grad[:, group_rows:2 * group_rows]),
                 parted(late_grad[:, 2 * group_rows:2 * group_rows + group_own]),
-                jnp.zeros((n_all, late.shape[0] - late_own, D), bf)], axis=1)
+                jnp.zeros((n_all, late_all_rows - late_own, D), bf)], axis=1)
         late_sum = lax.psum_scatter(late_grad, ALL, scatter_dimension=0, tiled=True)[0]
     d_query, d_key, d_value, d_key_rel, d_query_rel = grads
     late_sum = late_sum.astype(f32)

time: 461 us -> 455 us (0.987)
  the two profiles are of different devices: /device:TPU:26 before, /device:TPU:13 now
where the time goes in v7:
time: 455 us; the launch traced here: 446 us
  Pallas kernels  397 us (87%)
  local copies, waits for them, and re-layouts  27.8 us (6%)
  between operations  15.4 us (3%)
    pallas_call x1, Pallas kernels, begin(): pl.pallas_call(functools.partial(begin_kernel, n_t, n_dp, own, part, cols...  102 us
    pallas_call x4, Pallas kernels, attention_backward(): pl.pallas_call(kernel, grid=(count, 2), in_specs=specs + [pl.BlockSpec(me...  99.8 us
    pallas_call x1, Pallas kernels, finish(): pl.pallas_call(functools.partial(finish_kernel, n_t, n_dp, own, rel_rows,...  80.2 us
    pallas_call x1, Pallas kernels, attention_forward(): pl.pallas_call(functools.partial(fwd_kernel, R, L, B, C), grid=(pairs, 2)...  64.6 us
    pallas_call x1, Pallas kernels, feed(): pl.pallas_call(functools.partial(feed_kernel, R, D, tiles, per, rows_in,...  43.5 us
    unnamed x68, local copies, waits for them, and re-layouts  24.3 us
  transfers between devices with their start and end apart: 6, of which 0 were waited for; matrix products, arithmetic and copies ran while one was open for 0% of the time, Pallas kernels for 40%

profile of v7, /device:TPU:13, one launch (start us, length us, event | category | flops | bytes accessed | tf_op | source)
XLA Modules:
  0.0 446.0 jit_solution(12003430896319549401)
XLA Ops:
  7.2 0.0 reduce-scatter.2.cloned.1.call-start
  7.9 0.8 reverse
  8.7 0.1 slice.30
  8.7 1.4 pad_add_fusion
  10.2 101.9 %begin.1 = (bf16[512,768]{1,0:T(8,128)(2,1)}, bf16[2048,768]{1,0:T(8,128)(2,1)}, bf16[2048,768]{1,0:T(8,128)(2,1)}, bf16[256,768]{1,0:T(8,128)(2,1)}, bf16[256,7...) custom-call(bf16[512,768]{1,0:T(8,128)(2,1)} %tok_in.1, ...), custom_call_target="tpu_custom_call" | custom-call | tf_op jit(solution)/shard_map/begin/pallas_call | solution.py:726
  112.1 1.1 broadcast_in_dim.22.mask_ref
  113.2 64.6 %attend.1 = (bf16[512,768]{1,0:T(8,128)(2,1)}, f32[512,768]{1,0:T(8,128)}, bf16[12,512,2048]{2,1,0:T(8,128)(2,1)}) custom-call(bf16[2048,128]{1,0:T(8,128)(2,1)} %broadcast_in_dim.22.mask_ref, bf16[512,768]{1,0:T(8,128)(2,1)} %get-tuple-element.83.q_ref.refs_0_, bf16[2048,768]{1,0:T(8,128)(2,1)} %get-tuple-element.84.k_ref.refs_1_, ...), custom_call_target="tpu_custom_call" | custom-call | flops 12884901888 | bytes 40894464 | tf_op jit(solution)/shard_map/attend/pallas_call | solution.py:111
  177.8 43.5 %feed.1 = (bf16[512,768]{1,0:T(8,128)(2,1)}, f32[512,768]{1,0:T(8,128)}, bf16[512,768]{1,0:T(8,128)(2,1)}, f32[8,768]{1,0:T(8,128)}, f32[4,1,768]{2,1,0:T(1,128)...) custom-call(bf16[512,768]{1,0:T(8,128)(2,1)} %get-tuple-element.88.ctx_ref.refs_4_, ...), custom_call_target="tpu_custom_call" | custom-call | flops 16307453952 | bytes 29884416 | tf_op jit(solution)/shard_map/feed/pallas_call | solution.py:359
  221.3 0.5 collective-permute-start
  221.8 0.1 pad_add_fusion.2.place_ref
  221.9 1.1 copy-done.6
  223.0 1.1 copy-done.8
  224.2 1.0 copy-done.15
  225.2 17.9 %attend_back.4 = (bf16[512,768]{1,0:T(8,128)(2,1)S(1)}, bf16[2048,768]{1,0:T(8,128)(2,1)}, bf16[2048,768]{1,0:T(8,128)(2,1)}, f32[256,768]{1,0:T(8,128)S(1)}, f3...) custom-call(bf16[512,768]{1,0:T(8,128)(2,1)S(1)} %copy-done.4, ...), custom_call_target="tpu_custom_call", output_to_operand_aliasing={{5}: (10, {})} | custom-call | flops 4294967296 | bytes 9437184 | tf_op jit(solution)/shard_map/attend_back/pallas_call | solution.py:197
  243.1 0.0 collective-permute-done.refs_1_.refs_3_.refs_5_.refs_7_
  243.1 2.6 copy-done
  245.7 4.4 fold.3
  250.1 0.0 copy-start.10
  250.1 1.1 copy-done.10
  251.1 1.1 copy-done.12
  252.2 0.6 collective-permute-start.1
  252.8 0.9 collective-permute-start.2
  253.7 0.0 copy-done.17
  253.7 0.0 copy-done.18
  253.7 31.8 %attend_back.5 = (bf16[512,768]{1,0:T(8,128)(2,1)S(1)}, bf16[2048,768]{1,0:T(8,128)(2,1)}, bf16[2048,768]{1,0:T(8,128)(2,1)}, f32[256,768]{1,0:T(8,128)S(1)}, f3...) custom-call(bf16[512,768]{1,0:T(8,128)(2,1)S(1)} %copy-done.4, ...), custom_call_target="tpu_custom_call", output_to_operand_aliasing={{0}: (10, {}), {1}: (11, {}), {2}: (12, {}), {3}: (13, {}),... | custom-call | flops 8589934592 | bytes 18874368 | tf_op jit(solution)/shard_map/attend_back/pallas_call | solution.py:197
  285.6 0.0 collective-permute-done.1.refs_1_.refs_3_
  285.6 0.0 collective-permute-done.2.refs_5_.refs_7_
  285.6 0.0 copy-start.11
  285.6 1.3 copy-done.11
  286.9 1.3 copy-done.13
  288.3 1.2 fold.4
  289.5 1.3 collective-permute-start.3
  290.8 0.3 collective-permute-start.4
  291.0 17.8 %attend_back.6 = (bf16[512,768]{1,0:T(8,128)(2,1)S(1)}, bf16[2048,768]{1,0:T(8,128)(2,1)}, bf16[2048,768]{1,0:T(8,128)(2,1)}, f32[256,768]{1,0:T(8,128)S(1)}, f3...) custom-call(bf16[512,768]{1,0:T(8,128)(2,1)} %get-tuple-element.83.q, ...), custom_call_target="tpu_custom_call", output_to_operand_aliasing={{0}: (10, {}), {1}: (11, {}), {2}: (12, {}), {3}: (13, {}),... | custom-call | flops 4294967296 | bytes 9437184 | tf_op jit(solution)/shard_map/attend_back/pallas_call | solution.py:197
  308.9 0.0 collective-permute-done.3.refs_1_
  308.9 0.0 collective-permute-done.4.refs_3_
  308.9 0.9 fold.5
  309.8 0.9 constant_dynamic-update-slice_fusion.1
  310.7 0.9 constant_dynamic-update-slice_fusion.refs_15_
  311.6 0.0 reduce-scatter.2.cloned.1.call-update
  311.6 1.1 copy-done.7
  312.8 1.1 copy-done.9
  313.9 1.0 copy-done.16
  314.9 32.2 %attend_back.7 = (bf16[512,768]{1,0:T(8,128)(2,1)S(1)}, bf16[2048,768]{1,0:T(8,128)(2,1)}, bf16[2048,768]{1,0:T(8,128)(2,1)}, f32[256,768]{1,0:T(8,128)S(1)}, f32[256,768]{1,0:T(8,128)S(1)}) custom-call(bf16[512,768]{1,0:T(8,128)(2,1)S(1)} %copy-done.5, ...), custom_call_target="tpu_custom_call", output_to_operand_aliasing={{0}: (10, {}), {1}: (11, {}), {2}: (12, {}), {3}: (13, {}),... | custom-call | flops 8589934592 | bytes 18874368 | tf_op jit(solution)/shard_map/attend_back/pallas_call | solution.py:197
  347.1 0.9 copy-done.1
  348.0 0.9 copy-done.2
  348.9 0.9 copy-done.3
  349.8 80.2 %finish.1 = (f32[512,768]{1,0:T(8,128)}, f32[24,768]{1,0:T(8,128)}, f32[24,768]{1,0:T(8,128)}, f32[24,768]{1,0:T(8,128)}, f32[32,768]{1,0:T(8,128)}, /*index=5*/...) custom-call(bf16[512,768]{1,0:T(8,128)(2,1)} %copy-done.1, bf16[4,512,768]{2,1,0:T(8,128)(2,1)} %bitcast.21, ...), custom_call_target="tpu_custom_call" | custom-call | tf_op jit(solution)/shard_map/finish/pallas_call | solution.py:957
  430.1 0.0 reduce-scatter.2.cloned.1.call-done
  430.1 1.1 convert_element_type.12
  431.3 0.6 slice_bitcast_fusion.2
  431.9 0.8 slice_bitcast_fusion
  432.8 1.1 copy.79
  433.9 0.0 copy-done.23
  433.9 0.6 copy.80
  434.5 0.6 copy.81
  435.2 0.0 copy-done.21
  435.2 0.6 copy.82
  435.8 0.6 copy.83
  436.4 0.5 copy.84
  436.9 0.0 copy-done.20
  436.9 0.6 copy.85
  437.6 0.6 copy.86
  438.1 0.6 copy.87
  (36 shorter events, 0.1 us)
Async XLA Ops:
  7.2 422.9 %reduce-scatter.2.cloned.1.call-start = ((), (), s32[]{:S(2)}) async-start(), calls=%async_computation.1 | async-start | bytes 1720320 | tf_op jit(solution)/shard_map/reduce_scatter | solution.py:1082
  177.8 44.1 %copy-start.4 = (bf16[512,768]{1,0:T(8,128)(2,1)S(1)}, bf16[512,768]{1,0:T(8,128)(2,1)}, u32[]{:S(2)}) copy-start(bf16[512,768]{1,0:T(8,128)(2,1)} %get-tuple-element.83.q_ref.refs_0_) | copy-start | bytes 2359300
  177.8 44.1 %copy-start.14 = (bf16[256,768]{1,0:T(8,128)(2,1)S(1)}, bf16[256,768]{1,0:T(8,128)(2,1)}, u32[]{:S(2)}) copy-start(bf16[256,768]{1,0:T(8,128)(2,1)} %get-tuple-element.97.refs_6_) | copy-start | bytes 1179652
  221.3 21.8 %collective-permute-start = (bf16[4,2,2,224,768]{4,3,2,1,0:T(8,128)(2,1)}, bf16[4,2,2,224,768]{4,3,2,1,0:T(8,128)(2,1)}, u32[]{:S(2)}, u32[]{:S(2)}) collective-permute-start(bf16[4,2,2,224,768]{4,3,2,1,0:T(8,128)(2,1)} %bitcast.29), channel_id=1, source_target_pairs={{0,4},{4,0},{8,12},{12,8},{16,20},{20,16},{24,28},{28,24},{1,5},{5... | collective-permute-start | bytes 16515080 | tf_op jit(solution)/shard_map/ppermute | solution.py:1056
  221.9 1.1 copy-start.6
  223.0 1.1 copy-start.8
  224.2 1.0 copy-start.15
  243.1 2.6 copy-start
  250.1 1.1 copy-start.10
  251.1 1.1 copy-start.12
  252.2 1.5 copy-start.17
  252.2 1.5 copy-start.18
  252.2 33.4 %collective-permute-start.1 = (bf16[2,2,224,768]{3,2,1,0:T(8,128)(2,1)S(1)}, bf16[2,2,224,768]{3,2,1,0:T(8,128)(2,1)S(1)}, u32[]{:S(2)}, u32[]{:S(2)}) collective-permute-start(bf16[2,2,224,768]{3,2,1,0:T(8,128)(2,1)S(1)} %get-tuple-element.111.refs_17_), channel_id=1, source_target_pairs={{0,16},{4,20},{8,24},{12,28},{16,0},{20,4},{24,8},{28,12},{1,17},{... | collective-permute-start | bytes 4128776 | tf_op jit(solution)/shard_map/ppermute | solution.py:1056
  252.8 32.7 %collective-permute-start.2 = (bf16[2,2,224,768]{3,2,1,0:T(8,128)(2,1)S(1)}, bf16[2,2,224,768]{3,2,1,0:T(8,128)(2,1)S(1)}, u32[]{:S(2)}, u32[]{:S(2)}) collective-permute-start(bf16[2,2,224,768]{3,2,1,0:T(8,128)(2,1)S(1)} %get-tuple-element.112.refs_18_), channel_id=1, source_target_pairs={{0,8},{4,12},{8,0},{12,4},{16,24},{20,28},{24,16},{28,20},{1,9},{5... | collective-permute-start | bytes 4128776 | tf_op jit(solution)/shard_map/ppermute | solution.py:1056
  285.6 1.3 copy-start.11
  286.9 1.3 copy-start.13
  289.5 19.4 %collective-permute-start.3 = (bf16[2,224,768]{2,1,0:T(8,128)(2,1)S(1)}, bf16[2,224,768]{2,1,0:T(8,128)(2,1)S(1)}, u32[]{:S(2)}, u32[]{:S(2)}) collective-permute-start(bf16[2,224,768]{2,1,0:T(8,128)(2,1)S(1)} %get-tuple-element.122.refs_17_), channel_id=1, source_target_pairs={{0,8},{4,12},{8,0},{12,4},{16,24},{20,28},{24,16},{28,20},{1,9},{5... | collective-permute-start | bytes 2064392 | tf_op jit(solution)/shard_map/ppermute | solution.py:1056
  290.8 18.1 %collective-permute-start.4 = (bf16[2,224,768]{2,1,0:T(8,128)(2,1)S(1)}, bf16[2,224,768]{2,1,0:T(8,128)(2,1)S(1)}, u32[]{:S(2)}, u32[]{:S(2)}) collective-permute-start(bf16[2,224,768]{2,1,0:T(8,128)(2,1)S(1)} %get-tuple-element.123.refs_18_), channel_id=1, source_target_pairs={{0,16},{4,20},{8,24},{12,28},{16,0},{20,4},{24,8},{28,12},{1,17},{... | collective-permute-start | bytes 2064392 | tf_op jit(solution)/shard_map/ppermute | solution.py:1056
  308.9 2.7 copy-start.5
  311.6 1.1 copy-start.7
  312.8 1.1 copy-start.9
  313.9 1.0 copy-start.16
  347.1 0.9 copy-start.1
  348.0 0.9 copy-start.2
  348.9 0.9 copy-start.3
  430.0 2.8 copy-start.19
  430.0 3.9 copy-start.23
  430.0 4.5 %copy-start.22 = (f32[24,768]{1,0:T(8,128)S(1)}, f32[24,768]{1,0:T(8,128)}, u32[]{:S(2)}) copy-start(f32[24,768]{1,0:T(8,128)} %get-tuple-element.173) | copy-start | bytes 221188
  430.0 5.1 %copy-start.21 = (f32[24,768]{1,0:T(8,128)S(1)}, f32[24,768]{1,0:T(8,128)}, u32[]{:S(2)}) copy-start(f32[24,768]{1,0:T(8,128)} %get-tuple-element.174) | copy-start | bytes 221188
  430.0 5.8 %copy-start.25 = (f32[3,24]{1,0:T(4,128)S(1)}, f32[3,24]{1,0:T(4,128)}, u32[]{:S(2)}) copy-start(f32[3,24]{1,0:T(4,128)} %get-tuple-element.176) | copy-start | bytes 868
  430.1 6.3 %copy-start.27 = (f32[1,96]{1,0:T(1,128)S(1)}, f32[1,96]{1,0:T(1,128)}, u32[]{:S(2)}) copy-start(f32[1,96]{1,0:T(1,128)} %get-tuple-element.149) | copy-start | bytes 1156
  430.1 6.8 %copy-start.20 = (f32[32,768]{1,0:T(8,128)S(1)}, f32[32,768]{1,0:T(8,128)}, u32[]{:S(2)}) copy-start(f32[32,768]{1,0:T(8,128)} %get-tuple-element.180) | copy-start | bytes 294916
  430.1 7.5 %copy-start.26 = (f32[2,96]{1,0:T(2,128)S(1)}, f32[2,96]{1,0:T(2,128)}, u32[]{:S(2)}) copy-start(f32[2,96]{1,0:T(2,128)} %get-tuple-element.181) | copy-start | bytes 2308
  430.1 8.0 %copy-start.24 = (f32[4,96]{1,0:T(4,128)S(1)}, f32[4,96]{1,0:T(4,128)}, u32[]{:S(2)}) copy-start(f32[4,96]{1,0:T(4,128)} %get-tuple-element.182) | copy-start | bytes 4612
Sparse Core Ops, SparseCore 0:
  311.7 34.0 reduce-scatter.1

commit v8 on v7

--- a/solution.py
+++ b/solution.py
@@ -204,7 +204,7 @@
         scratch_shapes=[pltpu.VMEM((R,L),bf),pltpu.VMEM((R,128),bf),pltpu.VMEM((R,128),bf),
                         pltpu.VMEM((R,128),f32),pltpu.VMEM((L,128),f32),pltpu.VMEM((L,128),f32),
                         pltpu.VMEM((R,128),f32),pltpu.VMEM((2,B,L),f32),pltpu.VMEM((2,B,L+B),bf),pltpu.VMEM((2,C,R),bf),pltpu.VMEM((2,C,R+C),bf)],
-        compiler_params=pltpu.CompilerParams(vmem_limit_bytes=48*1024*1024,dimension_semantics=("arbitrary","arbitrary")),
+        compiler_params=pltpu.CompilerParams(vmem_limit_bytes=(48 if before else 60)*1024*1024,dimension_semantics=("arbitrary","arbitrary")),
         cost_estimate=pl.CostEstimate(flops=flops,bytes_accessed=2*count*R*L*2+20*L*128*count,transcendentals=0),
         name="attend_back",
     )(*args,*extra)

time: 455 us -> 452 us (level)
    unnamed x68 -> x74, local copies, waits for them, and re-layouts: 24.3 us -> 21.1 us
  transfers between devices with their start and end apart: 6 -> 6, of which waited for: 0 -> 0; matrix products, arithmetic and copies ran while one was open for 0% -> 0% of each run, Pallas kernels for 40% -> 41%
where the time goes in v8:
time: 452 us; the launch traced here: 443 us
  Pallas kernels  397 us (88%)
  local copies, waits for them, and re-layouts  24.7 us (5%)
  between operations  15.5 us (3%)
    pallas_call x1, Pallas kernels, begin(): pl.pallas_call(functools.partial(begin_kernel, n_t, n_dp, own, part, cols...  102 us
    pallas_call x4, Pallas kernels, attention_backward(): pl.pallas_call(kernel, grid=(count, 2), in_specs=specs + [pl.BlockSpec(me...  100 us
    pallas_call x1, Pallas kernels, finish(): pl.pallas_call(functools.partial(finish_kernel, n_t, n_dp, own, rel_rows,...  80.2 us
    pallas_call x1, Pallas kernels, attention_forward(): pl.pallas_call(functools.partial(fwd_kernel, R, L, B, C), grid=(pairs, 2)...  64.6 us
    pallas_call x1, Pallas kernels, feed(): pl.pallas_call(functools.partial(feed_kernel, R, D, tiles, per, rows_in,...  43.4 us
    unnamed x74, local copies, waits for them, and re-layouts  21.1 us
  transfers between devices with their start and end apart: 6, of which 0 were waited for; matrix products, arithmetic and copies ran while one was open for 0% of the time, Pallas kernels for 41%

profile of v8, /device:TPU:13, one launch (start us, length us, event | category | flops | bytes accessed | tf_op | source)
XLA Modules:
  0.0 443.3 jit_solution(6135076026470961535)
XLA Ops:
  7.2 0.0 reduce-scatter.2.cloned.1.call-start
  7.9 0.8 reverse
  8.7 0.1 slice.30
  8.7 1.4 pad_add_fusion
  10.2 101.9 %begin.1 = (bf16[512,768]{1,0:T(8,128)(2,1)}, bf16[2048,768]{1,0:T(8,128)(2,1)}, bf16[2048,768]{1,0:T(8,128)(2,1)}, bf16[256,768]{1,0:T(8,128)(2,1)}, bf16[256,7...) custom-call(bf16[512,768]{1,0:T(8,128)(2,1)} %tok_in.1, ...), custom_call_target="tpu_custom_call" | custom-call | tf_op jit(solution)/shard_map/begin/pallas_call | solution.py:726
  112.1 1.1 broadcast_in_dim.22.mask_ref
  113.2 64.6 %attend.1 = (bf16[512,768]{1,0:T(8,128)(2,1)}, f32[512,768]{1,0:T(8,128)}, bf16[12,512,2048]{2,1,0:T(8,128)(2,1)}) custom-call(bf16[2048,128]{1,0:T(8,128)(2,1)} %broadcast_in_dim.22.mask_ref, bf16[512,768]{1,0:T(8,128)(2,1)} %get-tuple-element.83.q_ref.refs_0_, bf16[2048,768]{1,0:T(8,128)(2,1)} %get-tuple-element.84.k_ref.refs_1_, ...), custom_call_target="tpu_custom_call" | custom-call | flops 12884901888 | bytes 40894464 | tf_op jit(solution)/shard_map/attend/pallas_call | solution.py:111
  177.9 43.4 %feed.1 = (bf16[512,768]{1,0:T(8,128)(2,1)}, f32[512,768]{1,0:T(8,128)}, bf16[512,768]{1,0:T(8,128)(2,1)}, f32[8,768]{1,0:T(8,128)}, f32[4,1,768]{2,1,0:T(1,128)...) custom-call(bf16[512,768]{1,0:T(8,128)(2,1)} %get-tuple-element.88.ctx_ref.refs_4_, ...), custom_call_target="tpu_custom_call" | custom-call | flops 16307453952 | bytes 29884416 | tf_op jit(solution)/shard_map/feed/pallas_call | solution.py:359
  221.3 0.5 collective-permute-start
  221.8 0.1 pad_add_fusion.2.place_ref
  221.8 18.2 %attend_back.4 = (bf16[512,768]{1,0:T(8,128)(2,1)}, bf16[2048,768]{1,0:T(8,128)(2,1)}, bf16[2048,768]{1,0:T(8,128)(2,1)}, f32[256,768]{1,0:T(8,128)}, f32[256,76...) custom-call(bf16[512,768]{1,0:T(8,128)(2,1)} %get-tuple-element.83.q_ref.refs_0_, ...), custom_call_target="tpu_custom_call", output_to_operand_aliasing={{5}: (10, {})} | custom-call | flops 4294967296 | bytes 9437184 | tf_op jit(solution)/shard_map/attend_back/pallas_call | solution.py:197
  240.1 0.0 collective-permute-done.refs_1_.refs_3_.refs_5_.refs_7_
  240.1 2.6 copy-done
  242.7 4.7 %fold.3 = (bf16[2,2,224,768]{3,2,1,0:T(8,128)(2,1)S(1)}, bf16[2,2,224,768]{3,2,1,0:T(8,128)(2,1)S(1)}, bf16[2,2,224,768]{3,2,1,0:T(8,128)(2,1)S(1)}, bf16[2,2,224,768]{3,2,1,0:T(8,128)(2,1)S(1)}) custom-call(s32[2]{0:T(128)S(1)} %pad_add_fusion.2.place_ref, bf16[4,2,2,224,768]{4,3,2,1,0:T(8,128)(2,1)S(1)} %copy-done, ...), custom_call_target="tpu_custom_call" | custom-call | bytes 16515072 | tf_op jit(solution)/shard_map/fold/pallas_call | solution.py:986
  247.4 0.0 copy-start.13
  247.4 1.1 copy-done.13
  248.4 1.1 copy-done.15
  249.5 0.5 collective-permute-start.1
  250.0 0.9 collective-permute-start.2
  250.9 0.0 copy-done.20
  250.9 0.1 copy-done.21
  251.1 0.0 copy-done.7
  251.1 0.0 copy-done.9
  251.1 0.0 copy-done.11
  251.1 0.0 copy-done.17
  251.1 0.0 copy-done.18
  251.1 31.9 %attend_back.5 = (bf16[512,768]{1,0:T(8,128)(2,1)S(1)}, bf16[2048,768]{1,0:T(8,128)(2,1)}, bf16[2048,768]{1,0:T(8,128)(2,1)}, f32[256,768]{1,0:T(8,128)S(1)}, f3...) custom-call(bf16[512,768]{1,0:T(8,128)(2,1)S(1)} %copy-done.7, ...), custom_call_target="tpu_custom_call", output_to_operand_aliasing={{0}: (10, {}), {1}: (11, {}), {2}: (12, {}), {3}: (13, {}),... | custom-call | flops 8589934592 | bytes 18874368 | tf_op jit(solution)/shard_map/attend_back/pallas_call | solution.py:197
  283.0 0.0 collective-permute-done.1.refs_1_.refs_3_
  283.0 0.0 collective-permute-done.2.refs_5_.refs_7_
  283.0 0.0 copy-start.14
  283.0 1.3 copy-done.14
  284.3 1.3 copy-done.16
  285.7 1.2 fold.4
  286.9 1.2 collective-permute-start.3
  288.1 0.3 collective-permute-start.4
  288.4 17.8 %attend_back.6 = (bf16[512,768]{1,0:T(8,128)(2,1)S(1)}, bf16[2048,768]{1,0:T(8,128)(2,1)}, bf16[2048,768]{1,0:T(8,128)(2,1)}, f32[256,768]{1,0:T(8,128)S(1)}, f3...) custom-call(bf16[512,768]{1,0:T(8,128)(2,1)} %get-tuple-element.83.q, ...), custom_call_target="tpu_custom_call", output_to_operand_aliasing={{0}: (10, {}), {1}: (11, {}), {2}: (12, {}), {3}: (13, {}),... | custom-call | flops 4294967296 | bytes 9437184 | tf_op jit(solution)/shard_map/attend_back/pallas_call | solution.py:197
  306.2 0.0 collective-permute-done.3.refs_1_
  306.2 0.0 collective-permute-done.4.refs_3_
  306.2 0.9 fold.5
  307.2 0.9 constant_dynamic-update-slice_fusion.1
  308.0 0.9 constant_dynamic-update-slice_fusion.refs_15_
  308.9 0.0 reduce-scatter.2.cloned.1.call-update
  309.0 1.1 copy-done.10
  310.1 1.1 copy-done.12
  311.2 1.0 copy-done.19
  312.2 32.2 %attend_back.7 = (bf16[512,768]{1,0:T(8,128)(2,1)S(1)}, bf16[2048,768]{1,0:T(8,128)(2,1)}, bf16[2048,768]{1,0:T(8,128)(2,1)}, f32[256,768]{1,0:T(8,128)S(1)}, f32[256,768]{1,0:T(8,128)S(1)}) custom-call(bf16[512,768]{1,0:T(8,128)(2,1)S(1)} %copy-done.8, ...), custom_call_target="tpu_custom_call", output_to_operand_aliasing={{0}: (10, {}), {1}: (11, {}), {2}: (12, {}), {3}: (13, {}),... | custom-call | flops 8589934592 | bytes 18874368 | tf_op jit(solution)/shard_map/attend_back/pallas_call | solution.py:197
  344.4 0.9 copy-done.2
  345.3 0.9 copy-done.4
  346.2 0.9 copy-done.6
  347.1 80.2 %finish.1 = (f32[512,768]{1,0:T(8,128)}, f32[24,768]{1,0:T(8,128)}, f32[24,768]{1,0:T(8,128)}, f32[24,768]{1,0:T(8,128)}, f32[32,768]{1,0:T(8,128)}, /*index=5*/...) custom-call(bf16[512,768]{1,0:T(8,128)(2,1)} %copy-done.2, bf16[4,512,768]{2,1,0:T(8,128)(2,1)} %bitcast.21, ...), custom_call_target="tpu_custom_call" | custom-call | tf_op jit(solution)/shard_map/finish/pallas_call | solution.py:957
  427.4 0.0 reduce-scatter.2.cloned.1.call-done
  427.4 1.1 convert_element_type.12
  428.6 0.6 slice_bitcast_fusion.2
  429.2 0.8 slice_bitcast_fusion
  430.1 1.1 copy.79
  431.2 0.6 copy.80
  431.8 0.6 copy.81
  432.5 0.6 copy.82
  433.1 0.0 copy-done.28
  433.1 0.6 copy.83
  433.7 0.5 copy.84
  434.2 0.6 copy.85
  434.8 0.6 copy.86
  435.4 0.6 copy.87
  (42 shorter events, 0.1 us)
Async XLA Ops:
  7.2 420.2 %reduce-scatter.2.cloned.1.call-start = ((), (), s32[]{:S(2)}) async-start(), calls=%async_computation.1 | async-start | bytes 1720320 | tf_op jit(solution)/shard_map/reduce_scatter | solution.py:1082
  221.3 18.8 %collective-permute-start = (bf16[4,2,2,224,768]{4,3,2,1,0:T(8,128)(2,1)}, bf16[4,2,2,224,768]{4,3,2,1,0:T(8,128)(2,1)}, u32[]{:S(2)}, u32[]{:S(2)}) collective-permute-start(bf16[4,2,2,224,768]{4,3,2,1,0:T(8,128)(2,1)} %bitcast.29), channel_id=1, source_target_pairs={{0,4},{4,0},{8,12},{12,8},{16,20},{20,16},{24,28},{28,24},{1,5},{5... | collective-permute-start | bytes 16515080 | tf_op jit(solution)/shard_map/ppermute | solution.py:1056
  240.1 2.6 copy-start
  242.6 8.4 %copy-start.1 = (bf16[512,768]{1,0:T(8,128)(2,1)S(1)}, bf16[512,768]{1,0:T(8,128)(2,1)}, u32[]{:S(2)}) copy-start(bf16[512,768]{1,0:T(8,128)(2,1)} %get-tuple-element.102.refs_10_) | copy-start | bytes 2359300
  242.6 8.4 %copy-start.3 = (f32[256,768]{1,0:T(8,128)S(1)}, f32[256,768]{1,0:T(8,128)}, u32[]{:S(2)}) copy-start(f32[256,768]{1,0:T(8,128)} %get-tuple-element.105.refs_13_) | copy-start | bytes 2359300
  242.6 8.4 %copy-start.5 = (f32[256,768]{1,0:T(8,128)S(1)}, f32[256,768]{1,0:T(8,128)}, u32[]{:S(2)}) copy-start(f32[256,768]{1,0:T(8,128)} %get-tuple-element.106.refs_14_) | copy-start | bytes 2359300
  242.6 8.4 %copy-start.7 = (bf16[512,768]{1,0:T(8,128)(2,1)S(1)}, bf16[512,768]{1,0:T(8,128)(2,1)}, u32[]{:S(2)}) copy-start(bf16[512,768]{1,0:T(8,128)(2,1)} %get-tuple-element.83.q_ref.refs_0_) | copy-start | bytes 2359300
  242.6 8.4 %copy-start.9 = (bf16[512,768]{1,0:T(8,128)(2,1)S(1)}, bf16[512,768]{1,0:T(8,128)(2,1)}, u32[]{:S(2)}) copy-start(bf16[512,768]{1,0:T(8,128)(2,1)} %get-tuple-element.88.ctx_ref.refs_4_) | copy-start | bytes 2359300
  242.7 8.4 %copy-start.11 = (bf16[512,768]{1,0:T(8,128)(2,1)S(1)}, bf16[512,768]{1,0:T(8,128)(2,1)}, u32[]{:S(2)}) copy-start(bf16[512,768]{1,0:T(8,128)(2,1)} %get-tuple-element.95.refs_3_) | copy-start | bytes 2359300
  242.7 8.4 %copy-start.17 = (bf16[256,768]{1,0:T(8,128)(2,1)S(1)}, bf16[256,768]{1,0:T(8,128)(2,1)}, u32[]{:S(2)}) copy-start(bf16[256,768]{1,0:T(8,128)(2,1)} %get-tuple-element.97.refs_6_) | copy-start | bytes 1179652
  242.7 8.4 %copy-start.18 = (bf16[256,768]{1,0:T(8,128)(2,1)S(1)}, bf16[256,768]{1,0:T(8,128)(2,1)}, u32[]{:S(2)}) copy-start(bf16[256,768]{1,0:T(8,128)(2,1)} %get-tuple-element.98.refs_7_) | copy-start | bytes 1179652
  247.4 1.1 copy-start.13
  248.4 1.1 copy-start.15
  249.5 1.4 copy-start.20
  249.5 1.5 copy-start.21
  249.5 33.5 %collective-permute-start.1 = (bf16[2,2,224,768]{3,2,1,0:T(8,128)(2,1)S(1)}, bf16[2,2,224,768]{3,2,1,0:T(8,128)(2,1)S(1)}, u32[]{:S(2)}, u32[]{:S(2)}) collective-permute-start(bf16[2,2,224,768]{3,2,1,0:T(8,128)(2,1)S(1)} %get-tuple-element.111.refs_17_), channel_id=1, source_target_pairs={{0,16},{4,20},{8,24},{12,28},{16,0},{20,4},{24,8},{28,12},{1,17},{... | collective-permute-start | bytes 4128776 | tf_op jit(solution)/shard_map/ppermute | solution.py:1056
  250.0 33.0 %collective-permute-start.2 = (bf16[2,2,224,768]{3,2,1,0:T(8,128)(2,1)S(1)}, bf16[2,2,224,768]{3,2,1,0:T(8,128)(2,1)S(1)}, u32[]{:S(2)}, u32[]{:S(2)}) collective-permute-start(bf16[2,2,224,768]{3,2,1,0:T(8,128)(2,1)S(1)} %get-tuple-element.112.refs_18_), channel_id=1, source_target_pairs={{0,8},{4,12},{8,0},{12,4},{16,24},{20,28},{24,16},{28,20},{1,9},{5... | collective-permute-start | bytes 4128776 | tf_op jit(solution)/shard_map/ppermute | solution.py:1056
  283.0 1.3 copy-start.14
  284.3 1.3 copy-start.16
  286.9 19.3 %collective-permute-start.3 = (bf16[2,224,768]{2,1,0:T(8,128)(2,1)S(1)}, bf16[2,224,768]{2,1,0:T(8,128)(2,1)S(1)}, u32[]{:S(2)}, u32[]{:S(2)}) collective-permute-start(bf16[2,224,768]{2,1,0:T(8,128)(2,1)S(1)} %get-tuple-element.122.refs_17_), channel_id=1, source_target_pairs={{0,8},{4,12},{8,0},{12,4},{16,24},{20,28},{24,16},{28,20},{1,9},{5... | collective-permute-start | bytes 2064392 | tf_op jit(solution)/shard_map/ppermute | solution.py:1056
  288.1 18.1 %collective-permute-start.4 = (bf16[2,224,768]{2,1,0:T(8,128)(2,1)S(1)}, bf16[2,224,768]{2,1,0:T(8,128)(2,1)S(1)}, u32[]{:S(2)}, u32[]{:S(2)}) collective-permute-start(bf16[2,224,768]{2,1,0:T(8,128)(2,1)S(1)} %get-tuple-element.123.refs_18_), channel_id=1, source_target_pairs={{0,16},{4,20},{8,24},{12,28},{16,0},{20,4},{24,8},{28,12},{1,17},{... | collective-permute-start | bytes 2064392 | tf_op jit(solution)/shard_map/ppermute | solution.py:1056
  306.2 2.7 copy-start.8
  309.0 1.1 copy-start.10
  310.1 1.1 copy-start.12
  311.2 1.0 copy-start.19
  344.4 0.9 copy-start.2
  345.3 0.9 copy-start.4
  346.2 0.9 copy-start.6
  427.3 2.8 copy-start.22
  427.3 3.9 copy-start.26
  427.3 4.5 %copy-start.25 = (f32[24,768]{1,0:T(8,128)S(1)}, f32[24,768]{1,0:T(8,128)}, u32[]{:S(2)}) copy-start(f32[24,768]{1,0:T(8,128)} %get-tuple-element.173) | copy-start | bytes 221188
  427.3 5.1 %copy-start.24 = (f32[24,768]{1,0:T(8,128)S(1)}, f32[24,768]{1,0:T(8,128)}, u32[]{:S(2)}) copy-start(f32[24,768]{1,0:T(8,128)} %get-tuple-element.174) | copy-start | bytes 221188
  427.3 5.8 %copy-start.28 = (f32[3,24]{1,0:T(4,128)S(1)}, f32[3,24]{1,0:T(4,128)}, u32[]{:S(2)}) copy-start(f32[3,24]{1,0:T(4,128)} %get-tuple-element.176) | copy-start | bytes 868
  427.4 6.3 %copy-start.30 = (f32[1,96]{1,0:T(1,128)S(1)}, f32[1,96]{1,0:T(1,128)}, u32[]{:S(2)}) copy-start(f32[1,96]{1,0:T(1,128)} %get-tuple-element.149) | copy-start | bytes 1156
  427.4 6.8 %copy-start.23 = (f32[32,768]{1,0:T(8,128)S(1)}, f32[32,768]{1,0:T(8,128)}, u32[]{:S(2)}) copy-start(f32[32,768]{1,0:T(8,128)} %get-tuple-element.180) | copy-start | bytes 294916
  427.4 7.5 %copy-start.29 = (f32[2,96]{1,0:T(2,128)S(1)}, f32[2,96]{1,0:T(2,128)}, u32[]{:S(2)}) copy-start(f32[2,96]{1,0:T(2,128)} %get-tuple-element.181) | copy-start | bytes 2308
  427.4 8.0 %copy-start.27 = (f32[4,96]{1,0:T(4,128)S(1)}, f32[4,96]{1,0:T(4,128)}, u32[]{:S(2)}) copy-start(f32[4,96]{1,0:T(4,128)} %get-tuple-element.182) | copy-start | bytes 4612
Sparse Core Ops, SparseCore 0:
  309.1 33.7 reduce-scatter.1
